TPU v7x, 32 devices: a whole 2x2x4 slice. The times are simulated.
32 devices in a mesh: dp: 16 (over z, y, x), group: 2 (over core).
Axes of the slice: x: 2, y: 2, z: 4, core: 2. Of those that a mesh axis runs over, the one named last changes fastest.
Arguments:
- hidden_in: bfloat16 [32768, 768], P(('dp', 'group')), may hold values from -6 to 6
- grad_out: bfloat16 [32768, 768], P(('dp', 'group')), may hold values from -6 to 6
- seq_lengths: int32 [64, 16], P(('dp', 'group')), may hold values from 0 to 512, as said below
- key_mask: int32 [32768], P(('dp', 'group')), may hold values from 0 to 1, as said below
- w_qkv: bfloat16 [768, 2304], P(('dp', 'group')), may hold values from -0.21875 to 0.21875
- b_qv: bfloat16 [1536], P(('dp', 'group')), may hold values from -4 to 4
- w_out: bfloat16 [768, 768], P(('dp', 'group')), may hold values from -1.25 to 1.25
- b_out: bfloat16 [768], P(('dp', 'group')), may hold values from -4 to 4
- ln1_gain: bfloat16 [768], P(('dp', 'group')), may hold values from 0.5 to 1.5
- ln1_bias: bfloat16 [768], P(('dp', 'group')), may hold values from -4 to 4
- w_in: bfloat16 [768, 3072], P(('dp', 'group')), may hold values from -0.21875 to 0.21875
- b_in: bfloat16 [3072], P(('dp', 'group')), may hold values from -4 to 4
- w_fc: bfloat16 [3072, 768], P(('dp', 'group')), may hold values from -0.109375 to 0.109375
- b_fc: bfloat16 [768], P(('dp', 'group')), may hold values from -4 to 4
- ln2_gain: bfloat16 [768], P(('dp', 'group')), may hold values from 0.5 to 1.5
- ln2_bias: bfloat16 [768], P(('dp', 'group')), may hold values from -4 to 4
- adapter_weight: float32 [24576], P(('dp', 'group')), may hold values from -0.6 to 0.6
- adapter_first: float32 [24576], P(('dp', 'group')), may hold values from -112 to 112
- adapter_second: float32 [24576], P(('dp', 'group')), may hold values from 32.768 to 524.288
Outputs:
- hidden_out: bfloat16 [32768, 768], P(('dp', 'group'))
- grad_in: float32 [32768, 768], P(('dp', 'group'))
- new_weight: float32 [24576], P(('dp', 'group'))
- new_first: float32 [24576], P(('dp', 'group'))
- new_second: float32 [24576], P(('dp', 'group'))
Inputs may be any that keep to these rules, and one draw needn't show every extreme that they name: `seq_lengths`: row r lists the sequence lengths of window r of 512 tokens (a device holds 2 windows, in order); each row sums to 512 and is either one document of 512 tokens followed by zeros, or 16 sentences of 16 tokens or more. `key_mask`: within each sequence the zeros form a tail of at most a quarter of its length; its first token is 1.
All inputs are finite; a program needn't handle non-finite values.
Results may differ from a plain program's by a relative error of at most 0.013.
Values may be sent and summed in bfloat16 or wider, within the bound.
No kernel may reach another device: no remote copies, remote signals or barrier semaphores. Data moves between devices by JAX's collectives and lax.ppermute only.
A program may use at most 128 MiB of HBM per device.

v0:
```python
import jax
import jax.numpy as jnp
from jax import lax
from jax.sharding import PartitionSpec as P

H = 12
ADAPTER_RANK = 8


norm_eps = 1e-05
low_rank_scale = 2.0
masked_score = -1e30
beta_one = 0.9
beta_two = 0.999
adam_eps = 1e-08
adam_step = 100.0
decay_rate = 0.01
rate_first = 0.002
rate_second = 0.032
slope_const = 0.3989422804014327
root_half = 0.7071067811865476


def to_half(values):
    return values.astype(jnp.bfloat16)


def widen(values):
    return values.astype(jnp.float32)


def matrix_product(left, right):
    return jnp.dot(left, right, preferred_element_type=jnp.float32)


def matrix_product_transposed_right(left, right):
    return lax.dot_general(
        left, right, (((1,), (1,)), ((), ())), preferred_element_type=jnp.float32
    )


def matrix_product_transposed_left(left, right):
    return lax.dot_general(
        left, right, (((0,), (0,)), ((), ())), preferred_element_type=jnp.float32
    )


def normalize(values, norm_gain, offset):
    centre = jnp.mean(values, axis=-1, keepdims=True)
    centred = values - centre
    spread = lax.rsqrt(jnp.mean(centred * centred, axis=-1, keepdims=True) + norm_eps)
    unit_rows = centred * spread
    return (unit_rows * norm_gain + offset, unit_rows, spread)


def normalize_back(incoming, unit_rows, spread, norm_gain):
    scaled = incoming * norm_gain
    return spread * (
        scaled
        - jnp.mean(scaled, axis=-1, keepdims=True)
        - unit_rows * jnp.mean(scaled * unit_rows, axis=-1, keepdims=True)
    )


def gelu_slope(values):
    return (
        0.5 * (1.0 + lax.erf(values * root_half))
        + values * jnp.exp(-0.5 * values * values) * slope_const
    )


def window_scores(query_rows, keys_all, allowed):
    scale_factor = query_rows.shape[-1] ** (-0.5)
    scores = (
        jnp.einsum("qhd,khd->hqk", query_rows, keys_all, preferred_element_type=jnp.float32)
        * scale_factor
    )
    return (jnp.where(allowed[None], scores, masked_score), scale_factor)


def attend(window_item):
    query_rows, keys_all, value_rows_full, allowed = window_item
    scores, scale_factor = window_scores(query_rows, keys_all, allowed)
    highest = jnp.max(scores, axis=-1, keepdims=True)
    exponent = jnp.exp(scores - highest)
    totals = jnp.sum(exponent, axis=-1, keepdims=True)
    probs_half = to_half(exponent / totals)
    mixed_heads = jnp.einsum(
        "hqk,khd->qhd", probs_half, value_rows_full, preferred_element_type=jnp.float32
    )
    return (to_half(mixed_heads.reshape(query_rows.shape[0], -1)), highest + jnp.log(totals))


def attend_back(window_item):
    query_rows, keys_all, value_rows_full, d_mixed, allowed, log_totals = window_item
    scores, scale_factor = window_scores(query_rows, keys_all, allowed)
    probs = jnp.exp(scores - log_totals)
    d_probs = jnp.einsum(
        "qhd,khd->hqk", d_mixed, value_rows_full, preferred_element_type=jnp.float32
    )
    centre = jnp.sum(probs * d_probs, axis=-1, keepdims=True)
    d_scores = to_half(probs * (d_probs - centre))
    query_gradient = (
        jnp.einsum("hqk,khd->qhd", d_scores, keys_all, preferred_element_type=jnp.float32)
        * scale_factor
    )
    d_key = (
        jnp.einsum("hqk,qhd->khd", d_scores, query_rows, preferred_element_type=jnp.float32)
        * scale_factor
    )
    value_gradient = jnp.einsum(
        "hqk,qhd->khd", to_half(probs), d_mixed, preferred_element_type=jnp.float32
    )
    rows_len = query_rows.shape[0]
    return (
        to_half(query_gradient).reshape(rows_len, -1),
        to_half(d_key).reshape(rows_len, -1),
        to_half(value_gradient).reshape(rows_len, -1),
    )


def body(
    hidden_in,
    grad_out,
    seq_lengths,
    key_mask,
    w_qkv,
    b_qv,
    w_out,
    b_out,
    ln1_gain,
    ln1_bias,
    w_in,
    b_in,
    w_fc,
    b_fc,
    ln2_gain,
    ln2_bias,
    adapter_weight,
    adapter_first,
    adapter_second,
):
    tok_rows, hidden_width = hidden_in.shape
    window_count = seq_lengths.shape[0]
    window_len = tok_rows // window_count
    head_count = H
    head_size = hidden_width // head_count
    low_rank_width = ADAPTER_RANK
    block_extent = hidden_width * low_rank_width
    seq_ends = jnp.cumsum(seq_lengths, axis=1)
    positions = jnp.arange(window_len, dtype=jnp.int32)
    slot_ids = jnp.sum((positions[None, :, None] >= seq_ends[:, None, :]).astype(jnp.int32), axis=2)
    key_valid = key_mask.reshape(window_count, window_len) > 0
    allowed = (slot_ids[:, :, None] == slot_ids[:, None, :]) & key_valid[:, None, :]
    attn_parts = (
        lax.all_gather(w_qkv, ("dp", "group"), axis=0, tiled=True),
        lax.all_gather(b_qv, ("dp", "group"), axis=0, tiled=True),
        lax.all_gather(w_out, ("dp", "group"), axis=0, tiled=True),
        lax.all_gather(b_out, ("dp", "group"), axis=0, tiled=True),
        lax.all_gather(ln1_gain, ("dp", "group"), axis=0, tiled=True),
        lax.all_gather(ln1_bias, ("dp", "group"), axis=0, tiled=True),
        lax.all_gather(to_half(adapter_weight), ("dp", "group"), axis=0, tiled=True),
    )
    qkv_all, bias_qv, out_all, bias_out, gain_one, offset_one, factor_list = attn_parts
    down_both = jnp.concatenate(
        [
            factor_list[:block_extent].reshape(hidden_width, low_rank_width),
            factor_list[block_extent : 2 * block_extent].reshape(hidden_width, low_rank_width),
        ],
        axis=1,
    )
    query_up_weight = factor_list[2 * block_extent : 3 * block_extent].reshape(
        hidden_width, low_rank_width
    )
    value_up_weight = factor_list[3 * block_extent :].reshape(hidden_width, low_rank_width)
    rank_reduced = to_half(matrix_product(hidden_in, down_both))
    down_projected = matrix_product(hidden_in, qkv_all)
    bias_wide = widen(bias_qv)
    query_rows = to_half(
        down_projected[:, :hidden_width]
        + bias_wide[:hidden_width]
        + low_rank_scale
        * matrix_product_transposed_right(rank_reduced[:, :low_rank_width], query_up_weight)
    )
    keys_all = to_half(down_projected[:, hidden_width : 2 * hidden_width])
    value_rows_full = to_half(
        down_projected[:, 2 * hidden_width :]
        + bias_wide[hidden_width:]
        + low_rank_scale
        * matrix_product_transposed_right(rank_reduced[:, low_rank_width:], value_up_weight)
    )
    head_shape = (window_count, window_len, head_count, head_size)
    query_heads = query_rows.reshape(head_shape)
    key_heads = keys_all.reshape(head_shape)
    value_heads = value_rows_full.reshape(head_shape)
    mixed_heads, log_totals = lax.map(attend, (query_heads, key_heads, value_heads, allowed))
    mixed_heads = mixed_heads.reshape(tok_rows, hidden_width)
    attended = matrix_product(mixed_heads, out_all) + widen(bias_out)
    normed_one, unit_one, spread_one = normalize(
        widen(hidden_in) + attended, widen(gain_one), widen(offset_one)
    )
    ffn_parts = (
        lax.all_gather(w_in, ("dp", "group"), axis=0, tiled=True),
        lax.all_gather(b_in, ("dp", "group"), axis=0, tiled=True),
        lax.all_gather(w_fc, ("dp", "group"), axis=0, tiled=True),
        lax.all_gather(b_fc, ("dp", "group"), axis=0, tiled=True),
        lax.all_gather(ln2_gain, ("dp", "group"), axis=0, tiled=True),
        lax.all_gather(ln2_bias, ("dp", "group"), axis=0, tiled=True),
    )
    in_all, bias_in, fc_all, bias_fc, gain_two, offset_two = ffn_parts
    pre_active = matrix_product(to_half(normed_one), in_all) + widen(bias_in)
    active = to_half(jax.nn.gelu(pre_active, approximate=False))
    branch = matrix_product(active, fc_all) + widen(bias_fc)
    normed_two, unit_two, spread_two = normalize(
        normed_one + branch, widen(gain_two), widen(offset_two)
    )
    hidden_out = to_half(normed_two)
    back_fc_parts = (
        lax.all_gather(w_in, ("dp", "group"), axis=0, tiled=True),
        lax.all_gather(w_fc, ("dp", "group"), axis=0, tiled=True),
        lax.all_gather(ln2_gain, ("dp", "group"), axis=0, tiled=True),
    )
    back_in, back_fc, back_gain_two = back_fc_parts
    back_attn_parts = (
        lax.all_gather(w_qkv, ("dp", "group"), axis=0, tiled=True),
        lax.all_gather(w_out, ("dp", "group"), axis=0, tiled=True),
        lax.all_gather(ln1_gain, ("dp", "group"), axis=0, tiled=True),
    )
    back_qkv, back_out, back_gain_one = back_attn_parts
    d_sum_two = normalize_back(widen(grad_out), unit_two, spread_two, widen(back_gain_two))
    d_branch = to_half(d_sum_two)
    d_active = matrix_product_transposed_right(d_branch, back_fc)
    d_pre = to_half(d_active * gelu_slope(pre_active))
    d_normed = d_sum_two + matrix_product_transposed_right(d_pre, back_in)
    d_sum_one = normalize_back(d_normed, unit_one, spread_one, widen(back_gain_one))
    d_attended = to_half(d_sum_one)
    d_mixed = to_half(matrix_product_transposed_right(d_attended, back_out))
    query_gradient, d_key, value_gradient = lax.map(
        attend_back,
        (query_heads, key_heads, value_heads, d_mixed.reshape(head_shape), allowed, log_totals),
    )
    query_gradient = query_gradient.reshape(tok_rows, hidden_width)
    d_key = d_key.reshape(tok_rows, hidden_width)
    value_gradient = value_gradient.reshape(tok_rows, hidden_width)
    d_projected = jnp.concatenate([query_gradient, d_key, value_gradient], axis=1)
    d_reduced = to_half(
        low_rank_scale
        * jnp.concatenate(
            [
                matrix_product(query_gradient, query_up_weight),
                matrix_product(value_gradient, value_up_weight),
            ],
            axis=1,
        )
    )
    grad_in = (
        d_sum_one
        + matrix_product_transposed_right(d_projected, back_qkv)
        + matrix_product_transposed_right(d_reduced, down_both)
    )
    down_gradient = matrix_product_transposed_left(hidden_in, d_reduced)
    query_up_gradient = low_rank_scale * matrix_product_transposed_left(
        query_gradient, rank_reduced[:, :low_rank_width]
    )
    value_up_gradient = low_rank_scale * matrix_product_transposed_left(
        value_gradient, rank_reduced[:, low_rank_width:]
    )
    partial_grad = jnp.concatenate(
        [
            down_gradient[:, :low_rank_width].reshape(-1),
            down_gradient[:, low_rank_width:].reshape(-1),
            query_up_gradient.reshape(-1),
            value_up_gradient.reshape(-1),
        ]
    )
    owned_grad = lax.psum_scatter(partial_grad, ("dp", "group"), scatter_dimension=0, tiled=True)
    shard_len = owned_grad.shape[0]
    flat_place = lax.axis_index(("dp", "group")) * shard_len + jnp.arange(
        shard_len, dtype=jnp.int32
    )
    step_rates = jnp.where(flat_place >= 2 * block_extent, rate_second, rate_first)
    new_first = beta_one * adapter_first + (1.0 - beta_one) * owned_grad
    new_second = beta_two * adapter_second + (1.0 - beta_two) * owned_grad * owned_grad
    update = (
        new_first
        / (1.0 - beta_one**adam_step)
        / (jnp.sqrt(new_second / (1.0 - beta_two**adam_step)) + adam_eps)
    )
    new_weight = adapter_weight - step_rates * (update + decay_rate * adapter_weight)
    return (hidden_out, grad_in, new_weight, new_first, new_second)


def solution(mesh):
    return jax.shard_map(
        body,
        mesh=mesh,
        in_specs=(
            P(("dp", "group"), None),
            P(("dp", "group"), None),
            P(("dp", "group"), None),
            P(("dp", "group")),
            P(("dp", "group"), None),
            P(("dp", "group")),
            P(("dp", "group"), None),
            P(("dp", "group")),
            P(("dp", "group")),
            P(("dp", "group")),
            P(("dp", "group"), None),
            P(("dp", "group")),
            P(("dp", "group"), None),
            P(("dp", "group")),
            P(("dp", "group")),
            P(("dp", "group")),
            P(("dp", "group")),
            P(("dp", "group")),
            P(("dp", "group")),
        ),
        out_specs=(
            P(("dp", "group"), None),
            P(("dp", "group"), None),
            P(("dp", "group")),
            P(("dp", "group")),
            P(("dp", "group")),
        ),
        check_vma=False,
    )
```

profile of v0, /device:TPU:0, one launch (start us, length us, event | category | flops | bytes accessed | tf_op | source)
XLA Modules:
  0.0 569.4 jit_solution(7279440806274293044)
XLA Ops:
  16.8 43.0 %all-reduce.9 = (bf16[1536]{0:T(1024)(128)(2,1)S(1)}, bf16[768]{0:T(1024)(128)(2,1)}, bf16[768]{0:T(1024)(128)(2,1)}, bf16[768]{0:T(1024)(128)(2,1)}, bf16[3072]...) all-reduce(bf16[1536]{0:T(1024)(128)(2,1)S(1)} %dynamic-update-slic, ...), channel_id=1, replica_groups=mesh['dp'=16,'group'=2] {'dp','group'}, use_global_device_ids=true, to_apply=%add | all-reduce | flops 9216 | bytes 36864
  61.1 40.7 %all-gather = bf16[32,1,768]{2,1,0:T(2,128)(2,1)S(1)} all-gather(bf16[1,1,768]{2,1,0:T(2,128)(2,1)S(1)} %reshape.214), channel_id=1, replica_groups=mesh['dp'=16,'group'=2] {'dp','group'}, dimensions={0}, use_global_device_ids=true | all-gather | bytes 50688 | tf_op jit(solution)/shard_map/all_gather | solution.py:162
  125.9 5.8 %fusion.137 = f32[1024,2304]{1,0:T(8,128)S(1)} fusion(bf16[1024,768]{1,0:T(8,128)(2,1)S(1)} %copy-done.4, bf16[768,2304]{1,0:T(8,128)(2,1)} %all-gather.6.cloned.1.call-done), kind=kOutput, calls=%fused_computation.199 | convolution fusion | flops 3623878656 | bytes 14548992 | tf_op jit(solution)/shard_map/dot_general | solution.py:33
  144.2 3.7 fusion.70
  160.9 27.1 %while.26 = (s32[]{:T(128)}, bf16[2,512,768]{2,1,0:T(8,128)(2,1)}, f32[2,12,512,1]{2,1,3,0:T(8,128)}, bf16[2,512,12,64]{1,3,2,0:T(8,128)(2,1)}, pred[2,512,512]{...) while((s32[]{:T(128)}, bf16[2,512,768]{2,1,0:T(8,128)(2,1)}, ...), condition=%wide.region_5.6_spmd, body=%wide.region_2.5_spmd.sunk | while | flops 843442176 | bytes 45558360 | solution.py:196
  168.7 4.7 fusion.188
  182.0 4.7 fusion.188
  188.0 3.9 fusion.135
  195.1 11.1 %fusion.77 = f32[1024,3072]{1,0:T(8,128)} fusion(bf16[768,3072]{1,0:T(8,128)(2,1)} %all-gather.10.cloned.1.call-done, f32[1024,768]{0,1:T(8,128)} %copy-done.2, f32[768]{0:T(1024)S(1)} %copy-done.22, f32[768]{0:T(1024)S(1)} %copy-done.21, f32[1024]{0:T(1024)S(1)} %add_rsqrt_fusion.1, f32[1024]{0:T(1024)S(1)} %broadcast_multiply_fusion.5), kind=kOutput, calls=%fused_computation.117 | convolution fusion | flops 4835770368 | bytes 20461568 | tf_op jit(solution)/shard_map/dot_general | solution.py:33
  206.2 54.2 %all-gather.12.cloned.1.call-done = bf16[3072,768]{1,0:T(8,128)(2,1)} async-done(((bf16[96,768]{1,0:T(8,128)(2,1)}), bf16[3072,768]{1,0:T(8,128)(2,1)}) %all-gather.12.cloned.1.call-update) | async-done | bytes 4718608 | tf_op jit(solution)/shard_map/all_gather | solution.py:205
  260.4 36.7 %fusion.136 = (f32[1024]{0:T(1024)S(1)}, f32[1024,768]{0,1:T(8,128)S(1)}) fusion(f32[768]{0:T(1024)S(1)} %copy-done.43, bf16[3072,768]{1,0:T(8,128)(2,1)} %all-gather.12.cloned.1.call-done, f32[1024,3072]{1,0:T(8,128)} %fusion.77, f32[3072]{0:T(1024)S(1)} %copy-done.42, f32[768]{0:T(1024)S(1)} %copy-done.22, f32[768]{0:T(1024)S(1)} %copy-done.21, ...), kind=kOutput, calls=%fused_computation.198 | convolution fusion | flops 5044960256 | bytes 23626752 | tf_op jit(solution)/shard_map/dot_general | solution.py:33
  301.9 22.4 %fusion.131 = (f32[1024]{0:T(1024)S(1)}, f32[1024]{0:T(1024)S(1)}, f32[1024,768]{0,1:T(8,128)}) fusion(f32[1024]{0:T(1024)S(1)} %add_rsqrt_fusion.1, f32[1024,768]{0,1:T(8,128)} %copy-done.2, f32[1024]{0:T(1024)S(1)} %broadcast_multiply_fusion.5, f32[768]{0:T(1024)S(1)} %copy-done.21, bf16[768,3072]{1,0:T(8,128)(2,1)} %all-gather.10.cloned.1.call-done, ...), kind=kOutput, calls=%fused_computation.194 | convolution fusion | flops 9717151744 | bytes 33081344 | tf_op jit(solution)/shard_map/dot_general | solution.py:37
  324.9 6.3 %convolution_convert_fusion = bf16[1024,768]{1,0:T(8,128)(2,1)} fusion(bf16[768,768]{1,0:T(8,128)(2,1)} %all-gather.8.cloned.1.call-done, f32[1024,768]{0,1:T(8,128)} %get-tuple-element.258, f32[1024,768]{0,1:T(8,128)} %copy-done.2, f32[1024]{0:T(1024)S(1)} %broadcast_multiply_fusion, f32[1024]{0:T(1024)S(1)} %broadcast_multiply_fusion.1, ...), kind=kOutput, calls=%fused_computation.116 | convolution fusion | flops 1214251008 | bytes 9060352 | tf_op jit(solution)/shard_map/dot_general | solution.py:37
  341.9 84.6 %while.27 = (s32[]{:T(128)}, bf16[2,512,768]{2,1,0:T(8,128)(2,1)}, bf16[2,512,768]{2,1,0:T(8,128)(2,1)}, bf16[2,512,768]{2,1,0:T(8,128)(2,1)}, bf16[2,512,12,64]...) while((s32[]{:T(128)}, bf16[2,512,768]{2,1,0:T(8,128)(2,1)}, ...), condition=%wide.region_16.17_spmd, body=%wide.region_14.16_spmd.sunk | while | flops 2062411776 | bytes 188657840 | solution.py:238
  346.3 11.2 %multiply_reduce_fusion.6 = (f32[12,512]{1,0:T(8,128)S(1)}, f32[12,512,512]{1,2,0:T(8,128)}) fusion(f32[12,512,512]{1,2,0:T(8,128)S(1)} %fusion.197, f32[12,512]{1,0:T(8,128)S(1)} %dynamic-slice_bitcast_fusion.7, pred[512,512]{0,1:T(8,128)(4,1)S(1)} %dynamic-slice_bitcast_fusion.8, bf16[2,512,12,64]{1,3,2,0:T(8,128)(2,1)} %get-tuple-element.432, ...), kind=kOutput, calls=%fused_computation.22.clone.1 | convolution fusion | flops 418375680 | bytes 27051008 | tf_op jit(solution)/shard_map/while/body/eval_jaxpr/qhd,khd->hqk/dot_general | solution.py:98
  357.5 7.0 %multiply_convert_fusion.6 = bf16[12,512,512]{1,2,0:T(8,128)(2,1)S(1)} fusion(f32[12,512,512]{1,2,0:T(8,128)} %get-tuple-element.373, f32[12,512,512]{1,2,0:T(8,128)S(1)} %fusion.197, f32[12,512]{1,0:T(8,128)S(1)} %get-tuple-element.374, f32[12,512]{1,0:T(8,128)S(1)} %dynamic-slice_bitcast_fusion.7, pred[512,512]{0,1:T(8,128)(4,1)S(1)} %dynamic-slice_bitcast_fusion.8), kind=kLoop, calls=%fused_computation.21.clone.1 | loop fusion | flops 18874368 | bytes 31768576 | tf_op jit(solution)/shard_map/while/body/eval_jaxpr/convert_element_type | solution.py:25
  367.3 8.8 %fusion.198 = bf16[12,64,512]{2,1,0:T(8,128)(2,1)} fusion(f32[12,512,512]{1,2,0:T(8,128)} %copy-done, f32[12,512]{1,0:T(8,128)S(1)} %dynamic-slice_bitcast_fusion.7, pred[512,512]{0,1:T(8,128)(4,1)S(1)} %dynamic-slice_bitcast_fusion.8, bf16[2,512,12,64]{1,3,2,0:T(8,128)(2,1)} %get-tuple-element.431, s32[]{:T(128)} %get-tuple-element.412), kind=kOutput, calls=%fused_computation.29.clone.1 | convolution fusion | flops 415629312 | bytes 14443008 | tf_op jit(solution)/shard_map/while/body/eval_jaxpr/hqk,qhd->khd/dot_general | solution.py:111
  378.9 4.2 multiply_convert_fusion.7
  388.4 11.2 %multiply_reduce_fusion.6 = (f32[12,512]{1,0:T(8,128)S(1)}, f32[12,512,512]{1,2,0:T(8,128)}) fusion(f32[12,512,512]{1,2,0:T(8,128)S(1)} %fusion.197, f32[12,512]{1,0:T(8,128)S(1)} %dynamic-slice_bitcast_fusion.7, pred[512,512]{0,1:T(8,128)(4,1)S(1)} %dynamic-slice_bitcast_fusion.8, bf16[2,512,12,64]{1,3,2,0:T(8,128)(2,1)} %get-tuple-element.432, ...), kind=kOutput, calls=%fused_computation.22.clone.1 | convolution fusion | flops 418375680 | bytes 27051008 | tf_op jit(solution)/shard_map/while/body/eval_jaxpr/qhd,khd->hqk/dot_general | solution.py:98
  399.6 7.0 %multiply_convert_fusion.6 = bf16[12,512,512]{1,2,0:T(8,128)(2,1)S(1)} fusion(f32[12,512,512]{1,2,0:T(8,128)} %get-tuple-element.373, f32[12,512,512]{1,2,0:T(8,128)S(1)} %fusion.197, f32[12,512]{1,0:T(8,128)S(1)} %get-tuple-element.374, f32[12,512]{1,0:T(8,128)S(1)} %dynamic-slice_bitcast_fusion.7, pred[512,512]{0,1:T(8,128)(4,1)S(1)} %dynamic-slice_bitcast_fusion.8), kind=kLoop, calls=%fused_computation.21.clone.1 | loop fusion | flops 18874368 | bytes 31768576 | tf_op jit(solution)/shard_map/while/body/eval_jaxpr/convert_element_type | solution.py:25
  409.5 8.8 %fusion.198 = bf16[12,64,512]{2,1,0:T(8,128)(2,1)} fusion(f32[12,512,512]{1,2,0:T(8,128)} %copy-done, f32[12,512]{1,0:T(8,128)S(1)} %dynamic-slice_bitcast_fusion.7, pred[512,512]{0,1:T(8,128)(4,1)S(1)} %dynamic-slice_bitcast_fusion.8, bf16[2,512,12,64]{1,3,2,0:T(8,128)(2,1)} %get-tuple-element.431, s32[]{:T(128)} %get-tuple-element.412), kind=kOutput, calls=%fused_computation.29.clone.1 | convolution fusion | flops 415629312 | bytes 14443008 | tf_op jit(solution)/shard_map/while/body/eval_jaxpr/hqk,qhd->khd/dot_general | solution.py:111
  421.0 4.2 multiply_convert_fusion.7
  441.8 6.5 %fusion.63 = f32[1024,768]{0,1:T(8,128)S(1)} fusion(bf16[768,2304]{1,0:T(8,128)(2,1)} %all-gather.6.cloned.1.call-done, bf16[1024,768]{1,0:T(8,128)(2,1)S(1)} %bitcast.147, bf16[1024,768]{1,0:T(8,128)(2,1)} %bitcast.148, bf16[1024,768]{1,0:T(8,128)(2,1)S(1)} %bitcast.144), kind=kOutput, calls=%fused_computation.85 | convolution fusion | flops 3638034432 | bytes 11403264 | tf_op jit(solution)/shard_map/dot_general | solution.py:37
  454.6 106.7 %all-reduce.12.cloned.1.call-done = f32[24576]{0:T(1024)} async-done(((f32[24576]{0:T(1024)}), f32[24576]{0:T(1024)}) %all-reduce.12.cloned.1.call-update) | async-done | bytes 98320
  (230 shorter events, 141.1 us)
Async XLA Ops:
  7.2 104.1 %copy-start.4 = (bf16[1024,768]{1,0:T(8,128)(2,1)S(1)}, bf16[1024,768]{1,0:T(8,128)(2,1)}, u32[]{:S(2)}) copy-start(bf16[1024,768]{1,0:T(8,128)(2,1)} %param.23) | copy-start | bytes 4718596
  7.2 113.3 %copy-start.15 = (bf16[1024,768]{1,0:T(8,128)(2,1)S(1)}, bf16[1024,768]{1,0:T(8,128)(2,1)}, u32[]{:S(2)}) copy-start(bf16[1024,768]{1,0:T(8,128)(2,1)} %param.24) | copy-start | bytes 4718596
  7.2 118.7 %all-gather.6.cloned.1.call-start = ((), (), s32[]{:S(2)}) async-start(), calls=%async_computation | async-start | bytes 3649536 | tf_op jit(solution)/shard_map/all_gather | solution.py:156
  7.9 180.0 %all-gather.8.cloned.1.call-start = ((), (), s32[]{:S(2)}) async-start(), calls=%async_computation.1 | async-start | bytes 1216512 | tf_op jit(solution)/shard_map/all_gather | solution.py:158
  8.7 186.4 %all-gather.10.cloned.1.call-start = ((), (), s32[]{:S(2)}) async-start(), calls=%async_computation.2 | async-start | bytes 4866048 | tf_op jit(solution)/shard_map/all_gather | solution.py:203
  9.4 251.0 %all-gather.12.cloned.1.call-start = ((), (), s32[]{:S(2)}) async-start(), calls=%async_computation.3 | async-start | bytes 4866048 | tf_op jit(solution)/shard_map/all_gather | solution.py:205
  10.0 551.3 %all-reduce.12.cloned.1.call-start = ((), (), s32[]{:S(2)}) async-start(), calls=%async_computation.4 | async-start | bytes 196608
  102.9 19.2 %copy-start.30 = (bf16[768,8]{0,1:T(8,128)(2,1)}, bf16[768,8]{0,1:T(8,128)(2,1)S(1)}, u32[]{:S(2)}) copy-start(bf16[768,8]{0,1:T(8,128)(2,1)S(1)} %copy.106) | copy-start | bytes 36868
  104.2 27.7 %copy-start.12 = (bf16[768,8]{1,0:T(8,128)(2,1)}, bf16[768,8]{1,0:T(8,128)(2,1)S(1)}, u32[]{:S(2)}) copy-start(bf16[768,8]{1,0:T(8,128)(2,1)S(1)} %slice.90) | copy-start | bytes 36868
  105.2 39.0 %copy-start.14 = (bf16[768,8]{1,0:T(8,128)(2,1)}, bf16[768,8]{1,0:T(8,128)(2,1)S(1)}, u32[]{:S(2)}) copy-start(bf16[768,8]{1,0:T(8,128)(2,1)S(1)} %slice.95) | copy-start | bytes 36868
  160.9 27.1 %copy-start.44 = (f32[768]{0:T(1024)S(1)}, f32[768]{0:T(1024)}, u32[]{:S(2)}) copy-start(f32[768]{0:T(1024)} %convert_element_type.126) | copy-start | bytes 9220
  191.9 132.3 %copy-start.16 = (f32[1024]{0:T(1024)}, f32[1024]{0:T(1024)S(1)}, u32[]{:S(2)}) copy-start(f32[1024]{0:T(1024)S(1)} %broadcast_multiply_fusion.5) | copy-start | bytes 12292
  194.0 130.3 %copy-start.18 = (f32[1024]{0:T(1024)}, f32[1024]{0:T(1024)S(1)}, u32[]{:S(2)}) copy-start(f32[1024]{0:T(1024)S(1)} %add_rsqrt_fusion.1) | copy-start | bytes 12292
  194.0 66.4 %copy-start.42 = (f32[3072]{0:T(1024)S(1)}, f32[3072]{0:T(1024)}, u32[]{:S(2)}) copy-start(f32[3072]{0:T(1024)} %convert_element_type.130) | copy-start | bytes 36868
  194.0 66.4 %copy-start.43 = (f32[768]{0:T(1024)S(1)}, f32[768]{0:T(1024)}, u32[]{:S(2)}) copy-start(f32[768]{0:T(1024)} %convert_element_type.132) | copy-start | bytes 9220
  341.9 86.7 %copy-start.25 = (bf16[1024,16]{0,1:T(8,128)(2,1)S(1)}, bf16[1024,16]{0,1:T(8,128)(2,1)}, u32[]{:S(2)}) copy-start(bf16[1024,16]{0,1:T(8,128)(2,1)} %fusion.85) | copy-start | bytes 98308
  345.1 12.4 %copy-start = (f32[12,512,512]{1,2,0:T(8,128)}, f32[12,512,512]{1,2,0:T(8,128)S(1)}, u32[]{:S(2)}) copy-start(f32[12,512,512]{1,2,0:T(8,128)S(1)} %fusion.197) | copy-start | bytes 37748740 | tf_op jit(solution)/shard_map/while
  387.2 12.4 %copy-start = (f32[12,512,512]{1,2,0:T(8,128)}, f32[12,512,512]{1,2,0:T(8,128)S(1)}, u32[]{:S(2)}) copy-start(f32[12,512,512]{1,2,0:T(8,128)S(1)} %fusion.197) | copy-start | bytes 37748740 | tf_op jit(solution)/shard_map/while
  431.5 10.2 %copy-start.6 = (bf16[2,512,768]{2,1,0:T(8,128)(2,1)S(1)}, bf16[2,512,768]{2,1,0:T(8,128)(2,1)}, u32[]{:S(2)}) copy-start(bf16[2,512,768]{2,1,0:T(8,128)(2,1)} %get-tuple-element.99) | copy-start | bytes 4718596
  441.7 6.6 %copy-start.3 = (f32[1024,768]{0,1:T(8,128)S(1)}, f32[1024,768]{0,1:T(8,128)}, u32[]{:S(2)}) copy-start(f32[1024,768]{0,1:T(8,128)} %copy-done.2) | copy-start | bytes 9437188
  441.7 6.6 %copy-start.11 = (f32[1024,768]{0,1:T(8,128)S(1)}, f32[1024,768]{0,1:T(8,128)}, u32[]{:S(2)}) copy-start(f32[1024,768]{0,1:T(8,128)} %get-tuple-element.258) | copy-start | bytes 9437188
  451.9 109.3 %copy-start.39 = (f32[768]{0:T(1024)S(1)}, f32[768]{0:T(1024)}, u32[]{:S(2)}) copy-start(f32[768]{0:T(1024)} %param.39) | copy-start | bytes 9220
  451.9 109.3 %copy-start.45 = (f32[768]{0:T(1024)S(1)}, f32[768]{0:T(1024)}, u32[]{:S(2)}) copy-start(f32[768]{0:T(1024)} %param.40) | copy-start | bytes 9220
  451.9 109.3 %copy-start.46 = (f32[768]{0:T(1024)S(1)}, f32[768]{0:T(1024)}, u32[]{:S(2)}) copy-start(f32[768]{0:T(1024)} %param.41) | copy-start | bytes 9220
  (30 other events, 125.5 us)
Sparse Core Ops, SparseCore 0:
  10.9 62.9 all-gather.5
  76.8 52.8 all-gather.7
  132.5 62.4 all-gather.9
  197.8 62.4 all-gather.11
  441.8 119.3 all-reduce.11
where the time goes:
time: 574 us; the launch traced here: 569 us
  matrix products  182 us (32%)
  waiting for transfers between devices  165 us (29%)
  blocking collectives  83.6 us (15%)
  local copies, waits for them, and re-layouts  82.6 us (14%)
  other arithmetic  41.2 us (7%)
  between operations  14.7 us (3%)
    unnamed x6, waiting for transfers between devices  109 us
    dot_general x7, matrix products, matrix_product(): return jnp.dot(left, right, preferred_element_type=jnp.float32)  61.9 us
    all_gather x1, waiting for transfers between devices, body(): lax.all_gather(w_fc, ('dp', 'group'), axis=0, tiled=True)  54.2 us
    unnamed x1, blocking collectives  43 us
    dot_general x6, matrix products, matrix_product_transposed_right(): lax.dot_general(left, right, (((1,), (1,)), ((), ())), preferred_element_...  41.9 us
    all_gather x1, blocking collectives, body(): lax.all_gather(to_half(adapter_weight), ('dp', 'group'), axis=0, tiled=True)  40.7 us
    unnamed x111, local copies, waits for them, and re-layouts  22.9 us
    dot_general x2, matrix products, attend_back(): jnp.einsum('qhd,khd->hqk', d_mixed, value_rows_full, preferred_element_ty...  22.4 us
  transfers between devices with their start and end apart: 5, of which 3 were waited for; matrix products, arithmetic and copies ran while one was open for 21% of the time, Pallas kernels for 0%

commit v1 on v0

v1 whole, which is shorter than its diff:
```python
import functools

import jax
import jax.numpy as jnp
from jax import lax
from jax.experimental import pallas as pl
from jax.experimental.pallas import tpu as pltpu
from jax.sharding import PartitionSpec as P

H = 12
ADAPTER_RANK = 8

norm_eps = 1e-05
low_rank_scale = 2.0
beta_one = 0.9
beta_two = 0.999
adam_eps = 1e-08
adam_step = 100.0
decay_rate = 0.01
rate_first = 0.002
rate_second = 0.032
slope_const = 0.3989422804014327
root_half = 0.7071067811865476
masked = -1e30

half = jnp.bfloat16
wide = jnp.float32
AXES = ("dp", "group")
PAIR = 128
FEAT = 128

NN = (((1,), (0,)), ((), ()))
NT = (((1,), (1,)), ((), ()))
TN = (((0,), (0,)), ((), ()))


def dot(left, right, dims=NN):
    return lax.dot_general(left, right, dims, preferred_element_type=wide)


def params(mib=58):
    return pltpu.CompilerParams(vmem_limit_bytes=mib * 2**20)


def shape(dims, dtype):
    return jax.ShapeDtypeStruct(dims, dtype)


def row_mean(values):
    return jnp.mean(values, axis=-1, keepdims=True)


def project_kernel(x_ref, ga_ref, ad_ref, bias_ref, q_ref, k_ref, v_ref, red_ref, wqkv_ref, wout_ref):
    devices = ga_ref.shape[0]
    rows = wout_ref.shape[0] // devices
    for d in range(devices):
        span = slice(rows * d, rows * d + rows)
        for j in range(3):
            wqkv_ref[j, span, :] = ga_ref[d, rows * j : rows * (j + 1), :]
        wout_ref[span, :] = ga_ref[d, rows * 3 : rows * 4, :]
    x = x_ref[...]
    reduced = dot(x, ad_ref[0:16, :], NT).astype(half)
    red_ref[...] = reduced
    up = ad_ref[16:32, :]
    lane = lax.broadcasted_iota(jnp.int32, reduced.shape, 1)
    zero = jnp.zeros_like(reduced)
    width = x.shape[1]
    bias = bias_ref[...].astype(wide)
    q = dot(x, wqkv_ref[0]) + bias[:, :width]
    q += low_rank_scale * dot(jnp.where(lane < 8, reduced, zero), up)
    q_ref[...] = (q.astype(half).astype(wide) * 0.125).astype(half)
    k_ref[...] = dot(x, wqkv_ref[1]).astype(half)
    v = dot(x, wqkv_ref[2]) + bias[:, width:]
    v += low_rank_scale * dot(jnp.where(lane < 8, zero, reduced), up)
    v_ref[...] = v.astype(half)


def project(x, ga, ad, bias):
    rows, width = x.shape
    return pl.pallas_call(
        project_kernel,
        out_shape=[shape((rows, width), half)] * 3
        + [shape((rows, 16), half), shape((3, width, width), half), shape((width, width), half)],
        compiler_params=params(),
    )(x, ga, ad, bias)


def low_lanes(dims):
    return lax.broadcasted_iota(jnp.int32, dims, 1) < 64


def attend_kernel(q_ref, k_ref, v_ref, fq_ref, fk_ref, mixed_ref, inv_ref, p_ref):
    length = q_ref.shape[0]
    tile = 256
    low = low_lanes((length, PAIR))
    zero = jnp.zeros((length, PAIR), half)
    one = jnp.ones((length, PAIR), half)
    v2 = v_ref[...]
    keys = jnp.concatenate([k_ref[...], fk_ref[0]], axis=1)
    values = [
        jnp.concatenate([jnp.where(low, v2, zero), jnp.where(low, one, zero)], axis=1),
        jnp.concatenate([jnp.where(low, zero, v2), jnp.where(low, zero, one)], axis=1),
    ]
    low_t = low_lanes((tile, PAIR))
    zero_t = jnp.zeros((tile, PAIR), half)
    for c in range(length // tile):
        span = slice(c * tile, (c + 1) * tile)
        q2 = q_ref[span, :]
        fq = fq_ref[0, span, :]
        total = None
        for h in range(2):
            qh = jnp.where(low_t, q2, zero_t) if h == 0 else jnp.where(low_t, zero_t, q2)
            scores = dot(jnp.concatenate([qh, fq], axis=1), keys, NT)
            highest = jnp.max(scores, axis=1, keepdims=True)
            p = jnp.exp(scores - highest).astype(half)
            p_ref[0, 0, h, span, :] = p
            part = dot(p, values[h])
            total = part if total is None else total + part
        inv = 1.0 / total[:, PAIR:]
        mixed_ref[span, :] = (total[:, :PAIR] * inv).astype(half)
        inv_ref[span, :] = inv


def attend(q, k, v, fq, fk):
    rows, width = q.shape
    windows, length, _ = fq.shape
    pairs = width // PAIR
    block = pl.BlockSpec((length, PAIR), lambda w, h: (w, h))
    feat = pl.BlockSpec((1, length, FEAT), lambda w, h: (w, 0, 0))
    return pl.pallas_call(
        attend_kernel,
        grid=(windows, pairs),
        in_specs=[block, block, block, feat, feat],
        out_specs=[block, block, pl.BlockSpec((1, 1, 2, length, length), lambda w, h: (w, h, 0, 0, 0))],
        out_shape=[
            shape((rows, width), half),
            shape((rows, width), wide),
            shape((windows, pairs, 2, length, length), half),
        ],
        compiler_params=params(),
    )(q, k, v, fq, fk)


def attend_back_kernel(q_ref, k_ref, v_ref, g_ref, mixed_ref, p_ref, dq_ref, dk_ref, dv_ref):
    length = q_ref.shape[0]
    low = low_lanes((length, PAIR))
    zero = jnp.zeros((length, PAIR), half)
    zero_w = jnp.zeros((length, PAIR), wide)
    k2, v2, g2 = k_ref[...], v_ref[...], g_ref[...]
    q_t, g_t = q_ref[...].T, g2.T
    prod = g2.astype(wide) * mixed_ref[...].astype(wide)
    dq, dks, dvs = None, [], []
    for h in range(2):
        pick = (lambda a, z: jnp.where(low, a, z)) if h == 0 else (lambda a, z: jnp.where(low, z, a))
        centre = jnp.sum(pick(prod, zero_w), axis=1, keepdims=True)
        d_probs = dot(pick(g2, zero), v2, NT) - centre
        p = p_ref[0, 0, h]
        ds = (p.astype(wide) * d_probs).astype(half)
        part = dot(ds, pick(k2, zero))
        dq = part if dq is None else dq + part
        lanes = slice(64 * h, 64 * h + 64)
        dks.append(dot(q_t[lanes], ds))
        dvs.append(dot(g_t[lanes], p))
    dq_ref[...] = (dq * 0.125).astype(half)
    dk_ref[...] = jnp.concatenate(dks, axis=0).astype(half).T
    dv_ref[...] = jnp.concatenate(dvs, axis=0).astype(half).T


def attend_back(q, k, v, g, mixed, p):
    rows, width = q.shape
    windows, pairs, _, length, _ = p.shape
    block = pl.BlockSpec((length, PAIR), lambda w, h: (w, h))
    return pl.pallas_call(
        attend_back_kernel,
        grid=(windows, pairs),
        in_specs=[block] * 5 + [pl.BlockSpec((1, 1, 2, length, length), lambda w, h: (w, h, 0, 0, 0))],
        out_specs=[block] * 3,
        out_shape=[shape((rows, width), half)] * 3,
        compiler_params=params(),
    )(q, k, v, g, mixed, p)


def norm_one_kernel(mixed_ref, wout_ref, x_ref, vec_ref, unit_ref, spread_ref):
    vec = vec_ref[...].astype(wide)
    r = x_ref[...].astype(wide) + (dot(mixed_ref[...], wout_ref[...]) + vec[0:1])
    centred = r - row_mean(r)
    spread = lax.rsqrt(row_mean(centred * centred) + norm_eps)
    unit_ref[...] = centred * spread
    spread_ref[...] = spread


def norm_one(mixed, wout, x, vec):
    rows, width = x.shape
    tile = 512
    block = pl.BlockSpec((tile, width), lambda i: (i, 0))
    thin = pl.BlockSpec((tile, 1), lambda i: (i, 0))
    return pl.pallas_call(
        norm_one_kernel,
        grid=(rows // tile,),
        in_specs=[block, pl.BlockSpec(wout.shape, lambda i: (0, 0)), block, pl.BlockSpec(vec.shape, lambda i: (0, 0))],
        out_specs=[block, thin],
        out_shape=[shape((rows, width), wide), shape((rows, 1), wide)],
        compiler_params=params(),
    )(mixed, wout, x, vec)


def ffn_in_kernel(unit_ref, gb_ref, vec_ref, bin_ref, act_ref, slope_ref, win_ref):
    devices = gb_ref.shape[0]
    width = win_ref.shape[1]
    rows = width // devices

    @pl.when(pl.program_id(0) == 0)
    def _():
        for d in range(devices):
            for j in range(win_ref.shape[0]):
                win_ref[j, rows * d : rows * (d + 1), :] = gb_ref[d, rows * j : rows * (j + 1), :]

    vec = vec_ref[...].astype(wide)
    normed = (unit_ref[...] * vec[1:2] + vec[2:3]).astype(half)
    for j in range(win_ref.shape[0]):
        cols = slice(j * width, (j + 1) * width)
        pre = dot(normed, win_ref[j]) + bin_ref[:, cols].astype(wide)
        phi = 0.5 * (1.0 + lax.erf(pre * root_half))
        act_ref[:, cols] = (pre * phi).astype(half)
        slope_ref[:, cols] = (phi + pre * jnp.exp(-0.5 * pre * pre) * slope_const).astype(half)


def ffn_in(unit, gb, vec, bias):
    rows, width = unit.shape
    devices, both, _ = gb.shape
    hidden = bias.shape[1]
    parts = hidden // width
    tile = 512
    return pl.pallas_call(
        ffn_in_kernel,
        grid=(rows // tile,),
        in_specs=[
            pl.BlockSpec((tile, width), lambda i: (i, 0)),
            pl.BlockSpec((devices, both // 2, width), lambda i: (0, 1, 0)),
            pl.BlockSpec(vec.shape, lambda i: (0, 0)),
            pl.BlockSpec(bias.shape, lambda i: (0, 0)),
        ],
        out_specs=[
            pl.BlockSpec((tile, hidden), lambda i: (i, 0)),
            pl.BlockSpec((tile, hidden), lambda i: (i, 0)),
            pl.BlockSpec((parts, width, width), lambda i: (0, 0, 0)),
        ],
        out_shape=[
            shape((rows, hidden), half),
            shape((rows, hidden), half),
            shape((parts, width, width), half),
        ],
        compiler_params=params(),
    )(unit, gb, vec, bias)


def middle_kernel(
    act_ref, slope_ref, unit_ref, spread_ref, grad_ref, inv_ref, gb_ref, win_ref, wout_ref, vec_ref,
    out_ref, d_one_ref, g_ref,
):
    vec = vec_ref[...].astype(wide)
    devices, rows, width = gb_ref.shape
    parts = win_ref.shape[0]
    per = width // rows
    unit_one = unit_ref[...]
    branch = None
    for j in range(parts):
        w = gb_ref[per * j : per * (j + 1)].reshape(width, width)
        part = dot(act_ref[:, j * width : (j + 1) * width], w)
        branch = part if branch is None else branch + part
    r = unit_one * vec[1:2] + vec[2:3] + (branch + vec[3:4])
    centred = r - row_mean(r)
    spread = lax.rsqrt(row_mean(centred * centred) + norm_eps)
    unit = centred * spread
    out_ref[...] = (unit * vec[4:5] + vec[5:6]).astype(half)
    e = grad_ref[...].astype(wide) * vec[4:5]
    d_two = spread * (e - row_mean(e) - unit * row_mean(e * unit))
    d_branch = d_two.astype(half)
    d_normed = d_two
    for j in range(parts):
        w = gb_ref[per * j : per * (j + 1)].reshape(width, width)
        d_act = dot(d_branch, w, NT)
        d_pre = (d_act * slope_ref[:, j * width : (j + 1) * width].astype(wide)).astype(half)
        d_normed += dot(d_pre, win_ref[j], NT)
    e = d_normed * vec[1:2]
    d_one = spread_ref[...] * (e - row_mean(e) - unit_one * row_mean(e * unit_one))
    d_one_ref[...] = d_one
    d_mixed = dot(d_one.astype(half), wout_ref[...], NT)
    g_ref[...] = (d_mixed * inv_ref[...]).astype(half)


def middle(act, slope, unit, spread, grad, inv, gb, win, wout, vec):
    rows, width = unit.shape
    devices, both, _ = gb.shape
    hidden = act.shape[1]
    tile = 256
    block = pl.BlockSpec((tile, width), lambda i: (i, 0))
    long = pl.BlockSpec((tile, hidden), lambda i: (i, 0))

    def whole(array):
        return pl.BlockSpec(array.shape, lambda i: (0,) * array.ndim, pipeline_mode=pl.Buffered(1))

    return pl.pallas_call(
        middle_kernel,
        grid=(rows // tile,),
        in_specs=[
            long,
            long,
            block,
            pl.BlockSpec((tile, 1), lambda i: (i, 0)),
            block,
            block,
            pl.BlockSpec((devices, both // 2, width), lambda i: (0, 0, 0), pipeline_mode=pl.Buffered(1)),
            whole(win),
            whole(wout),
            whole(vec),
        ],
        out_specs=[block] * 3,
        out_shape=[shape((rows, width), half), shape((rows, width), wide), shape((rows, width), half)],
        compiler_params=params(),
    )(act, slope, unit, spread, grad, inv, gb, win, wout, vec)


def project_back_kernel(dq_ref, dk_ref, dv_ref, d_one_ref, x_ref, red_ref, wqkv_ref, ad_ref, grad_ref, ga_ref):
    dq, dk, dv = dq_ref[...], dk_ref[...], dv_ref[...]
    down, up = ad_ref[0:16, :], ad_ref[16:32, :]
    row = lax.broadcasted_iota(jnp.int32, up.shape, 0)
    none = jnp.zeros_like(up)
    d_red = dot(dq, jnp.where(row < 8, up, none), NT) + dot(dv, jnp.where(row < 8, none, up), NT)
    d_red = (low_rank_scale * d_red).astype(half)
    grad = d_one_ref[...] + dot(dq, wqkv_ref[0], NT)
    grad += dot(dk, wqkv_ref[1], NT)
    grad += dot(dv, wqkv_ref[2], NT)
    grad_ref[...] = grad + dot(d_red, down)
    red = red_ref[...]
    both = jnp.concatenate(
        [
            dot(d_red, x_ref[...], TN),
            low_rank_scale * dot(red, dq, TN)[0:8],
            low_rank_scale * dot(red, dv, TN)[8:16],
        ],
        axis=0,
    )

    @pl.when(pl.program_id(0) == 0)
    def _():
        ga_ref[...] = both

    @pl.when(pl.program_id(0) > 0)
    def _():
        ga_ref[...] += both


def project_back(dq, dk, dv, d_one, x, red, wqkv, ad):
    rows, width = x.shape
    tile = 512
    block = pl.BlockSpec((tile, width), lambda i: (i, 0))
    return pl.pallas_call(
        project_back_kernel,
        grid=(rows // tile,),
        in_specs=[
            block,
            block,
            block,
            block,
            block,
            pl.BlockSpec((tile, 16), lambda i: (i, 0)),
            pl.BlockSpec(wqkv.shape, lambda i: (0, 0, 0)),
            pl.BlockSpec(ad.shape, lambda i: (0, 0)),
        ],
        out_specs=[block, pl.BlockSpec((32, width), lambda i: (0, 0))],
        out_shape=[shape((rows, width), wide), shape((32, width), wide)],
        compiler_params=params(),
    )(dq, dk, dv, d_one, x, red, wqkv, ad)


def body(
    hidden_in, grad_out, seq_lengths, key_mask, w_qkv, b_qv, w_out, b_out, ln1_gain, ln1_bias,
    w_in, b_in, w_fc, b_fc, ln2_gain, ln2_bias, adapter_weight, adapter_first, adapter_second,
):
    tok_rows, width = hidden_in.shape
    windows = seq_lengths.shape[0]
    length = tok_rows // windows
    rank = ADAPTER_RANK
    own_rows = w_out.shape[0]
    devices = width // own_rows
    ffn_parts = w_in.shape[1] // width
    block_extent = width * rank
    span = adapter_weight.shape[0] // rank
    shards = width // span

    factor = adapter_weight.astype(half).reshape(span, rank).T
    line_a = jnp.concatenate([b_qv, b_out, ln1_gain])
    line_b = jnp.concatenate([ln1_bias, b_fc, ln2_gain, ln2_bias])
    lines = jnp.concatenate([b_in[None], line_a[None], line_b[None], jnp.zeros((rank - 3, span), half)], axis=0)
    small = jnp.concatenate([factor, lines, jnp.zeros((rank, width - 2 * span), half)], axis=1)
    pack_a = jnp.concatenate([w_qkv[:, width * j : width * (j + 1)] for j in range(3)] + [w_out, small], axis=0)
    pack_b = jnp.concatenate([w_fc] + [w_in[:, width * j : width * (j + 1)] for j in range(ffn_parts)], axis=0)
    all_a = lax.all_gather(pack_a, AXES, axis=0, tiled=False)
    all_b = lax.all_gather(pack_b, AXES, axis=0, tiled=False)

    seq_ends = jnp.cumsum(seq_lengths, axis=1)
    positions = jnp.arange(length, dtype=jnp.int32)
    slot_ids = jnp.sum((positions[None, :, None] >= seq_ends[:, None, :]).astype(jnp.int32), axis=2)
    slots = seq_lengths.shape[1]
    lane = jnp.arange(FEAT, dtype=jnp.int32)[None, None, :]
    same = slot_ids[:, :, None] == lane
    padded = (key_mask.reshape(windows, length) == 0)[:, :, None]
    query_feat = jnp.where((lane <= slots) & ~same, 1.0, 0.0).astype(half)
    key_feat = jnp.where(same | ((lane == slots) & padded), masked, 0.0).astype(half)

    small_all = all_a[:, 4 * own_rows :, :]
    factors = small_all[:, :, :span].reshape(4, shards, rank, span)
    factors = jnp.swapaxes(factors, 1, 2).reshape(4 * rank, width)
    bias_in = small_all[:, 0, span : 2 * span].reshape(1, -1)
    row_a = small_all[:, 1, span : 2 * span]
    row_b = small_all[:, 2, span : 2 * span]
    bias_qv = row_a[:, : 2 * own_rows].reshape(1, -1)
    vec = jnp.concatenate(
        [row_a[:, 2 * own_rows :].reshape(devices, 2, own_rows), row_b.reshape(devices, 4, own_rows)], axis=1
    )
    vec = jnp.swapaxes(vec, 0, 1).reshape(6, width)
    vec = jnp.concatenate([vec, jnp.zeros((2, width), half)], axis=0)

    q, k, v, reduced, wqkv, wout = project(hidden_in, all_a, factors, bias_qv)
    mixed, inv, probs = attend(q, k, v, query_feat, key_feat)
    unit_one, spread_one = norm_one(mixed, wout, hidden_in, vec)
    act, slope, win = ffn_in(unit_one, all_b, vec, bias_in)
    hidden_out, d_one, g = middle(act, slope, unit_one, spread_one, grad_out, inv, all_b, win, wout, vec)
    dq, dk, dv = attend_back(q, k, v, g, mixed, probs)
    grad_in, factor_grad = project_back(dq, dk, dv, d_one, hidden_in, reduced, wqkv, factors)

    partial_grad = factor_grad.reshape(4, rank, shards, span).swapaxes(1, 2).reshape(devices, rank, span)
    owned = lax.all_to_all(partial_grad, AXES, 0, 0, tiled=True)
    owned_grad = jnp.sum(owned, axis=0).T.reshape(-1)
    shard_len = owned_grad.shape[0]
    flat_place = lax.axis_index(AXES) * shard_len + jnp.arange(shard_len, dtype=jnp.int32)
    step_rates = jnp.where(flat_place >= 2 * block_extent, rate_second, rate_first)
    new_first = beta_one * adapter_first + (1.0 - beta_one) * owned_grad
    new_second = beta_two * adapter_second + (1.0 - beta_two) * owned_grad * owned_grad
    update = (
        new_first
        / (1.0 - beta_one**adam_step)
        / (jnp.sqrt(new_second / (1.0 - beta_two**adam_step)) + adam_eps)
    )
    new_weight = adapter_weight - step_rates * (update + decay_rate * adapter_weight)
    return (hidden_out, grad_in, new_weight, new_first, new_second)


def solution(mesh):
    rows, line = P(AXES, None), P(AXES)
    return jax.shard_map(
        body,
        mesh=mesh,
        in_specs=(
            rows, rows, rows, line, rows, line, rows, line, line, line,
            rows, line, rows, line, line, line, line, line, line,
        ),
        out_specs=(rows, rows, line, line, line),
        check_vma=False,
    )
```

time: 574 us -> 263 us (0.46)
  matrix products: 182 us -> 0 us
  Pallas kernels: 0 us -> 110 us
  blocking collectives: 83.6 us -> 0 us
  local copies, waits for them, and re-layouts: 82.6 us -> 15.9 us
  waiting for transfers between devices: 165 us -> 113 us
  other arithmetic: 41.2 us -> 5.75 us
    dot_general x30 -> x0, matrix products: 182 us -> none  [the longest x7 61.9 us: matrix_product(): return jnp.dot(left, right, preferred_element_type=jnp.float32)]
    pallas_call x0 -> x7, Pallas kernels: none -> 110 us  [the longest x1 29.4 us: middle(): pl.pallas_call(middle_kernel, grid=(rows // tile,), in_specs=[long, long,...]
    unnamed x6 -> x2, waiting for transfers between devices: 109 us -> 0.03 us
    all_gather x4 -> x2, waiting for transfers between devices: 55.3 us -> 104 us  [the longest x1 60.1 us: body(): all_a = lax.all_gather(pack_a, AXES, axis=0, tiled=False)]
    unnamed x1 -> x0, blocking collectives: 43 us -> none
    all_gather x1 -> x0, blocking collectives: 40.7 us -> none  [body(): lax.all_gather(to_half(adapter_weight), ('dp', 'group'), axis=0, tiled=True)]
    convert_element_type x10 -> x2, other arithmetic: 23.6 us -> 1.82 us  [the longest x1 1.13 us: body(): jnp.where(same | (lane == slots) & padded, masked, 0.0).astype(half)]
    unnamed x111 -> x19, local copies, waits for them, and re-layouts: 22.9 us -> 7.75 us
  transfers between devices with their start and end apart: 5 -> 3, of which waited for: 3 -> 3; matrix products, arithmetic and copies ran while one was open for 21% -> 5% of each run, Pallas kernels for 0% -> 13%
where the time goes in v1:
time: 263 us; the launch traced here: 261 us
  waiting for transfers between devices  113 us (43%)
  Pallas kernels  110 us (42%)
  local copies, waits for them, and re-layouts  15.9 us (6%)
  between operations  14.2 us (5%)
  other arithmetic  5.75 us (2%)
  starting transfers between devices  3.27 us (1%)
    all_gather x1, waiting for transfers between devices, body(): all_a = lax.all_gather(pack_a, AXES, axis=0, tiled=False)  60.1 us
    all_gather x1, waiting for transfers between devices, body(): all_b = lax.all_gather(pack_b, AXES, axis=0, tiled=False)  44.3 us
    pallas_call x1, Pallas kernels, middle(): pl.pallas_call(middle_kernel, grid=(rows // tile,), in_specs=[long, long,...  29.4 us
    pallas_call x1, Pallas kernels, attend_back(): pl.pallas_call(attend_back_kernel, grid=(windows, pairs), in_specs=[block...  19.6 us
    pallas_call x1, Pallas kernels, attend(): pl.pallas_call(attend_kernel, grid=(windows, pairs), in_specs=[block, blo...  19 us
    pallas_call x1, Pallas kernels, ffn_in(): pl.pallas_call(ffn_in_kernel, grid=(rows // tile,), in_specs=[pl.BlockSpe...  14.6 us
    pallas_call x1, Pallas kernels, project_back(): pl.pallas_call(project_back_kernel, grid=(rows // tile,), in_specs=[block...  11.4 us
    pallas_call x1, Pallas kernels, project(): pl.pallas_call(project_kernel, out_shape=[shape((rows, width), half)] * 3...  10.4 us
  transfers between devices with their start and end apart: 3, of which 3 were waited for; matrix products, arithmetic and copies ran while one was open for 5% of the time, Pallas kernels for 13%

profile of v1, /device:TPU:0, one launch (start us, length us, event | category | flops | bytes accessed | tf_op | source)
XLA Modules:
  0.0 261.4 jit_solution(9880910110580247799)
XLA Ops:
  7.2 0.8 slice_dynamic-update-slice_fusion.6
  8.0 0.8 slice_dynamic-update-slice_fusion.5
  8.8 0.8 slice_dynamic-update-slice_fusion.4
  10.4 0.8 constant_dynamic-update-slice_fusion.1
  11.3 0.8 maximum_bitcast_fusion.1
  13.6 0.9 constant_dynamic-update-slice_fusion.2
  14.5 0.8 slice_dynamic-update-slice_fusion.3
  16.0 0.8 slice_dynamic-update-slice_fusion.1
  19.0 0.9 reduce_window_sum.11
  20.0 1.1 select_convert_fusion
  21.1 60.1 %all-gather.5.cloned.1.call-done = bf16[3328,768]{1,0:T(8,128)(2,1)} async-done(((bf16[104,768]{1,0:T(8,128)(2,1)}), bf16[3328,768]{1,0:T(8,128)(2,1)}) %all-gather.5.cloned.1.call-update) | async-done | bytes 5111824 | tf_op jit(solution)/shard_map/all_gather | solution.py:399
  81.2 0.8 slice.57
  82.0 1.3 slice_reduce_fusion
  86.6 10.4 %shard_map.218 = (bf16[1024,768]{1,0:T(8,128)(2,1)}, bf16[1024,768]{1,0:T(8,128)(2,1)}, bf16[1024,768]{1,0:T(8,128)(2,1)}, bf16[1024,16]{1,0:T(8,128)(2,1)}, bf1...) custom-call(bf16[1024,768]{1,0:T(8,128)(2,1)} %x_ref.5, bf16[32,104,768]{2,1,0:T(8,128)(2,1)} %bitcast.28, ...), custom_call_target="tpu_custom_call" | custom-call | tf_op jit(solution)/shard_map/pallas_call | solution.py:80
  97.0 19.0 %shard_map.219 = (bf16[1024,768]{1,0:T(8,128)(2,1)}, f32[1024,768]{1,0:T(8,128)}, bf16[2,6,2,512,512]{4,3,2,1,0:T(8,128)(2,1)}) custom-call(bf16[1024,768]{1,0:T(8,128)(2,1)} %get-tuple-element.27.q_ref, bf16[1024,768]{1,0:T(8,128)(2,1)} %get-tuple-element.28.k_ref, bf16[1024,768]{1,0:T(8,128)(2,1)} %get-tuple-element.29.v_ref, ...), custom_call_target="tpu_custom_call" | custom-call | tf_op jit(solution)/shard_map/pallas_call | solution.py:130
  116.0 5.3 %shard_map.220 = (f32[1024,768]{1,0:T(8,128)}, f32[1024,1]{1,0:T(8,128)}) custom-call(bf16[1024,768]{1,0:T(8,128)(2,1)} %get-tuple-element.30.mixed_ref, bf16[768,768]{1,0:T(8,128)(2,1)} %get-tuple-element.31.wout_ref, bf16[1024,768]{1,0:T(8,128)(2,1)} %x_ref.5, bf16[8,768]{1,0:T(8,128)(2,1)} %concatenate.30.vec_ref), custom_call_target="tpu_custom_call" | custom-call | tf_op jit(solution)/shard_map/pallas_call | solution.py:197
  121.3 44.3 %all-gather.7.cloned.1.call-done = bf16[6144,768]{1,0:T(8,128)(2,1)} async-done(((bf16[192,768]{1,0:T(8,128)(2,1)}), bf16[6144,768]{1,0:T(8,128)(2,1)}) %all-gather.7.cloned.1.call-update) | async-done | bytes 9437200 | tf_op jit(solution)/shard_map/all_gather | solution.py:400
  165.6 14.6 %shard_map.221 = (bf16[1024,3072]{1,0:T(8,128)(2,1)}, bf16[1024,3072]{1,0:T(8,128)(2,1)}, bf16[4,768,768]{2,1,0:T(8,128)(2,1)}) custom-call(f32[1024,768]{1,0:T(8,128)} %get-tuple-element.32.unit_ref, bf16[32,192,768]{2,1,0:T(8,128)(2,1)} %bitcast.24, bf16[8,768]{1,0:T(8,128)(2,1)} %concatenate.30.vec_ref, bf16[1,3072]{1,0:T(2,128)(2,1)} %reshape_squeeze.7.bin_ref), custom_call_target="tpu_custom_call" | custom-call | tf_op jit(solution)/shard_map/pallas_call | solution.py:234
  180.2 29.4 %shard_map.222 = (bf16[1024,768]{1,0:T(8,128)(2,1)}, f32[1024,768]{1,0:T(8,128)}, bf16[1024,768]{1,0:T(8,128)(2,1)}) custom-call(bf16[1024,3072]{1,0:T(8,128)(2,1)} %get-tuple-element.33.act_ref, bf16[1024,3072]{1,0:T(8,128)(2,1)} %get-tuple-element.34.slope_ref, f32[1024,768]{1,0:T(8,128)} %get-tuple-element.32.unit_ref, ...), custom_call_target="tpu_custom_call" | custom-call | tf_op jit(solution)/shard_map/pallas_call | solution.py:303
  209.6 19.6 %shard_map.223 = (bf16[1024,768]{1,0:T(8,128)(2,1)}, bf16[1024,768]{1,0:T(8,128)(2,1)}, bf16[1024,768]{1,0:T(8,128)(2,1)}) custom-call(bf16[1024,768]{1,0:T(8,128)(2,1)} %get-tuple-element.27.q_ref, bf16[1024,768]{1,0:T(8,128)(2,1)} %get-tuple-element.28.k_ref, bf16[1024,768]{1,0:T(8,128)(2,1)} %get-tuple-element.29.v_ref, ...), custom_call_target="tpu_custom_call" | custom-call | tf_op jit(solution)/shard_map/pallas_call | solution.py:173
  229.2 11.4 %shard_map.224 = (f32[1024,768]{1,0:T(8,128)}, f32[32,768]{1,0:T(8,128)}) custom-call(bf16[1024,768]{1,0:T(8,128)(2,1)} %get-tuple-element.41.dq_ref, bf16[1024,768]{1,0:T(8,128)(2,1)} %get-tuple-element.42.dk_ref, bf16[1024,768]{1,0:T(8,128)(2,1)} %get-tuple-element.43.dv_ref, f32[1024,768]{1,0:T(8,128)} %get-tuple-element.44.d_one_ref, ...), custom_call_target="tpu_custom_call" | custom-call | tf_op jit(solution)/shard_map/pallas_call | solution.py:358
  240.6 1.0 reshape.65
  242.3 3.2 %all-to-all-start = ((f32[32,8,96]{2,1,0:T(8,128)}), f32[32,8,96]{2,1,0:T(8,128)S(1)}, u32[]{:S(2)}, u32[]{:S(2)}) async-start(f32[32,8,96]{2,1,0:T(8,128)} %bitcast.11), calls=%async_computation | async-start | bytes 262144 | tf_op jit(solution)/shard_map/all_to_all | solution.py:434
  245.5 8.2 %all-to-all-done = f32[32,8,96]{2,1,0:T(8,128)S(1)} async-done(((f32[32,8,96]{2,1,0:T(8,128)}), f32[32,8,96]{2,1,0:T(8,128)S(1)}, u32[]{:S(2)}, u32[]{:S(2)}) %all-to-all-start) | async-done | bytes 98336 | tf_op jit(solution)/shard_map/all_to_all | solution.py:434
  (45 shorter events, 10.3 us)
Async XLA Ops:
  7.2 74.0 %all-gather.5.cloned.1.call-start = ((), (), s32[]{:S(2)}) async-start(), calls=%async_computation.1 | async-start | bytes 5271552 | tf_op jit(solution)/shard_map/all_gather | solution.py:399
  12.8 0.7 copy-start.1
  13.5 152.1 %all-gather.7.cloned.1.call-start = ((), (), s32[]{:S(2)}) async-start(), calls=%async_computation.2 | async-start | bytes 9732096 | tf_op jit(solution)/shard_map/all_gather | solution.py:400
  17.6 0.7 copy-start
  229.1 24.8 %copy-start.2 = (f32[768]{0:T(1024)S(1)}, f32[768]{0:T(1024)}, u32[]{:S(2)}) copy-start(f32[768]{0:T(1024)} %param.35) | copy-start | bytes 9220
  229.2 24.8 %copy-start.3 = (f32[768]{0:T(1024)S(1)}, f32[768]{0:T(1024)}, u32[]{:S(2)}) copy-start(f32[768]{0:T(1024)} %param.36) | copy-start | bytes 9220
  229.2 24.8 %copy-start.4 = (f32[768]{0:T(1024)S(1)}, f32[768]{0:T(1024)}, u32[]{:S(2)}) copy-start(f32[768]{0:T(1024)} %param.37) | copy-start | bytes 9220
  242.3 11.4 %all-to-all-start = ((f32[32,8,96]{2,1,0:T(8,128)}), f32[32,8,96]{2,1,0:T(8,128)S(1)}, u32[]{:S(2)}, u32[]{:S(2)}) async-start(f32[32,8,96]{2,1,0:T(8,128)} %bitcast.11), calls=%async_computation | async-start | bytes 262144 | tf_op jit(solution)/shard_map/all_to_all | solution.py:434
Sparse Core Ops, SparseCore 0:
  13.6 67.5 all-gather.4
  84.7 80.8 all-gather.6

commit v2 on v1

v2 whole, which is shorter than its diff:
```python
import functools

import jax
import jax.numpy as jnp
import numpy as np
from jax import lax
from jax.experimental import pallas as pl
from jax.experimental.pallas import tpu as pltpu
from jax.sharding import PartitionSpec as P

H = 12
ADAPTER_RANK = 8

norm_eps = 1e-05
low_rank_scale = 2.0
beta_one = 0.9
beta_two = 0.999
adam_eps = 1e-08
adam_step = 100.0
decay_rate = 0.01
rate_first = 0.002
rate_second = 0.032
slope_const = 0.3989422804014327
root_half = 0.7071067811865476
masked = -1e30

half = jnp.bfloat16
wide = jnp.float32
AXES = ("dp", "group")
WIDTH = 768
PAIR = 128
FEAT = 128

NN = (((1,), (0,)), ((), ()))
NT = (((1,), (1,)), ((), ()))
TN = (((0,), (0,)), ((), ()))


def dot(left, right, dims=NN):
    return lax.dot_general(left, right, dims, preferred_element_type=wide)


def params(mib=58):
    return pltpu.CompilerParams(vmem_limit_bytes=mib * 2**20)


def cost(us):
    return pl.CostEstimate(flops=int(us * 8e8), bytes_accessed=int(us * 2.5e6), transcendentals=0)


def shape(dims, dtype):
    return jax.ShapeDtypeStruct(dims, dtype)


def row_mean(values):
    return jnp.mean(values, axis=-1, keepdims=True)


class Held:
    def __init__(self, array, owner):
        self.array, self.owner = array, owner

    def send(self, to):
        count = self.owner.shape[0]
        pairs = [(i, to(i)) for i in range(count)]
        owner = np.zeros_like(self.owner)
        for i, j in pairs:
            owner[j] = self.owner[i]
        return Held(lax.ppermute(self.array, AXES, pairs), owner)

    def rows_from(self, start):
        part = Held(self.array, self.owner)
        part.start = start
        return part

    start = 0


def join_after(gate, *held):
    arrays = lax.optimization_barrier((gate, *[h.array for h in held]))[1:]
    return join(*[Held(array, h.owner) for array, h in zip(arrays, held)])


def join(*held):
    return Held(
        jnp.concatenate([h.array for h in held], axis=0), np.concatenate([h.owner for h in held], axis=1)
    )


def after(held, *others):
    first, *_ = lax.optimization_barrier((held.array, *[o.array for o in others]))
    return Held(first, held.owner)


def own(array, devices):
    return Held(array[None], np.arange(devices, dtype=np.int32)[:, None])


def other_core(i):
    return i ^ 1


def first_way(i):
    return i ^ (2 if i % 2 == 0 else 4)


def second_way(i):
    return i ^ (4 if i % 2 == 0 else 2)


def along(i):
    return (i + (8 if i % 2 == 0 else -8)) % 32


def up(i):
    return (i + 8) % 32


def down(i):
    return (i - 8) % 32


def across(i):
    return (i + 16) % 32


def gather_attention(pack_a, pack_b):
    a, b = own(pack_a, 32), own(pack_b, 32)
    near = [a.send(up), a.send(down)]
    ways = a.send(first_way)
    far = a.send(across)
    b_ways = b.send(first_way)
    a_own = join(a, ways)
    a_own2 = a_own.send(second_way)
    near = join(*near)
    near_ways = near.send(first_way)
    far_ways = after(far, near_ways).send(first_way)
    near = join(near, after(near_ways, a_own2))
    near2 = near.send(second_way)
    far = join(far, far_ways)
    far2 = far.send(second_way)
    held = [a_own, a_own2, near, far, near2, far2]
    held += [h.send(other_core) for h in held]
    return held, (b, b_ways, far_ways, far2)


class Ring:
    def __init__(self, state):
        b, b_ways, far_ways, far2 = state
        gate = far2.array
        self.held = []
        self.now = after(b, far_ways).send(along)
        self.ways = [join_after(gate, b, b_ways)]
        self.seconds = [self.ways[0].send(second_way)]
        self.waiting = []
        self.now = after(self.now, far2)
        self.turn()

    def turn(self):
        arrived = self.now
        self.now = arrived.send(along)
        self.waiting.append((arrived, arrived.send(first_way)))

    def step(self, token):
        if self.waiting:
            pair = join_after(token, *self.waiting.pop())
            self.ways.append(pair)
            self.seconds.append(pair.send(second_way))
        if self.now is not None:
            self.now = after(self.now, Held(token, None))
            if len(self.ways) < 3:
                self.turn()
            else:
                self.waiting.append((self.now, self.now.send(first_way)))
                self.now = None

    def swap(self, token, count):
        for pair, second in list(zip(self.ways, self.seconds))[len(self.held) // 4 : count]:
            gated = lax.optimization_barrier((token, pair.array, second.array))[1:]
            pair, second = Held(gated[0], pair.owner), Held(gated[1], second.owner)
            self.held += [pair, second, pair.send(other_core), second.send(other_core)]


def everyone(array, devices):
    owner = np.tile(np.arange(devices, dtype=np.int32), (devices, 1))
    return Held(lax.all_gather(array, AXES, axis=0, tiled=False), owner)


def places(held):
    table = np.concatenate([h.owner for h in held], axis=1)
    assert all(sorted(line) == list(range(len(table))) for line in table)
    return lax.dynamic_index_in_dim(jnp.asarray(table, jnp.int32), lax.axis_index(AXES), 0, keepdims=False)


def place_blocks(starts, table_ref, block_refs, all_ref, sems):
    copies = []
    rows = all_ref.shape[1]
    for start, ref in zip(starts, block_refs):
        for b in range(ref.shape[0]):
            i = len(copies)
            source = ref.at[b] if ref.shape[1] == rows else ref.at[b, pl.ds(start, rows)]
            copies.append(pltpu.make_async_copy(source, all_ref.at[table_ref[i]], sems.at[i]))
    return copies


def run(copies):
    for copy in copies:
        copy.start()
    for copy in copies:
        copy.wait()


SCALARS = pl.BlockSpec(memory_space=pltpu.SMEM)
PLACED = pl.BlockSpec(memory_space=pl.ANY)


def pack_kernel(span, wqkv_ref, wout_ref, win_ref, wfc_ref, factor_ref, lines_ref, a_ref, b_ref, one_ref):
    rows, width = wout_ref.shape
    for j in range(3):
        a_ref[rows * j : rows * (j + 1), :] = wqkv_ref[:, width * j : width * (j + 1)]
    rank = ADAPTER_RANK
    count = factor_ref.shape[1]
    lane = lax.broadcasted_iota(jnp.int32, (rank, count), 1)
    row = lax.broadcasted_iota(jnp.int32, (rank, count), 0)
    spread = jnp.where(lane % rank == row, factor_ref[...].astype(half).astype(wide), 0.0).astype(half)
    place = lax.broadcasted_iota(jnp.int32, (count, PAIR), 0) // rank
    take = (place == lax.broadcasted_iota(jnp.int32, (count, PAIR), 1)).astype(wide).astype(half)
    a_ref[3 * rows :, :PAIR] = dot(spread, take).astype(half)
    a_ref[3 * rows :, PAIR : 2 * PAIR] = jnp.zeros((rank, PAIR), half)
    a_ref[3 * rows : 3 * rows + 3, PAIR : PAIR + span] = lines_ref[...]
    a_ref[3 * rows :, 2 * PAIR :] = jnp.zeros((rank, width - 2 * PAIR), half)
    split = wfc_ref.shape[0]
    one_ref[...] = jnp.zeros_like(one_ref)
    for j in range(win_ref.shape[1] // width):
        one_ref[rows * j : rows * (j + 1), :] = win_ref[:, width * j : width * (j + 1)]
    one_ref[split : split + rows, :] = wout_ref[...]
    b_ref[:split, :] = wfc_ref[...]
    b_ref[split:, :] = one_ref[...]


def pack(w_qkv, w_out, w_in, w_fc, factor, lines):
    rows, width = w_out.shape
    one_rows = w_fc.shape[0] + rows
    one_rows += (-one_rows) % 16
    return pl.pallas_call(
        functools.partial(pack_kernel, lines.shape[1]),
        out_shape=[
            shape((3 * rows + ADAPTER_RANK, width), half),
            shape((w_fc.shape[0] + one_rows, width), half),
            shape((one_rows, width), half),
        ],
        compiler_params=params(),
        cost_estimate=cost(2),
    )(w_qkv, w_out, w_in, w_fc, factor, lines)


def unfold(pieces, piece, per):
    devices, rows, lanes = pieces.shape
    width = WIDTH
    part = width // per
    lane = lax.broadcasted_iota(jnp.int32, (lanes, width), 1)
    row = lax.broadcasted_iota(jnp.int32, (lanes, width), 0)
    repeat = (lane % part + piece == row).astype(wide).astype(half)
    spread = dot(pieces.reshape(devices * rows, lanes), repeat).reshape(devices // per, per, rows, width)
    shard = lax.broadcasted_iota(jnp.int32, (per, rows, width), 0)
    place = lax.broadcasted_iota(jnp.int32, (per, rows, width), 2) // part
    return jnp.sum(jnp.where((shard == place)[None], spread, 0.0), axis=1)


def project_kernel(starts, shards, table_ref, x_ref, *refs):
    blocks = len(starts)
    block_refs = refs[:blocks]
    qkv_ref, red_ref, ad_ref, vec_ref, bin_ref, wout_ref, ga_ref, w_ref, bias_ref, sems, sem = refs[blocks:]
    devices = ga_ref.shape[0]
    width = x_ref.shape[1]
    rows = width // devices
    keep = pltpu.make_async_copy(w_ref, wout_ref, sem)

    @pl.when(pl.program_id(0) == 0)
    def _():
        run(place_blocks(starts, table_ref, block_refs, ga_ref, sems))
        for d in range(devices):
            span = slice(rows * d, rows * d + rows)
            for j in range(3):
                w_ref[j, span, :] = ga_ref[d, rows * j : rows * (j + 1), :]
        keep.start()
        small = ga_ref[:, 3 * rows :, :PAIR]
        lines = ga_ref[:, 3 * rows :, PAIR : 2 * PAIR]
        ad_ref[...] = unfold(small, 0, shards).reshape(4 * ADAPTER_RANK, width).astype(half)
        bin_ref[...] = unfold(lines, 0, shards)[:, 0:1].astype(half)
        bias = unfold(lines, 0, devices // 2)[:, 1:2]
        bias_ref[0], bias_ref[1], bias_ref[2] = bias[0], jnp.zeros_like(bias[0]), bias[1]
        vecs = [unfold(lines, rows * j, devices)[0] for j in range(4)]
        vec_ref[...] = jnp.concatenate(
            [vecs[2][1:2], vecs[3][1:2], vecs[0][2:3], vecs[1][2:3], vecs[2][2:3], vecs[3][2:3], vecs[0][0:2]],
            axis=0,
        )

        red_ref[...] = dot(x_ref[...], ad_ref[0:16, :], NT).astype(half)

    j = pl.program_id(0)
    reduced = red_ref[...]
    lane = lax.broadcasted_iota(jnp.int32, reduced.shape, 1)
    own_lanes = jnp.where(lane // 8 * 2 == j, reduced, jnp.zeros_like(reduced))
    wide_row = dot(x_ref[...], w_ref[j]) + bias_ref[j]
    wide_row += low_rank_scale * dot(own_lanes, ad_ref[16:32, :])
    scale = jnp.where(j == 0, 0.125, 1.0)
    qkv_ref[0] = (wide_row.astype(half).astype(wide) * scale).astype(half)

    @pl.when(j == pl.num_programs(0) - 1)
    def _():
        keep.wait()


def constant(dims):
    return pl.BlockSpec(dims, lambda i: (0,) * len(dims))


def project(x, held, table, parts, shards):
    rows, width = x.shape
    devices = held[0].owner.shape[0]
    return pl.pallas_call(
        functools.partial(project_kernel, [h.start for h in held], shards),
        grid=(3,),
        in_specs=[SCALARS, constant(x.shape)] + [PLACED] * len(held),
        out_specs=[
            pl.BlockSpec((1, rows, width), lambda i: (i, 0, 0)),
            constant((rows, 16)),
            constant((4 * ADAPTER_RANK, width)),
            constant((8, width)),
            constant((parts, 1, width)),
            PLACED,
        ],
        out_shape=[
            shape((3, rows, width), half),
            shape((rows, 16), half),
            shape((4 * ADAPTER_RANK, width), half),
            shape((8, width), wide),
            shape((parts, 1, width), half),
            shape((3, width, width), half),
        ],
        scratch_shapes=[
            pltpu.VMEM((devices, 3 * (width // devices) + ADAPTER_RANK, width), half),
            pltpu.VMEM((3, width, width), half),
            pltpu.VMEM((3, 1, width), wide),
            pltpu.SemaphoreType.DMA((devices,)),
            pltpu.SemaphoreType.DMA,
        ],
        compiler_params=params(),
        cost_estimate=cost(8),
    )(table, x, *[h.array for h in held])


STEP = 2


def low_lanes(length):
    return lax.broadcasted_iota(jnp.int32, (length, PAIR), 1) < 64


def apart(pair, low):
    zero = jnp.zeros_like(pair)
    return jnp.concatenate([jnp.where(low, pair, zero), jnp.where(low, zero, pair)], axis=0)


def together(heads, low):
    length = low.shape[0]
    return jnp.where(low, heads[:length], heads[length:])


def attend_kernel(q_ref, k_ref, v_ref, fq_ref, fk_ref, *refs):
    mixed_ref, inv_ref, p_ref = refs[-3:]
    length = q_ref.shape[1]
    low = low_lanes(length)
    one = jnp.ones((length, PAIR), half)
    fq = jnp.concatenate([fq_ref[0], fq_ref[0]], axis=0)

    def scores_of(i):
        lanes = slice(i * PAIR, (i + 1) * PAIR)
        queries = jnp.concatenate([apart(q_ref[0, :, lanes], low), fq], axis=1)
        keys = jnp.concatenate([k_ref[0, :, lanes], fk_ref[0]], axis=1)
        return dot(queries, keys, NT)

    scores = [scores_of(i) for i in range(STEP)]
    for i in range(STEP):
        lanes = slice(i * PAIR, (i + 1) * PAIR)
        highest = jnp.max(scores[i], axis=1, keepdims=True)
        p = jnp.exp(scores[i] - highest).astype(half)
        p_ref[0, i] = p
        total = dot(p, jnp.concatenate([v_ref[0, :, lanes], one], axis=1))
        inv = together(1.0 / total[:, PAIR:], low)
        mixed_ref[:, lanes] = (together(total[:, :PAIR], low) * inv).astype(half)
        inv_ref[:, lanes] = inv


def attend(window, qkv, fq, fk, before):
    _, rows, width = qkv.shape
    windows, length, _ = fq.shape
    pairs = width // PAIR
    block = pl.BlockSpec((length, STEP * PAIR), lambda h: (window, h))
    feat = pl.BlockSpec((1, length, FEAT), lambda h: (window, 0, 0))
    heads = [pl.BlockSpec((1, length, STEP * PAIR), lambda h, j=j: (j, window, h)) for j in range(3)]
    return pl.pallas_call(
        attend_kernel,
        grid=(pairs // STEP,),
        in_specs=heads + [feat, feat] + [PLACED] * len(before),
        out_specs=[block, block, pl.BlockSpec((1, STEP, 2 * length, length), lambda h: (window, h, 0, 0))],
        out_shape=[
            shape((rows, width), half),
            shape((rows, width), wide),
            shape((windows, pairs, 2 * length, length), half),
        ],
        input_output_aliases={5 + i: i for i in range(len(before))},
        compiler_params=params(),
        cost_estimate=cost(6),
    )(qkv, qkv, qkv, fq, fk, *before)


def attend_back_kernel(
    q_ref, k_ref, v_ref, g_ref, mixed_ref, p_ref, x_ref, red_ref, ad_ref, d_ref, d_red_ref, out_ref, sum_ref, total_ref
):
    length = q_ref.shape[1]
    low = low_lanes(length)
    w, h = pl.program_id(0), pl.program_id(1)
    last = h == pl.num_programs(1) - 1
    row = lax.broadcasted_iota(jnp.int32, (16, PAIR), 0)
    red = red_ref[...]
    zero = jnp.zeros((16, PAIR), half)

    def d_probs_of(i):
        lanes = slice(i * PAIR, (i + 1) * PAIR)
        g2 = g_ref[:, lanes]
        prod = g2.astype(wide) * mixed_ref[:, lanes].astype(wide)
        centre = jnp.sum(apart(prod, low), axis=1, keepdims=True)
        return dot(apart(g2, low), v_ref[0, :, lanes], NT), centre

    d_probs = [d_probs_of(i) for i in range(STEP)]
    d_red = None
    grads = []
    for i in range(STEP):
        lanes = slice(i * PAIR, (i + 1) * PAIR)
        p = p_ref[0, i]
        raw, centre = d_probs[i]
        ds = (p.astype(wide) * (raw - centre)).astype(half)
        q_t, g_t = q_ref[0, :, lanes].T, g_ref[:, lanes].T
        dv = [dot(g_t[64 * n : 64 * n + 64], p[n * length : (n + 1) * length]) for n in range(2)]
        dk = [dot(q_t[64 * n : 64 * n + 64], ds[n * length : (n + 1) * length]) for n in range(2)]
        dq = (together(dot(ds, k_ref[0, :, lanes]), low) * 0.125).astype(half)
        dv = jnp.concatenate(dv, axis=0).astype(half).T
        d_ref[0, :, lanes] = dq
        d_ref[1, :, lanes] = jnp.concatenate(dk, axis=0).astype(half).T
        d_ref[2, :, lanes] = dv
        both = jnp.concatenate([dq, dv], axis=1)
        up = ad_ref[16:32, pl.ds(pl.multiple_of((h * STEP + i) * PAIR, PAIR), PAIR)]
        up = jnp.concatenate([jnp.where(row < 8, up, zero), jnp.where(row < 8, zero, up)], axis=1)
        part = dot(both, up, NT)
        d_red = part if d_red is None else d_red + part
        grads.append(dot(red, both, TN))

    @pl.when(h == 0)
    def _():
        total_ref[...] = d_red

    @pl.when(h > 0)
    def _():
        total_ref[...] += d_red

    for i in range(STEP):
        cols = pl.ds(pl.multiple_of((h * STEP + i) * PAIR, PAIR), PAIR)
        grad = low_rank_scale * jnp.concatenate([grads[i][0:8, :PAIR], grads[i][8:16, PAIR:]], axis=0)

        @pl.when(w == 0)
        def _():
            sum_ref[16:32, cols] = grad

        @pl.when(w > 0)
        def _():
            sum_ref[16:32, cols] += grad

    @pl.when(last)
    def _():
        d_reduced = (low_rank_scale * total_ref[...]).astype(half)
        d_red_ref[...] = d_reduced
        grad = dot(d_reduced, x_ref[...], TN)

        @pl.when(w == 0)
        def _():
            sum_ref[0:16, :] = grad

        @pl.when(w > 0)
        def _():
            sum_ref[0:16, :] += grad

    @pl.when(last & (w == pl.num_programs(0) - 1))
    def _():
        devices, rank, span = out_ref.shape
        shards = sum_ref.shape[1] // span
        for d in range(devices):
            m, i = d // shards, d % shards
            out_ref[d] = sum_ref[m * rank : (m + 1) * rank, i * span : (i + 1) * span]


def attend_back(qkv, g, mixed, p, x, red, ad, devices):
    _, rows, width = qkv.shape
    windows, pairs, _, length = p.shape
    block = pl.BlockSpec((length, STEP * PAIR), lambda w, h: (w, h))
    heads = [pl.BlockSpec((1, length, STEP * PAIR), lambda w, h, j=j: (j, w, h)) for j in range(3)]
    thin = pl.BlockSpec((length, 16), lambda w, h: (w, 0))
    out = (devices, ADAPTER_RANK, 4 * width // devices)
    return pl.pallas_call(
        attend_back_kernel,
        grid=(windows, pairs // STEP),
        in_specs=heads
        + [
            block,
            block,
            pl.BlockSpec((1, STEP, 2 * length, length), lambda w, h: (w, h, 0, 0)),
            pl.BlockSpec((length, width), lambda w, h: (w, 0)),
            thin,
            pl.BlockSpec(ad.shape, lambda w, h: (0, 0)),
        ],
        out_specs=[
            pl.BlockSpec((3, length, STEP * PAIR), lambda w, h: (0, w, h)),
            thin,
            pl.BlockSpec(out, lambda w, h: (0, 0, 0)),
        ],
        out_shape=[shape((3, rows, width), half), shape((rows, 16), half), shape(out, wide)],
        scratch_shapes=[pltpu.VMEM((4 * ADAPTER_RANK, width), wide), pltpu.VMEM((length, 16), wide)],
        compiler_params=params(),
        cost_estimate=cost(20),
    )(qkv, qkv, qkv, g, mixed, p, x, red, ad)


def feed_kernel(
    specs, table_ref, vec_ref, bin_ref, mixed_in, x_in, grad_in, inv_in, *refs
):
    arrays = 1 + max(i for i, _ in specs[0] + specs[1])
    block_refs = refs[:arrays]
    out_out, d_one_out, g_out = refs[arrays : arrays + 3]
    (
        fc_ref, one_ref, win_ref, wout_ref, mixed_ref, x_ref, grad_ref, inv_ref,
        normed_ref, unit_ref, spread_ref, act_ref, slope_ref, sum_ref, out_ref, sems, in_sems, out_sems,
    ) = refs[arrays + 3 :]
    devices, fc_rows, width = fc_ref.shape
    rows_all = x_ref.shape[0]
    parts = win_ref.shape[0]
    per = devices // parts
    rows = width // devices
    copies = []
    for target, spec in ((one_ref, specs[0]), (fc_ref, specs[1])):
        i = 0
        for k, start in spec:
            ref = block_refs[k]
            for b in range(ref.shape[0]):
                count = target.shape[1]
                source = ref.at[b] if ref.shape[1] == count else ref.at[b, pl.ds(start, count)]
                copies.append(pltpu.make_async_copy(source, target.at[table_ref[i]], sems.at[len(copies)]))
                i += 1
    ins = [
        pltpu.make_async_copy(source, target, in_sems.at[i])
        for i, (source, target) in enumerate(
            ((mixed_in, mixed_ref), (x_in, x_ref), (grad_in, grad_ref), (inv_in, inv_ref))
        )
    ]
    for copy in ins[:2] + copies + ins[2:]:
        copy.start()
    for copy in copies[:devices]:
        copy.wait()
    for d in range(devices):
        span = slice(rows * d, rows * (d + 1))
        for j in range(parts):
            win_ref[j, span, :] = one_ref[d, rows * j : rows * (j + 1), :]
        wout_ref[span, :] = one_ref[d, rows * parts : rows * (parts + 1), :]
    vec = vec_ref[...]
    tile = 256
    tiles = rows_all // tile
    for copy in ins[:2]:
        copy.wait()

    @pl.loop(0, tiles)
    def _(t):
        at = pl.ds(pl.multiple_of(t * tile, tile), tile)
        r = x_ref[at, :].astype(wide) + (dot(mixed_ref[at, :], wout_ref[...]) + vec[0:1])
        centred = r - row_mean(r)
        spread = lax.rsqrt(row_mean(centred * centred) + norm_eps)
        unit = centred * spread
        unit_ref[at, :] = unit
        spread_ref[at, :] = spread
        normed_ref[at, :] = (unit * vec[1:2] + vec[2:3]).astype(half)

    piece = 256

    @pl.loop(0, parts)
    def _(j):
        for n in range(width // piece):
            cols = slice(n * piece, (n + 1) * piece)
            pre = dot(normed_ref[...], win_ref[j, :, cols]) + bin_ref[j, :, cols].astype(wide)
            phi = 0.5 * (1.0 + lax.erf(pre * root_half))
            act_ref[j, :, cols] = (pre * phi).astype(half)
            slope_ref[j, :, cols] = (phi + pre * jnp.exp(-0.5 * pre * pre) * slope_const).astype(half)

    for copy in copies[devices:]:
        copy.wait()

    def second(j):
        return fc_ref[pl.ds(j * per, per)].reshape(width, width)

    sum_ref[...] = dot(act_ref[0], second(0))

    @pl.loop(1, parts)
    def _(j):
        sum_ref[...] += dot(act_ref[j], second(j))

    for copy in ins[2:]:
        copy.wait()
    d_branch_ref = normed_ref

    @pl.loop(0, tiles)
    def _(t):
        at = pl.ds(pl.multiple_of(t * tile, tile), tile)
        r = unit_ref[at, :] * vec[1:2] + vec[2:3] + (sum_ref[at, :] + vec[3:4])
        centred = r - row_mean(r)
        spread = lax.rsqrt(row_mean(centred * centred) + norm_eps)
        unit = centred * spread
        out_ref[at, :] = (unit * vec[4:5] + vec[5:6]).astype(half)
        e = grad_ref[at, :].astype(wide) * vec[4:5]
        d_two = spread * (e - row_mean(e) - unit * row_mean(e * unit))
        sum_ref[at, :] = d_two
        d_branch_ref[at, :] = d_two.astype(half)

    outs = [pltpu.make_async_copy(out_ref, out_out, out_sems.at[0])]
    outs[0].start()

    @pl.loop(0, parts)
    def _(j):
        d_act = dot(d_branch_ref[...], second(j), NT)
        d_pre = (d_act * slope_ref[j].astype(wide)).astype(half)
        sum_ref[...] += dot(d_pre, win_ref[j], NT)

    g_ref = mixed_ref

    @pl.loop(0, tiles)
    def _(t):
        at = pl.ds(pl.multiple_of(t * tile, tile), tile)
        unit_one = unit_ref[at, :]
        e = sum_ref[at, :] * vec[1:2]
        d_one = spread_ref[at, :] * (e - row_mean(e) - unit_one * row_mean(e * unit_one))
        sum_ref[at, :] = d_one
        d_mixed = dot(d_one.astype(half), wout_ref[...], NT)
        g_ref[at, :] = (d_mixed * inv_ref[at, :]).astype(half)

    outs += [
        pltpu.make_async_copy(sum_ref, d_one_out, out_sems.at[1]),
        pltpu.make_async_copy(g_ref, g_out, out_sems.at[2]),
    ]
    for copy in outs[1:]:
        copy.start()
    for copy in outs:
        copy.wait()


def feed(mixed, x, grad, inv, arrays, specs, table, vec, bias, fc_rows, one_rows):
    rows, width = x.shape
    devices = table.shape[0]
    parts = bias.shape[0]
    vmem = pltpu.VMEM
    return pl.pallas_call(
        functools.partial(feed_kernel, specs),
        in_specs=[SCALARS, pl.BlockSpec(memory_space=vmem), pl.BlockSpec(memory_space=vmem)]
        + [PLACED] * (4 + len(arrays)),
        out_specs=[PLACED] * 3,
        out_shape=[shape((rows, width), half), shape((rows, width), wide), shape((rows, width), half)],
        scratch_shapes=[
            vmem((devices, fc_rows, width), half),
            vmem((devices, one_rows, width), half),
            vmem((parts, width, width), half),
            vmem((width, width), half),
            vmem((rows, width), half),
            vmem((rows, width), half),
            vmem((rows, width), half),
            vmem((rows, width), wide),
            vmem((rows, width), half),
            vmem((rows, width), wide),
            vmem((rows, 1), wide),
            vmem((parts, rows, width), half),
            vmem((parts, rows, width), half),
            vmem((rows, width), wide),
            vmem((rows, width), half),
            pltpu.SemaphoreType.DMA((2 * devices,)),
            pltpu.SemaphoreType.DMA((4,)),
            pltpu.SemaphoreType.DMA((3,)),
        ],
        compiler_params=params(60),
        cost_estimate=cost(40),
    )(table, vec, bias, mixed, x, grad, inv, *arrays)


def project_back_kernel(d_ref, w_ref, d_one_ref, d_red_ref, ad_ref, grad_ref):
    j = pl.program_id(0)
    part = dot(d_ref[0], w_ref[0], NT)

    @pl.when(j == 0)
    def _():
        grad_ref[...] = d_one_ref[...] + dot(d_red_ref[...], ad_ref[0:16, :]) + part

    @pl.when(j > 0)
    def _():
        grad_ref[...] += part


def project_back(d_qkv, d_one, d_red, wqkv, ad):
    rows, width = d_one.shape
    single = pl.BlockSpec((rows, width), lambda i: (0, 0), pipeline_mode=pl.Buffered(1))
    return pl.pallas_call(
        project_back_kernel,
        grid=(3,),
        in_specs=[
            pl.BlockSpec((1, rows, width), lambda i: (i, 0, 0)),
            pl.BlockSpec((1, width, width), lambda i: (i, 0, 0)),
            single,
            constant(d_red.shape),
            constant(ad.shape),
        ],
        out_specs=constant((rows, width)),
        out_shape=shape((rows, width), wide),
        compiler_params=params(),
        cost_estimate=cost(8),
    )(d_qkv, wqkv, d_one, d_red, ad)


def body(
    hidden_in, grad_out, seq_lengths, key_mask, w_qkv, b_qv, w_out, b_out, ln1_gain, ln1_bias,
    w_in, b_in, w_fc, b_fc, ln2_gain, ln2_bias, adapter_weight, adapter_first, adapter_second,
):
    tok_rows, width = hidden_in.shape
    windows = seq_lengths.shape[0]
    length = tok_rows // windows
    rank = ADAPTER_RANK
    own_rows = w_out.shape[0]
    devices = width // own_rows
    ffn_parts = w_in.shape[1] // width
    block_extent = width * rank
    span = adapter_weight.shape[0] // rank
    shards = width // span

    line_a = jnp.concatenate([b_qv, b_out, ln1_gain])
    line_b = jnp.concatenate([ln1_bias, b_fc, ln2_gain, ln2_bias])
    lines = jnp.stack([b_in, line_a, line_b])
    pack_a, pack_b, pack_1 = pack(w_qkv, w_out, w_in, w_fc, adapter_weight.reshape(1, -1), lines)

    seq_ends = jnp.cumsum(seq_lengths, axis=1)
    positions = jnp.arange(length, dtype=jnp.int32)
    slot_ids = jnp.sum((positions[None, :, None] >= seq_ends[:, None, :]).astype(jnp.int32), axis=2)
    slots = seq_lengths.shape[1]
    lane = jnp.arange(FEAT, dtype=jnp.int32)[None, None, :]
    same = slot_ids[:, :, None] == lane
    padded = (key_mask.reshape(windows, length) == 0)[:, :, None]
    query_feat = jnp.where((lane <= slots) & ~same, 1.0, 0.0).astype(half)
    key_feat = jnp.where(same | ((lane == slots) & padded), masked, 0.0).astype(half)

    staged = devices == 32
    if staged:
        list_a, state = gather_attention(pack_a, pack_b)
        ring = Ring(state)
    else:
        list_a, list_1, list_2 = [[everyone(p, devices)] for p in (pack_a, pack_1, w_fc)]
    qkv, reduced, factors, vec, bias_in, wqkv = project(hidden_in, list_a, places(list_a), ffn_parts, shards)
    before = ()
    if staged:
        ring.step(reduced)
    for w in range(windows):
        before = attend(w, qkv, query_feat, key_feat, before)
        if staged:
            ring.step(before[0])
            ring.swap(before[0], w + 1)
    mixed, inv, probs = before
    if staged:
        ring.swap(mixed, 4)
        held = ring.held
        arrays = [h.array for h in held]
        specs = [[(i, w_fc.shape[0]) for i in range(len(held))], [(i, 0) for i in range(len(held))]]
    else:
        held, arrays = list_1, [list_1[0].array, list_2[0].array]
        specs = [[(0, 0)], [(1, 0)]]
    hidden_out, d_one, g = feed(
        mixed, hidden_in, grad_out, inv, arrays, specs, places(held), vec, bias_in, w_fc.shape[0], pack_1.shape[0]
    )
    d_qkv, d_reduced, partial_grad = attend_back(qkv, g, mixed, probs, hidden_in, reduced, factors, devices)
    grad_in = project_back(d_qkv, d_one, d_reduced, wqkv, factors)
    owned = lax.all_to_all(partial_grad, AXES, 0, 0, tiled=True)
    owned_grad = jnp.sum(owned, axis=0).T.reshape(-1)
    shard_len = owned_grad.shape[0]
    flat_place = lax.axis_index(AXES) * shard_len + jnp.arange(shard_len, dtype=jnp.int32)
    step_rates = jnp.where(flat_place >= 2 * block_extent, rate_second, rate_first)
    new_first = beta_one * adapter_first + (1.0 - beta_one) * owned_grad
    new_second = beta_two * adapter_second + (1.0 - beta_two) * owned_grad * owned_grad
    update = (
        new_first
        / (1.0 - beta_one**adam_step)
        / (jnp.sqrt(new_second / (1.0 - beta_two**adam_step)) + adam_eps)
    )
    new_weight = adapter_weight - step_rates * (update + decay_rate * adapter_weight)
    return (hidden_out, grad_in, new_weight, new_first, new_second)


def solution(mesh):
    rows, line = P(AXES, None), P(AXES)
    return jax.shard_map(
        body,
        mesh=mesh,
        in_specs=(
            rows, rows, rows, line, rows, line, rows, line, line, line,
            rows, line, rows, line, line, line, line, line, line,
        ),
        out_specs=(rows, rows, line, line, line),
        check_vma=False,
    )
```

time: 263 us -> 185 us (0.70)
  waiting for transfers between devices: 113 us -> 30.3 us
  starting transfers between devices: 3.27 us -> 32.7 us
  between operations: 14.2 us -> 1.07 us
  local copies, waits for them, and re-layouts: 15.9 us -> 7.08 us
    all_gather x2 -> x0, waiting for transfers between devices: 104 us -> none  [the longest x1 60.1 us: body(): all_a = lax.all_gather(pack_a, AXES, axis=0, tiled=False)]
    ppermute x0 -> x34, waiting for transfers between devices: none -> 30.3 us  [send(): return Held(lax.ppermute(self.array, AXES, pairs), owner)]
    ppermute x0 -> x34, starting transfers between devices: none -> 28.7 us  [send(): return Held(lax.ppermute(self.array, AXES, pairs), owner)]
    all_to_all x1, waiting for transfers between devices: 8.22 us -> 0.01 us  [body(): owned = lax.all_to_all(partial_grad, AXES, 0, 0, tiled=True)]
    unnamed x19 -> x57, local copies, waits for them, and re-layouts: 7.75 us -> 3.09 us
  transfers between devices with their start and end apart: 3 -> 35, of which waited for: 3 -> 12; matrix products, arithmetic and copies ran while one was open for 5% -> 3% of each run, Pallas kernels for 13% -> 21%
where the time goes in v2:
time: 185 us; the launch traced here: 184 us
  Pallas kernels  108 us (58%)
  starting transfers between devices  32.7 us (18%)
  waiting for transfers between devices  30.3 us (16%)
  local copies, waits for them, and re-layouts  7.08 us (4%)
  other arithmetic  5.11 us (3%)
    pallas_call x1, Pallas kernels, feed(): pl.pallas_call(functools.partial(feed_kernel, specs), in_specs=[SCALARS,...  42.4 us
    ppermute x34, waiting for transfers between devices, send(): return Held(lax.ppermute(self.array, AXES, pairs), owner)  30.3 us
    ppermute x34, starting transfers between devices, send(): return Held(lax.ppermute(self.array, AXES, pairs), owner)  28.7 us
    pallas_call x1, Pallas kernels, attend_back(): pl.pallas_call(attend_back_kernel, grid=(windows, pairs // STEP), in_spec...  25.1 us
    pallas_call x2, Pallas kernels, attend(): pl.pallas_call(attend_kernel, grid=(pairs // STEP,), in_specs=heads + [fe...  15.9 us
    pallas_call x1, Pallas kernels, project(): pl.pallas_call(functools.partial(project_kernel, [h.start for h in held],...  12.4 us
    pallas_call x1, Pallas kernels, project_back(): pl.pallas_call(project_back_kernel, grid=(3,), in_specs=[pl.BlockSpec((1,...  9.97 us
    all_to_all x1, starting transfers between devices, body(): owned = lax.all_to_all(partial_grad, AXES, 0, 0, tiled=True)  3.99 us
  transfers between devices with their start and end apart: 35, of which 12 were waited for; matrix products, arithmetic and copies ran while one was open for 3% of the time, Pallas kernels for 21%

profile of v2, /device:TPU:0, one launch (start us, length us, event | category | flops | bytes accessed | tf_op | source)
XLA Modules:
  0.0 184.0 jit_solution(7744053142462176885)
XLA Ops:
  4.0 2.0 %shard_map.236 = (bf16[80,768]{1,0:T(8,128)(2,1)}, bf16[224,768]{1,0:T(8,128)(2,1)}, bf16[128,768]{1,0:T(8,128)(2,1)}) custom-call(bf16[24,2304]{1,0:T(8,128)(2,1)} %wqkv_ref.1, bf16[24,768]{1,0:T(8,128)(2,1)} %wout_ref.1, bf16[24,3072]{1,0:T(8,128)(2,1)} %win_ref.1, bf16[96,768]{1,0:T(8,128)(2,1)} %wfc_ref.1, f32[1,768]{1,0:T(1,128)} %reshape.38.factor_ref, ...), custom_call_target="tpu_custom_call" | custom-call | flops 1600000000 | bytes 5000000 | tf_op jit(solution)/shard_map/pallas_call | solution.py:245
  6.0 2.9 %collective-permute-start = (bf16[1,80,768]{2,1,0:T(8,128)(2,1)}, bf16[1,80,768]{2,1,0:T(8,128)(2,1)S(1)}, u32[]{:S(2)}, u32[]{:S(2)}) collective-permute-start(bf16[1,80,768]{2,1,0:T(8,128)(2,1)} %bitcast.15), channel_id=1, source_target_pairs={{0,2},{1,5},{2,0},{3,7},{4,6},{5,1},{6,4},{7,3},{8,10},{9,13},{10,... | collective-permute-start | bytes 368648 | tf_op jit(solution)/shard_map/ppermute | solution.py:69
  8.9 1.6 collective-permute-start.2
  10.5 2.2 %collective-permute-start.3 = (bf16[1,80,768]{2,1,0:T(8,128)(2,1)}, bf16[1,80,768]{2,1,0:T(8,128)(2,1)S(1)}, u32[]{:S(2)}, u32[]{:S(2)}) collective-permute-start(bf16[1,80,768]{2,1,0:T(8,128)(2,1)} %bitcast.17), channel_id=1, source_target_pairs={{0,24},{1,25},{2,26},{3,27},{4,28},{5,29},{6,30},{7,31},{8,0},{9,1... | collective-permute-start | bytes 368648 | tf_op jit(solution)/shard_map/ppermute | solution.py:69
  13.7 1.6 collective-permute-start.1
  15.3 1.7 collective-permute-done.2
  21.4 2.8 %collective-permute-done.4 = bf16[2,80,768]{2,1,0:T(8,128)(2,1)S(1)} collective-permute-done((bf16[2,80,768]{2,1,0:T(8,128)(2,1)S(1)}, bf16[2,80,768]{2,1,0:T(8,128)(2,1)S(1)}, u32[]{:S(2)}, u32[]{:S(2)}) %collective-permute-start.4) | collective-permute-done | bytes 245792 | tf_op jit(solution)/shard_map/ppermute | solution.py:69
  25.0 1.7 collective-permute-done.5
  28.1 5.5 %collective-permute-done.6 = bf16[1,80,768]{2,1,0:T(8,128)(2,1)S(1)} collective-permute-done((bf16[1,80,768]{2,1,0:T(8,128)(2,1)S(1)}, bf16[1,80,768]{2,1,0:T(8,128)(2,1)S(1)}, u32[]{:S(2)}, u32[]{:S(2)}) %collective-permute-start.6) | collective-permute-done | bytes 122912 | tf_op jit(solution)/shard_map/ppermute | solution.py:69
  37.2 2.8 %collective-permute-done.8.refs_5_ = bf16[2,80,768]{2,1,0:T(8,128)(2,1)} collective-permute-done((bf16[2,80,768]{2,1,0:T(8,128)(2,1)S(1)}, bf16[2,80,768]{2,1,0:T(8,128)(2,1)}, u32[]{:S(2)}, u32[]{:S(2)}) %collective-permute-start.8) | collective-permute-done | bytes 245792 | tf_op jit(solution)/shard_map/ppermute | solution.py:69
  40.0 3.7 %collective-permute-done.19 = bf16[1,224,768]{2,1,0:T(8,128)(2,1)S(1)} collective-permute-done((bf16[1,224,768]{2,1,0:T(8,128)(2,1)}, bf16[1,224,768]{2,1,0:T(8,128)(2,1)S(1)}, u32[]{:S(2)}, u32[]{:S(2)}) %collective-permute-start.19) | collective-permute-done | bytes 344096 | tf_op jit(solution)/shard_map/ppermute | solution.py:69
  45.0 1.9 %collective-permute-start.16 = (bf16[2,224,768]{2,1,0:T(8,128)(2,1)S(1)}, bf16[2,224,768]{2,1,0:T(8,128)(2,1)S(1)}, u32[]{:S(2)}, u32[]{:S(2)}) collective-permute-start(bf16[2,224,768]{2,1,0:T(8,128)(2,1)S(1)} %constant_dynamic-update-slice_fusion.5.refs_0_), channel_id=1, source_target_pairs={{0,4},{1,3},{2,6},{3,1},{4,0},{5,7},{6,2},{7,5},{8,12},{9,11},{10,... | collective-permute-start | bytes 2064392 | tf_op jit(solution)/shard_map/ppermute | solution.py:69
  46.9 1.8 collective-permute-start.24
  50.3 12.4 %shard_map.237 = (bf16[3,1024,768]{2,1,0:T(8,128)(2,1)}, bf16[1024,16]{1,0:T(8,128)(2,1)}, bf16[32,768]{1,0:T(8,128)(2,1)}, f32[8,768]{1,0:T(8,128)}, bf16[4,1,7...) custom-call(s32[32]{0:T(128)} %dynamic-slice_bitcast_fusion.table_ref, bf16[1024,768]{1,0:T(8,128)(2,1)} %x_ref.3, ...), custom_call_target="tpu_custom_call" | custom-call | flops 6400000000 | bytes 20000000 | tf_op jit(solution)/shard_map/pallas_call | solution.py:322
  65.5 8.0 %shard_map.238 = (bf16[1024,768]{1,0:T(8,128)(2,1)}, f32[1024,768]{1,0:T(8,128)}, bf16[2,6,1024,512]{3,2,1,0:T(8,128)(2,1)}) custom-call(bf16[3,1024,768]{2,1,0:T(8,128)(2,1)} %get-tuple-element.52.q_ref.k_ref.v_ref, bf16[3,1024,768]{2,1,0:T(8,128)(2,1)} %get-tuple-element.52.q_ref.k_ref.v_ref, bf16[3,1024,768]{2,1,0:T(8,128)(2,1)} %get-tuple-element.52.q_ref.k_ref.v_ref, ...), custom_call_target="tpu_custom_call" | custom-call | flops 4800000000 | bytes 15000000 | tf_op jit(solution)/shard_map/pallas_call | solution.py:403
  73.7 1.6 collective-permute-start.30
  76.5 7.9 %shard_map.239 = (bf16[1024,768]{1,0:T(8,128)(2,1)}, f32[1024,768]{1,0:T(8,128)}, bf16[2,6,1024,512]{3,2,1,0:T(8,128)(2,1)}) custom-call(bf16[3,1024,768]{2,1,0:T(8,128)(2,1)} %get-tuple-element.52.q_ref.k_ref.v_ref, bf16[3,1024,768]{2,1,0:T(8,128)(2,1)} %get-tuple-element.52.q_ref.k_ref.v_ref, ...), custom_call_target="tpu_custom_call", output_to_operand_aliasing={{0}: (5, {}), {1}: (6, {}), {2}: (7, {})} | custom-call | flops 4800000000 | bytes 15000000 | tf_op jit(solution)/shard_map/pallas_call | solution.py:403
  84.5 1.8 collective-permute-start.31
  86.9 1.8 collective-permute-done.26.refs_9_
  88.7 7.4 %collective-permute-done.31.refs_13_ = bf16[2,224,768]{2,1,0:T(8,128)(2,1)} collective-permute-done((bf16[2,224,768]{2,1,0:T(8,128)(2,1)S(1)}, bf16[2,224,768]{2,1,0:T(8,128)(2,1)}, u32[]{:S(2)}, u32[]{:S(2)}) %collective-permute-start.31) | collective-permute-done | bytes 688160 | tf_op jit(solution)/shard_map/ppermute | solution.py:69
  101.5 42.4 %shard_map.240 = (bf16[1024,768]{1,0:T(8,128)(2,1)}, f32[1024,768]{1,0:T(8,128)}, bf16[1024,768]{1,0:T(8,128)(2,1)}) custom-call(s32[32]{0:T(128)} %dynamic-slice_bitcast_fusion.1.table_ref, f32[8,768]{1,0:T(8,128)} %get-tuple-element.50.vec_ref, bf16[4,1,768]{2,1,0:T(2,128)(2,1)} %get-tuple-element.51.bin_ref, ...), custom_call_target="tpu_custom_call" | custom-call | flops 32000000000 | bytes 100000000 | tf_op jit(solution)/shard_map/pallas_call | solution.py:667
  144.0 25.1 %shard_map.241 = (bf16[3,1024,768]{2,1,0:T(8,128)(2,1)}, bf16[1024,16]{1,0:T(8,128)(2,1)}, f32[32,8,96]{2,1,0:T(8,128)}) custom-call(bf16[3,1024,768]{2,1,0:T(8,128)(2,1)} %get-tuple-element.52.q_ref.k_ref.v_ref, bf16[3,1024,768]{2,1,0:T(8,128)(2,1)} %get-tuple-element.52.q_ref.k_ref.v_ref, bf16[3,1024,768]{2,1,0:T(8,128)(2,1)} %get-tuple-element.52.q_ref.k_ref.v_ref, ...), custom_call_target="tpu_custom_call" | custom-call | flops 16000000000 | bytes 50000000 | tf_op jit(solution)/shard_map/pallas_call | solution.py:510
  169.1 4.0 %all-to-all-start = ((f32[32,8,96]{2,1,0:T(8,128)}), f32[32,8,96]{2,1,0:T(8,128)S(1)}, u32[]{:S(2)}, u32[]{:S(2)}) async-start(f32[32,8,96]{2,1,0:T(8,128)} %get-tuple-element.88), calls=%async_computation | async-start | bytes 262144 | tf_op jit(solution)/shard_map/all_to_all | solution.py:790
  173.1 10.0 %shard_map.242 = f32[1024,768]{1,0:T(8,128)} custom-call(bf16[3,1024,768]{2,1,0:T(8,128)(2,1)} %get-tuple-element.84.d_ref, bf16[3,768,768]{2,1,0:T(8,128)(2,1)} %get-tuple-element.85.w_ref, f32[1024,768]{1,0:T(8,128)} %get-tuple-element.86.d_one_ref, bf16[1024,16]{1,0:T(8,128)(2,1)} %get-tuple-element.87.d_red_ref, bf16[32,768]{1,0:T(8,128)(2,1)} %get-tuple-element.83.ad_ref), custom_call_target="tpu_custom_call" | custom-call | flops 6400000000 | bytes 20000000 | tf_op jit(solution)/shard_map/pallas_call | solution.py:714
  (133 shorter events, 28.4 us)
Async XLA Ops:
  8.9 8.1 %collective-permute-start.2 = (bf16[1,80,768]{2,1,0:T(8,128)(2,1)}, bf16[1,80,768]{2,1,0:T(8,128)(2,1)S(1)}, u32[]{:S(2)}, u32[]{:S(2)}) collective-permute-start(bf16[1,80,768]{2,1,0:T(8,128)(2,1)} %bitcast.16), channel_id=1, source_target_pairs={{0,8},{1,9},{2,10},{3,11},{4,12},{5,13},{6,14},{7,15},{8,16},{9,17... | collective-permute-start | bytes 368648 | tf_op jit(solution)/shard_map/ppermute | solution.py:69
  10.5 7.4 %collective-permute-start.3 = (bf16[1,80,768]{2,1,0:T(8,128)(2,1)}, bf16[1,80,768]{2,1,0:T(8,128)(2,1)S(1)}, u32[]{:S(2)}, u32[]{:S(2)}) collective-permute-start(bf16[1,80,768]{2,1,0:T(8,128)(2,1)} %bitcast.17), channel_id=1, source_target_pairs={{0,24},{1,25},{2,26},{3,27},{4,28},{5,29},{6,30},{7,31},{8,0},{9,1... | collective-permute-start | bytes 368648 | tf_op jit(solution)/shard_map/ppermute | solution.py:69
  13.7 7.7 %collective-permute-start.1 = (bf16[2,80,768]{2,1,0:T(8,128)(2,1)S(1)}, bf16[2,80,768]{2,1,0:T(8,128)(2,1)S(1)}, u32[]{:S(2)}, u32[]{:S(2)}) collective-permute-start(bf16[2,80,768]{2,1,0:T(8,128)(2,1)S(1)} %pad_maximum_fusion.refs_0_), channel_id=1, source_target_pairs={{0,4},{1,3},{2,6},{3,1},{4,0},{5,7},{6,2},{7,5},{8,12},{9,11},{10,... | collective-permute-start | bytes 737288 | tf_op jit(solution)/shard_map/ppermute | solution.py:69
  20.7 14.7 %collective-permute-start.15 = (bf16[1,224,768]{2,1,0:T(8,128)(2,1)}, bf16[1,224,768]{2,1,0:T(8,128)(2,1)S(1)}, u32[]{:S(2)}, u32[]{:S(2)}) collective-permute-start(bf16[1,224,768]{2,1,0:T(8,128)(2,1)} %bitcast.12), channel_id=1, source_target_pairs={{0,2},{1,5},{2,0},{3,7},{4,6},{5,1},{6,4},{7,3},{8,10},{9,13},{10,... | collective-permute-start | bytes 1032200 | tf_op jit(solution)/shard_map/ppermute | solution.py:69
  24.2 11.3 %collective-permute-start.7 = (bf16[4,80,768]{2,1,0:T(8,128)(2,1)S(1)}, bf16[4,80,768]{2,1,0:T(8,128)(2,1)S(1)}, u32[]{:S(2)}, u32[]{:S(2)}) collective-permute-start(bf16[4,80,768]{2,1,0:T(8,128)(2,1)S(1)} %constant_dynamic-update-slice_fusion.refs_2_), channel_id=1, source_target_pairs={{0,4},{1,3},{2,6},{3,1},{4,0},{5,7},{6,2},{7,5},{8,12},{9,11},{10,... | collective-permute-start | bytes 1474568 | tf_op jit(solution)/shard_map/ppermute | solution.py:69
  28.0 9.1 %collective-permute-start.9 = (bf16[2,80,768]{2,1,0:T(8,128)(2,1)S(1)}, bf16[2,80,768]{2,1,0:T(8,128)(2,1)S(1)}, u32[]{:S(2)}, u32[]{:S(2)}) collective-permute-start(bf16[2,80,768]{2,1,0:T(8,128)(2,1)S(1)} %pad_maximum_fusion.refs_0_), channel_id=1, source_target_pairs={{0,1},{1,0},{2,3},{3,2},{4,5},{5,4},{6,7},{7,6},{8,9},{9,8},{10,11... | collective-permute-start | bytes 737288 | tf_op jit(solution)/shard_map/ppermute | solution.py:69
  34.4 9.4 %collective-permute-start.19 = (bf16[1,224,768]{2,1,0:T(8,128)(2,1)}, bf16[1,224,768]{2,1,0:T(8,128)(2,1)S(1)}, u32[]{:S(2)}, u32[]{:S(2)}) collective-permute-start(bf16[1,224,768]{2,1,0:T(8,128)(2,1)} %bitcast.13), channel_id=1, source_target_pairs={{0,8},{1,25},{2,10},{3,27},{4,12},{5,29},{6,14},{7,31},{8,16},{9,1... | collective-permute-start | bytes 1032200 | tf_op jit(solution)/shard_map/ppermute | solution.py:69
  35.4 13.3 %collective-permute-start.11 = (bf16[4,80,768]{2,1,0:T(8,128)(2,1)S(1)}, bf16[4,80,768]{2,1,0:T(8,128)(2,1)S(1)}, u32[]{:S(2)}, u32[]{:S(2)}) collective-permute-start(bf16[4,80,768]{2,1,0:T(8,128)(2,1)S(1)} %constant_dynamic-update-slice_fusion.refs_2_), channel_id=1, source_target_pairs={{0,1},{1,0},{2,3},{3,2},{4,5},{5,4},{6,7},{7,6},{8,9},{9,8},{10,11... | collective-permute-start | bytes 1474568 | tf_op jit(solution)/shard_map/ppermute | solution.py:69
  35.5 13.5 %collective-permute-start.13 = (bf16[4,80,768]{2,1,0:T(8,128)(2,1)S(1)}, bf16[4,80,768]{2,1,0:T(8,128)(2,1)S(1)}, u32[]{:S(2)}, u32[]{:S(2)}) collective-permute-start(bf16[4,80,768]{2,1,0:T(8,128)(2,1)S(1)} %collective-permute-done.7.refs_4_), channel_id=1, source_target_pairs={{0,1},{1,0},{2,3},{3,2},{4,5},{5,4},{6,7},{7,6},{8,9},{9,8},{10,11... | collective-permute-start | bytes 1474568 | tf_op jit(solution)/shard_map/ppermute | solution.py:69
  37.1 7.9 %collective-permute-start.10 = (bf16[2,80,768]{2,1,0:T(8,128)(2,1)S(1)}, bf16[2,80,768]{2,1,0:T(8,128)(2,1)S(1)}, u32[]{:S(2)}, u32[]{:S(2)}) collective-permute-start(bf16[2,80,768]{2,1,0:T(8,128)(2,1)S(1)} %collective-permute-done.1.refs_1_), channel_id=1, source_target_pairs={{0,1},{1,0},{2,3},{3,2},{4,5},{5,4},{6,7},{7,6},{8,9},{9,8},{10,11... | collective-permute-start | bytes 737288 | tf_op jit(solution)/shard_map/ppermute | solution.py:69
  45.0 28.4 %collective-permute-start.16 = (bf16[2,224,768]{2,1,0:T(8,128)(2,1)S(1)}, bf16[2,224,768]{2,1,0:T(8,128)(2,1)S(1)}, u32[]{:S(2)}, u32[]{:S(2)}) collective-permute-start(bf16[2,224,768]{2,1,0:T(8,128)(2,1)S(1)} %constant_dynamic-update-slice_fusion.5.refs_0_), channel_id=1, source_target_pairs={{0,4},{1,3},{2,6},{3,1},{4,0},{5,7},{6,2},{7,5},{8,12},{9,11},{10,... | collective-permute-start | bytes 2064392 | tf_op jit(solution)/shard_map/ppermute | solution.py:69
  46.9 15.8 %collective-permute-start.24 = (bf16[1,224,768]{2,1,0:T(8,128)(2,1)S(1)}, bf16[1,224,768]{2,1,0:T(8,128)(2,1)S(1)}, u32[]{:S(2)}, u32[]{:S(2)}) collective-permute-start(bf16[1,224,768]{2,1,0:T(8,128)(2,1)S(1)} %collective-permute-done.19), channel_id=1, source_target_pairs={{0,8},{1,25},{2,10},{3,27},{4,12},{5,29},{6,14},{7,31},{8,16},{9,1... | collective-permute-start | bytes 1032200 | tf_op jit(solution)/shard_map/ppermute | solution.py:69
  48.7 16.6 %collective-permute-start.20 = (bf16[1,224,768]{2,1,0:T(8,128)(2,1)S(1)}, bf16[1,224,768]{2,1,0:T(8,128)(2,1)S(1)}, u32[]{:S(2)}, u32[]{:S(2)}) collective-permute-start(bf16[1,224,768]{2,1,0:T(8,128)(2,1)S(1)} %collective-permute-done.19), channel_id=1, source_target_pairs={{0,2},{1,5},{2,0},{3,7},{4,6},{5,1},{6,4},{7,3},{8,10},{9,13},{10,... | collective-permute-start | bytes 1032200 | tf_op jit(solution)/shard_map/ppermute | solution.py:69
  62.7 10.8 %collective-permute-start.25 = (bf16[1,224,768]{2,1,0:T(8,128)(2,1)S(1)}, bf16[1,224,768]{2,1,0:T(8,128)(2,1)S(1)}, u32[]{:S(2)}, u32[]{:S(2)}) collective-permute-start(bf16[1,224,768]{2,1,0:T(8,128)(2,1)S(1)} %collective-permute-done.24), channel_id=1, source_target_pairs={{0,2},{1,5},{2,0},{3,7},{4,6},{5,1},{6,4},{7,3},{8,10},{9,13},{10,... | collective-permute-start | bytes 1032200 | tf_op jit(solution)/shard_map/ppermute | solution.py:69
  64.0 9.7 %collective-permute-start.29 = (bf16[1,224,768]{2,1,0:T(8,128)(2,1)S(1)}, bf16[1,224,768]{2,1,0:T(8,128)(2,1)S(1)}, u32[]{:S(2)}, u32[]{:S(2)}) collective-permute-start(bf16[1,224,768]{2,1,0:T(8,128)(2,1)S(1)} %collective-permute-done.24), channel_id=1, source_target_pairs={{0,8},{1,25},{2,10},{3,27},{4,12},{5,29},{6,14},{7,31},{8,16},{9,1... | collective-permute-start | bytes 1032200 | tf_op jit(solution)/shard_map/ppermute | solution.py:69
  65.3 21.5 %collective-permute-start.21 = (bf16[2,224,768]{2,1,0:T(8,128)(2,1)S(1)}, bf16[2,224,768]{2,1,0:T(8,128)(2,1)S(1)}, u32[]{:S(2)}, u32[]{:S(2)}) collective-permute-start(bf16[2,224,768]{2,1,0:T(8,128)(2,1)S(1)} %constant_dynamic-update-slice_fusion.7.refs_4_), channel_id=1, source_target_pairs={{0,4},{1,3},{2,6},{3,1},{4,0},{5,7},{6,2},{7,5},{8,12},{9,11},{10,... | collective-permute-start | bytes 2064392 | tf_op jit(solution)/shard_map/ppermute | solution.py:69
  73.7 10.7 %collective-permute-start.30 = (bf16[1,224,768]{2,1,0:T(8,128)(2,1)S(1)}, bf16[1,224,768]{2,1,0:T(8,128)(2,1)S(1)}, u32[]{:S(2)}, u32[]{:S(2)}) collective-permute-start(bf16[1,224,768]{2,1,0:T(8,128)(2,1)S(1)} %collective-permute-done.29), channel_id=1, source_target_pairs={{0,2},{1,5},{2,0},{3,7},{4,6},{5,1},{6,4},{7,3},{8,10},{9,13},{10,... | collective-permute-start | bytes 1032200 | tf_op jit(solution)/shard_map/ppermute | solution.py:69
  75.4 13.3 %collective-permute-start.26 = (bf16[2,224,768]{2,1,0:T(8,128)(2,1)S(1)}, bf16[2,224,768]{2,1,0:T(8,128)(2,1)}, u32[]{:S(2)}, u32[]{:S(2)}) collective-permute-start(bf16[2,224,768]{2,1,0:T(8,128)(2,1)S(1)} %constant_dynamic-update-slice_fusion.9.refs_8_), channel_id=1, source_target_pairs={{0,4},{1,3},{2,6},{3,1},{4,0},{5,7},{6,2},{7,5},{8,12},{9,11},{10,... | collective-permute-start | bytes 2064392 | tf_op jit(solution)/shard_map/ppermute | solution.py:69
  84.5 11.6 %collective-permute-start.31 = (bf16[2,224,768]{2,1,0:T(8,128)(2,1)S(1)}, bf16[2,224,768]{2,1,0:T(8,128)(2,1)}, u32[]{:S(2)}, u32[]{:S(2)}) collective-permute-start(bf16[2,224,768]{2,1,0:T(8,128)(2,1)S(1)} %constant_dynamic-update-slice_fusion.11.refs_12_), channel_id=1, source_target_pairs={{0,4},{1,3},{2,6},{3,1},{4,0},{5,7},{6,2},{7,5},{8,12},{9,11},{10,... | collective-permute-start | bytes 2064392 | tf_op jit(solution)/shard_map/ppermute | solution.py:69
  86.3 9.8 %collective-permute-start.17 = (bf16[2,224,768]{2,1,0:T(8,128)(2,1)S(1)}, bf16[2,224,768]{2,1,0:T(8,128)(2,1)S(1)}, u32[]{:S(2)}, u32[]{:S(2)}) collective-permute-start(bf16[2,224,768]{2,1,0:T(8,128)(2,1)S(1)} %constant_dynamic-update-slice_fusion.5.refs_0_), channel_id=1, source_target_pairs={{0,1},{1,0},{2,3},{3,2},{4,5},{5,4},{6,7},{7,6},{8,9},{9,8},{10,11... | collective-permute-start | bytes 2064392 | tf_op jit(solution)/shard_map/ppermute | solution.py:69
  86.3 10.3 %collective-permute-start.18 = (bf16[2,224,768]{2,1,0:T(8,128)(2,1)S(1)}, bf16[2,224,768]{2,1,0:T(8,128)(2,1)S(1)}, u32[]{:S(2)}, u32[]{:S(2)}) collective-permute-start(bf16[2,224,768]{2,1,0:T(8,128)(2,1)S(1)} %collective-permute-done.16.refs_1_), channel_id=1, source_target_pairs={{0,1},{1,0},{2,3},{3,2},{4,5},{5,4},{6,7},{7,6},{8,9},{9,8},{10,11... | collective-permute-start | bytes 2064392 | tf_op jit(solution)/shard_map/ppermute | solution.py:69
  86.8 9.9 %collective-permute-start.22 = (bf16[2,224,768]{2,1,0:T(8,128)(2,1)S(1)}, bf16[2,224,768]{2,1,0:T(8,128)(2,1)S(1)}, u32[]{:S(2)}, u32[]{:S(2)}) collective-permute-start(bf16[2,224,768]{2,1,0:T(8,128)(2,1)S(1)} %constant_dynamic-update-slice_fusion.7.refs_4_), channel_id=1, source_target_pairs={{0,1},{1,0},{2,3},{3,2},{4,5},{5,4},{6,7},{7,6},{8,9},{9,8},{10,11... | collective-permute-start | bytes 2064392 | tf_op jit(solution)/shard_map/ppermute | solution.py:69
  88.7 11.1 %collective-permute-start.23 = (bf16[2,224,768]{2,1,0:T(8,128)(2,1)S(1)}, bf16[2,224,768]{2,1,0:T(8,128)(2,1)}, u32[]{:S(2)}, u32[]{:S(2)}) collective-permute-start(bf16[2,224,768]{2,1,0:T(8,128)(2,1)S(1)} %collective-permute-done.21.refs_5_), channel_id=1, source_target_pairs={{0,1},{1,0},{2,3},{3,2},{4,5},{5,4},{6,7},{7,6},{8,9},{9,8},{10,11... | collective-permute-start | bytes 2064392 | tf_op jit(solution)/shard_map/ppermute | solution.py:69
  169.1 14.0 %all-to-all-start = ((f32[32,8,96]{2,1,0:T(8,128)}), f32[32,8,96]{2,1,0:T(8,128)S(1)}, u32[]{:S(2)}, u32[]{:S(2)}) async-start(f32[32,8,96]{2,1,0:T(8,128)} %get-tuple-element.88), calls=%async_computation | async-start | bytes 262144 | tf_op jit(solution)/shard_map/all_to_all | solution.py:790
  (36 other events, 434.1 us)

commit v3 on v2

--- a/solution.py
+++ b/solution.py
@@ -22,6 +22,7 @@
 rate_second = 0.032
 slope_const = 0.3989422804014327
 root_half = 0.7071067811865476
+half_log2e = -0.7213475204444817
 masked = -1e30
 
 half = jnp.bfloat16
@@ -40,6 +41,9 @@
     return lax.dot_general(left, right, dims, preferred_element_type=wide)
 
 
+LIMITS = 28, 24, 56, 30, 30
+
+
 def params(mib=58):
     return pltpu.CompilerParams(vmem_limit_bytes=mib * 2**20)
 
@@ -49,7 +53,11 @@
 
 
 def shape(dims, dtype):
-    return jax.ShapeDtypeStruct(dims, dtype)
+    return pltpu.HBM(dims, dtype)
+
+
+def near(dims, dtype):
+    return pltpu.VMEM(dims, dtype)
 
 
 def row_mean(values):
@@ -126,30 +134,30 @@
 
 def gather_attention(pack_a, pack_b):
     a, b = own(pack_a, 32), own(pack_b, 32)
-    near = [a.send(up), a.send(down)]
+    close = [a.send(up), a.send(down)]
     ways = a.send(first_way)
-    far = a.send(across)
+    far = far_first = a.send(across)
     b_ways = b.send(first_way)
     a_own = join(a, ways)
     a_own2 = a_own.send(second_way)
-    near = join(*near)
-    near_ways = near.send(first_way)
-    far_ways = after(far, near_ways).send(first_way)
-    near = join(near, after(near_ways, a_own2))
-    near2 = near.send(second_way)
+    close = join(*close)
+    close_ways = close.send(first_way)
+    far_ways = far.send(first_way)
+    close = join(close, close_ways)
+    close2 = close.send(second_way)
     far = join(far, far_ways)
     far2 = far.send(second_way)
-    held = [a_own, a_own2, near, far, near2, far2]
+    held = [a_own, a_own2, close, far, close2, far2]
     held += [h.send(other_core) for h in held]
-    return held, (b, b_ways, far_ways, far2)
+    return held, (b, b_ways, far_first, far2)
 
 
 class Ring:
     def __init__(self, state):
-        b, b_ways, far_ways, far2 = state
+        b, b_ways, far, far2 = state
         gate = far2.array
         self.held = []
-        self.now = after(b, far_ways).send(along)
+        self.now = after(b, far).send(along)
         self.ways = [join_after(gate, b, b_ways)]
         self.seconds = [self.ways[0].send(second_way)]
         self.waiting = []
@@ -192,42 +200,39 @@
     return lax.dynamic_index_in_dim(jnp.asarray(table, jnp.int32), lax.axis_index(AXES), 0, keepdims=False)
 
 
-def place_blocks(starts, table_ref, block_refs, all_ref, sems):
-    copies = []
-    rows = all_ref.shape[1]
-    for start, ref in zip(starts, block_refs):
+def place_blocks(table_ref, block_refs, all_ref):
+    i = 0
+    for ref in block_refs:
         for b in range(ref.shape[0]):
-            i = len(copies)
-            source = ref.at[b] if ref.shape[1] == rows else ref.at[b, pl.ds(start, rows)]
-            copies.append(pltpu.make_async_copy(source, all_ref.at[table_ref[i]], sems.at[i]))
-    return copies
-
-
-def run(copies):
-    for copy in copies:
-        copy.start()
-    for copy in copies:
-        copy.wait()
+            all_ref[table_ref[i]] = ref[b]
+            i += 1
 
 
 SCALARS = pl.BlockSpec(memory_space=pltpu.SMEM)
 PLACED = pl.BlockSpec(memory_space=pl.ANY)
-
-
-def pack_kernel(span, wqkv_ref, wout_ref, win_ref, wfc_ref, factor_ref, lines_ref, a_ref, b_ref, one_ref):
+NEAR = pl.BlockSpec(memory_space=pltpu.VMEM)
+
+
+def pack_kernel(span, wqkv_ref, wout_ref, win_ref, wfc_ref, factor_ref, *refs):
+    line_refs, (a_ref, b_ref, one_ref) = refs[:-3], refs[-3:]
     rows, width = wout_ref.shape
     for j in range(3):
         a_ref[rows * j : rows * (j + 1), :] = wqkv_ref[:, width * j : width * (j + 1)]
     rank = ADAPTER_RANK
-    count = factor_ref.shape[1]
+    count = factor_ref.shape[0]
     lane = lax.broadcasted_iota(jnp.int32, (rank, count), 1)
     row = lax.broadcasted_iota(jnp.int32, (rank, count), 0)
-    spread = jnp.where(lane % rank == row, factor_ref[...].astype(half).astype(wide), 0.0).astype(half)
+    spread = jnp.where(lane % rank == row, factor_ref[...].reshape(1, count).astype(half).astype(wide), 0.0).astype(half)
     place = lax.broadcasted_iota(jnp.int32, (count, PAIR), 0) // rank
     take = (place == lax.broadcasted_iota(jnp.int32, (count, PAIR), 1)).astype(wide).astype(half)
     a_ref[3 * rows :, :PAIR] = dot(spread, take).astype(half)
     a_ref[3 * rows :, PAIR : 2 * PAIR] = jnp.zeros((rank, PAIR), half)
-    a_ref[3 * rows : 3 * rows + 3, PAIR : PAIR + span] = lines_ref[...]
+    for i, line in enumerate(LINES):
+        at = PAIR
+        for k in line:
+            n = line_refs[k].shape[0]
+            a_ref[3 * rows + i : 3 * rows + i + 1, at : at + n] = line_refs[k][...].reshape(1, n)
+            at += n
     a_ref[3 * rows :, 2 * PAIR :] = jnp.zeros((rank, width - 2 * PAIR), half)
     split = wfc_ref.shape[0]
     one_ref[...] = jnp.zeros_like(one_ref)
@@ -238,20 +243,23 @@
     b_ref[split:, :] = one_ref[...]
 
 
-def pack(w_qkv, w_out, w_in, w_fc, factor, lines):
+LINES = (0,), (1, 2, 3), (4, 5, 6, 7)
+
+
+def pack(w_qkv, w_out, w_in, w_fc, factor, vectors):
     rows, width = w_out.shape
     one_rows = w_fc.shape[0] + rows
     one_rows += (-one_rows) % 16
     return pl.pallas_call(
-        functools.partial(pack_kernel, lines.shape[1]),
+        functools.partial(pack_kernel, factor.shape[0] // ADAPTER_RANK),
         out_shape=[
-            shape((3 * rows + ADAPTER_RANK, width), half),
-            shape((w_fc.shape[0] + one_rows, width), half),
-            shape((one_rows, width), half),
+            jax.ShapeDtypeStruct((3 * rows + ADAPTER_RANK, width), half),
+            jax.ShapeDtypeStruct((w_fc.shape[0] + one_rows, width), half),
+            jax.ShapeDtypeStruct((one_rows, width), half),
         ],
         compiler_params=params(),
         cost_estimate=cost(2),
-    )(w_qkv, w_out, w_in, w_fc, factor, lines)
+    )(w_qkv, w_out, w_in, w_fc, factor, *vectors)
 
 
 def unfold(pieces, piece, per):
@@ -267,10 +275,9 @@
     return jnp.sum(jnp.where((shard == place)[None], spread, 0.0), axis=1)
 
 
-def project_kernel(starts, shards, table_ref, x_ref, *refs):
-    blocks = len(starts)
+def project_kernel(blocks, shards, table_ref, x_ref, *refs):
     block_refs = refs[:blocks]
-    qkv_ref, red_ref, ad_ref, vec_ref, bin_ref, wout_ref, ga_ref, w_ref, bias_ref, sems, sem = refs[blocks:]
+    qkv_ref, far_ref, red_ref, ad_ref, vec_ref, bin_ref, wout_ref, ga_ref, w_ref, bias_ref, sem, sems = refs[blocks:]
     devices = ga_ref.shape[0]
     width = x_ref.shape[1]
     rows = width // devices
@@ -278,7 +285,7 @@
 
     @pl.when(pl.program_id(0) == 0)
     def _():
-        run(place_blocks(starts, table_ref, block_refs, ga_ref, sems))
+        place_blocks(table_ref, block_refs, ga_ref)
         for d in range(devices):
             span = slice(rows * d, rows * d + rows)
             for j in range(3):
@@ -305,11 +312,14 @@
     wide_row = dot(x_ref[...], w_ref[j]) + bias_ref[j]
     wide_row += low_rank_scale * dot(own_lanes, ad_ref[16:32, :])
     scale = jnp.where(j == 0, 0.125, 1.0)
-    qkv_ref[0] = (wide_row.astype(half).astype(wide) * scale).astype(half)
+    qkv_ref[j] = (wide_row.astype(half).astype(wide) * scale).astype(half)
+    pltpu.make_async_copy(qkv_ref.at[j], far_ref.at[j], sems.at[j]).start()
 
     @pl.when(j == pl.num_programs(0) - 1)
     def _():
         keep.wait()
+        for i in range(3):
+            pltpu.make_async_copy(qkv_ref.at[i], far_ref.at[i], sems.at[i]).wait()
 
 
 def constant(dims):
@@ -320,11 +330,12 @@
     rows, width = x.shape
     devices = held[0].owner.shape[0]
     return pl.pallas_call(
-        functools.partial(project_kernel, [h.start for h in held], shards),
+        functools.partial(project_kernel, len(held), shards),
         grid=(3,),
-        in_specs=[SCALARS, constant(x.shape)] + [PLACED] * len(held),
+        in_specs=[SCALARS, NEAR] + [NEAR] * len(held),
         out_specs=[
-            pl.BlockSpec((1, rows, width), lambda i: (i, 0, 0)),
+            NEAR,
+            PLACED,
             constant((rows, 16)),
             constant((4 * ADAPTER_RANK, width)),
             constant((8, width)),
@@ -332,6 +343,7 @@
             PLACED,
         ],
         out_shape=[
+            near((3, rows, width), half),
             shape((3, rows, width), half),
             shape((rows, 16), half),
             shape((4 * ADAPTER_RANK, width), half),
@@ -343,10 +355,10 @@
             pltpu.VMEM((devices, 3 * (width // devices) + ADAPTER_RANK, width), half),
             pltpu.VMEM((3, width, width), half),
             pltpu.VMEM((3, 1, width), wide),
-            pltpu.SemaphoreType.DMA((devices,)),
             pltpu.SemaphoreType.DMA,
-        ],
-        compiler_params=params(),
+            pltpu.SemaphoreType.DMA((3,)),
+        ],
+        compiler_params=params(LIMITS[0]),
         cost_estimate=cost(8),
     )(table, x, *[h.array for h in held])
 
@@ -411,21 +423,18 @@
             shape((windows, pairs, 2 * length, length), half),
         ],
         input_output_aliases={5 + i: i for i in range(len(before))},
-        compiler_params=params(),
+        compiler_params=params(LIMITS[1]),
         cost_estimate=cost(6),
     )(qkv, qkv, qkv, fq, fk, *before)
 
 
 def attend_back_kernel(
-    q_ref, k_ref, v_ref, g_ref, mixed_ref, p_ref, x_ref, red_ref, ad_ref, d_ref, d_red_ref, out_ref, sum_ref, total_ref
+    q_ref, k_ref, v_ref, g_ref, mixed_ref, p_ref, x_ref, red_ref, ad_ref, d_ref, d_red_ref, out_ref, sum_ref, keep_ref
 ):
     length = q_ref.shape[1]
     low = low_lanes(length)
     w, h = pl.program_id(0), pl.program_id(1)
     last = h == pl.num_programs(1) - 1
-    row = lax.broadcasted_iota(jnp.int32, (16, PAIR), 0)
-    red = red_ref[...]
-    zero = jnp.zeros((16, PAIR), half)
 
     def d_probs_of(i):
         lanes = slice(i * PAIR, (i + 1) * PAIR)
@@ -435,61 +444,53 @@
         return dot(apart(g2, low), v_ref[0, :, lanes], NT), centre
 
     d_probs = [d_probs_of(i) for i in range(STEP)]
-    d_red = None
-    grads = []
     for i in range(STEP):
         lanes = slice(i * PAIR, (i + 1) * PAIR)
         p = p_ref[0, i]
         raw, centre = d_probs[i]
         ds = (p.astype(wide) * (raw - centre)).astype(half)
         q_t, g_t = q_ref[0, :, lanes].T, g_ref[:, lanes].T
-        dv = [dot(g_t[64 * n : 64 * n + 64], p[n * length : (n + 1) * length]) for n in range(2)]
-        dk = [dot(q_t[64 * n : 64 * n + 64], ds[n * length : (n + 1) * length]) for n in range(2)]
+
+        def own_rows(left, both):
+            return jnp.concatenate(
+                [dot(left, both[n * length : (n + 1) * length])[64 * n : 64 * n + 64] for n in range(2)], axis=0
+            )
+
+        dv = own_rows(g_t, p).astype(half).T
+        dk = own_rows(q_t, ds).astype(half).T
         dq = (together(dot(ds, k_ref[0, :, lanes]), low) * 0.125).astype(half)
-        dv = jnp.concatenate(dv, axis=0).astype(half).T
         d_ref[0, :, lanes] = dq
-        d_ref[1, :, lanes] = jnp.concatenate(dk, axis=0).astype(half).T
+        d_ref[1, :, lanes] = dk
         d_ref[2, :, lanes] = dv
-        both = jnp.concatenate([dq, dv], axis=1)
-        up = ad_ref[16:32, pl.ds(pl.multiple_of((h * STEP + i) * PAIR, PAIR), PAIR)]
-        up = jnp.concatenate([jnp.where(row < 8, up, zero), jnp.where(row < 8, zero, up)], axis=1)
-        part = dot(both, up, NT)
-        d_red = part if d_red is None else d_red + part
-        grads.append(dot(red, both, TN))
-
-    @pl.when(h == 0)
+        cols = pl.ds(pl.multiple_of((h * STEP + i) * PAIR, PAIR), PAIR)
+        keep_ref[0, :, cols] = dq
+        keep_ref[1, :, cols] = dv
+
+    @pl.when(last)
     def _():
-        total_ref[...] = d_red
-
-    @pl.when(h > 0)
-    def _():
-        total_ref[...] += d_red
-
-    for i in range(STEP):
-        cols = pl.ds(pl.multiple_of((h * STEP + i) * PAIR, PAIR), PAIR)
-        grad = low_rank_scale * jnp.concatenate([grads[i][0:8, :PAIR], grads[i][8:16, PAIR:]], axis=0)
+        dq, dv = keep_ref[0], keep_ref[1]
+        up, red = ad_ref[16:32, :], red_ref[...]
+        row = lax.broadcasted_iota(jnp.int32, up.shape, 0)
+        none = jnp.zeros_like(up)
+        d_red = dot(dq, jnp.where(row < 8, up, none), NT) + dot(dv, jnp.where(row < 8, none, up), NT)
+        d_red = (low_rank_scale * d_red).astype(half)
+        d_red_ref[...] = d_red
+        grad = jnp.concatenate(
+            [
+                dot(d_red, x_ref[...], TN),
+                low_rank_scale * dot(red, dq, TN)[0:8],
+                low_rank_scale * dot(red, dv, TN)[8:16],
+            ],
+            axis=0,
+        )
 
         @pl.when(w == 0)
         def _():
-            sum_ref[16:32, cols] = grad
+            sum_ref[...] = grad
 
         @pl.when(w > 0)
         def _():
-            sum_ref[16:32, cols] += grad
-
-    @pl.when(last)
-    def _():
-        d_reduced = (low_rank_scale * total_ref[...]).astype(half)
-        d_red_ref[...] = d_reduced
-        grad = dot(d_reduced, x_ref[...], TN)
-
-        @pl.when(w == 0)
-        def _():
-            sum_ref[0:16, :] = grad
-
-        @pl.when(w > 0)
-        def _():
-            sum_ref[0:16, :] += grad
+            sum_ref[...] += grad
 
     @pl.when(last & (w == pl.num_programs(0) - 1))
     def _():
@@ -525,81 +526,73 @@
             pl.BlockSpec(out, lambda w, h: (0, 0, 0)),
         ],
         out_shape=[shape((3, rows, width), half), shape((rows, 16), half), shape(out, wide)],
-        scratch_shapes=[pltpu.VMEM((4 * ADAPTER_RANK, width), wide), pltpu.VMEM((length, 16), wide)],
-        compiler_params=params(),
+        scratch_shapes=[pltpu.VMEM((4 * ADAPTER_RANK, width), wide), pltpu.VMEM((2, length, width), half)],
+        compiler_params=params(LIMITS[3]),
         cost_estimate=cost(20),
-    )(qkv, qkv, qkv, g, mixed, p, x, red, ad)
-
-
-def feed_kernel(
-    specs, table_ref, vec_ref, bin_ref, mixed_in, x_in, grad_in, inv_in, *refs
-):
-    arrays = 1 + max(i for i, _ in specs[0] + specs[1])
+    )(*[pltpu.with_memory_space_constraint(t, pltpu.HBM) for t in (qkv, qkv, qkv, g, mixed, p, x)], red, ad)
+
+
+def feed_kernel(specs, table_ref, vec_ref, bin_ref, mixed_ref, x_ref, grad_ref, inv_ref, *refs):
+    arrays = 1 + max(i for spec in specs for i, _ in spec)
     block_refs = refs[:arrays]
     out_out, d_one_out, g_out = refs[arrays : arrays + 3]
     (
-        fc_ref, one_ref, win_ref, wout_ref, mixed_ref, x_ref, grad_ref, inv_ref,
-        normed_ref, unit_ref, spread_ref, act_ref, slope_ref, sum_ref, out_ref, sems, in_sems, out_sems,
+        wo_ref, one_ref, fc_ref, win_ref, wout_ref,
+        normed_ref, unit_ref, act_ref, slope_ref, sum_ref, out_ref, d_pre_ref, sems, out_sems,
     ) = refs[arrays + 3 :]
-    devices, fc_rows, width = fc_ref.shape
-    rows_all = x_ref.shape[0]
+    devices = fc_ref.shape[0]
+    rows_all, width = x_ref.shape
     parts = win_ref.shape[0]
     per = devices // parts
     rows = width // devices
     copies = []
-    for target, spec in ((one_ref, specs[0]), (fc_ref, specs[1])):
-        i = 0
+    for n, (target, spec) in enumerate(zip((wo_ref, one_ref, fc_ref), specs)):
+        count = target.shape[1]
+        some = []
         for k, start in spec:
             ref = block_refs[k]
             for b in range(ref.shape[0]):
-                count = target.shape[1]
                 source = ref.at[b] if ref.shape[1] == count else ref.at[b, pl.ds(start, count)]
-                copies.append(pltpu.make_async_copy(source, target.at[table_ref[i]], sems.at[len(copies)]))
-                i += 1
-    ins = [
-        pltpu.make_async_copy(source, target, in_sems.at[i])
-        for i, (source, target) in enumerate(
-            ((mixed_in, mixed_ref), (x_in, x_ref), (grad_in, grad_ref), (inv_in, inv_ref))
-        )
-    ]
-    for copy in ins[:2] + copies + ins[2:]:
+                i = len(some)
+                some.append(pltpu.make_async_copy(source, target.at[table_ref[i]], sems.at[n, i]))
+        copies.append(some)
+    for copy in copies[0]:
         copy.start()
-    for copy in copies[:devices]:
-        copy.wait()
-    for d in range(devices):
-        span = slice(rows * d, rows * (d + 1))
-        for j in range(parts):
-            win_ref[j, span, :] = one_ref[d, rows * j : rows * (j + 1), :]
-        wout_ref[span, :] = one_ref[d, rows * parts : rows * (parts + 1), :]
     vec = vec_ref[...]
     tile = 256
-    tiles = rows_all // tile
-    for copy in ins[:2]:
+    tiles = [slice(t, t + tile) for t in range(0, rows_all, tile)]
+    for copy in copies[0]:
         copy.wait()
-
-    @pl.loop(0, tiles)
-    def _(t):
-        at = pl.ds(pl.multiple_of(t * tile, tile), tile)
+    for copy in copies[1]:
+        copy.start()
+    for d in range(devices):
+        wout_ref[rows * d : rows * (d + 1), :] = wo_ref[d, 0:rows, :]
+    spreads = []
+    for at in tiles:
         r = x_ref[at, :].astype(wide) + (dot(mixed_ref[at, :], wout_ref[...]) + vec[0:1])
         centred = r - row_mean(r)
         spread = lax.rsqrt(row_mean(centred * centred) + norm_eps)
+        spreads.append(spread)
         unit = centred * spread
         unit_ref[at, :] = unit
-        spread_ref[at, :] = spread
         normed_ref[at, :] = (unit * vec[1:2] + vec[2:3]).astype(half)
-
+    for copy in copies[1]:
+        copy.wait()
+    for copy in copies[2]:
+        copy.start()
+    for d in range(devices):
+        for j in range(parts):
+            win_ref[j, rows * d : rows * (d + 1), :] = one_ref[d, rows * j : rows * (j + 1), :]
     piece = 256
-
-    @pl.loop(0, parts)
-    def _(j):
+    for j in range(parts):
         for n in range(width // piece):
             cols = slice(n * piece, (n + 1) * piece)
             pre = dot(normed_ref[...], win_ref[j, :, cols]) + bin_ref[j, :, cols].astype(wide)
-            phi = 0.5 * (1.0 + lax.erf(pre * root_half))
+            phi = 0.5 + 0.5 * lax.erf(pre * root_half)
             act_ref[j, :, cols] = (pre * phi).astype(half)
-            slope_ref[j, :, cols] = (phi + pre * jnp.exp(-0.5 * pre * pre) * slope_const).astype(half)
-
-    for copy in copies[devices:]:
+            slope_ref[j, :, cols] = (phi + (pre * slope_const) * jnp.exp2(pre * pre * half_log2e)).astype(half)
+
+    for copy in copies[2]:
         copy.wait()
 
     def second(j):
@@ -611,13 +604,9 @@
     def _(j):
         sum_ref[...] += dot(act_ref[j], second(j))
 
-    for copy in ins[2:]:
-        copy.wait()
-    d_branch_ref = normed_ref
-
-    @pl.loop(0, tiles)
-    def _(t):
-        at = pl.ds(pl.multiple_of(t * tile, tile), tile)
+    d_branch_ref, g_ref = normed_ref, d_pre_ref
+    first = second(0)
+    for at in tiles:
         r = unit_ref[at, :] * vec[1:2] + vec[2:3] + (sum_ref[at, :] + vec[3:4])
         centred = r - row_mean(r)
         spread = lax.rsqrt(row_mean(centred * centred) + norm_eps)
@@ -626,106 +615,90 @@
         e = grad_ref[at, :].astype(wide) * vec[4:5]
         d_two = spread * (e - row_mean(e) - unit * row_mean(e * unit))
         sum_ref[at, :] = d_two
-        d_branch_ref[at, :] = d_two.astype(half)
+        d_branch = d_two.astype(half)
+        d_branch_ref[at, :] = d_branch
+        d_pre_ref[at, :] = (dot(d_branch, first, NT) * slope_ref[0, at, :].astype(wide)).astype(half)
 
     outs = [pltpu.make_async_copy(out_ref, out_out, out_sems.at[0])]
     outs[0].start()
-
-    @pl.loop(0, parts)
+    sum_ref[...] += dot(d_pre_ref[...], win_ref[0], NT)
+
+    @pl.loop(1, parts)
     def _(j):
         d_act = dot(d_branch_ref[...], second(j), NT)
         d_pre = (d_act * slope_ref[j].astype(wide)).astype(half)
         sum_ref[...] += dot(d_pre, win_ref[j], NT)
 
-    g_ref = mixed_ref
-
-    @pl.loop(0, tiles)
-    def _(t):
-        at = pl.ds(pl.multiple_of(t * tile, tile), tile)
+    for i, at in enumerate(tiles):
         unit_one = unit_ref[at, :]
         e = sum_ref[at, :] * vec[1:2]
-        d_one = spread_ref[at, :] * (e - row_mean(e) - unit_one * row_mean(e * unit_one))
+        d_one = spreads[i] * (e - row_mean(e) - unit_one * row_mean(e * unit_one))
         sum_ref[at, :] = d_one
         d_mixed = dot(d_one.astype(half), wout_ref[...], NT)
         g_ref[at, :] = (d_mixed * inv_ref[at, :]).astype(half)
-
-    outs += [
-        pltpu.make_async_copy(sum_ref, d_one_out, out_sems.at[1]),
-        pltpu.make_async_copy(g_ref, g_out, out_sems.at[2]),
-    ]
-    for copy in outs[1:]:
-        copy.start()
+        outs.append(pltpu.make_async_copy(sum_ref.at[at], d_one_out.at[at], out_sems.at[1 + 2 * i]))
+        outs.append(pltpu.make_async_copy(g_ref.at[at], g_out.at[at], out_sems.at[2 + 2 * i]))
+        for copy in outs[-2:]:
+            copy.start()
     for copy in outs:
         copy.wait()
 
 
-def feed(mixed, x, grad, inv, arrays, specs, table, vec, bias, fc_rows, one_rows):
+def feed(mixed, x, grad, inv, arrays, specs, counts, table, vec, bias):
     rows, width = x.shape
     devices = table.shape[0]
     parts = bias.shape[0]
     vmem = pltpu.VMEM
     return pl.pallas_call(
         functools.partial(feed_kernel, specs),
-        in_specs=[SCALARS, pl.BlockSpec(memory_space=vmem), pl.BlockSpec(memory_space=vmem)]
-        + [PLACED] * (4 + len(arrays)),
+        in_specs=[SCALARS] + [NEAR] * 6 + [PLACED] * len(arrays),
         out_specs=[PLACED] * 3,
         out_shape=[shape((rows, width), half), shape((rows, width), wide), shape((rows, width), half)],
-        scratch_shapes=[
-            vmem((devices, fc_rows, width), half),
-            vmem((devices, one_rows, width), half),
+        scratch_shapes=[vmem((devices, count, width), half) for count in counts]
+        + [
             vmem((parts, width, width), half),
             vmem((width, width), half),
             vmem((rows, width), half),
-            vmem((rows, width), half),
-            vmem((rows, width), half),
             vmem((rows, width), wide),
-            vmem((rows, width), half),
-            vmem((rows, width), wide),
-            vmem((rows, 1), wide),
             vmem((parts, rows, width), half),
             vmem((parts, rows, width), half),
             vmem((rows, width), wide),
             vmem((rows, width), half),
-            pltpu.SemaphoreType.DMA((2 * devices,)),
-            pltpu.SemaphoreType.DMA((4,)),
-            pltpu.SemaphoreType.DMA((3,)),
-        ],
-        compiler_params=params(60),
+            vmem((rows, width), half),
+            pltpu.SemaphoreType.DMA((3, devices)),
+            pltpu.SemaphoreType.DMA((1 + 2 * (rows // 256),)),
+        ],
+        compiler_params=params(LIMITS[2]),
         cost_estimate=cost(40),
     )(table, vec, bias, mixed, x, grad, inv, *arrays)
 
 
-def project_back_kernel(d_ref, w_ref, d_one_ref, d_red_ref, ad_ref, grad_ref):
-    j = pl.program_id(0)
-    part = dot(d_ref[0], w_ref[0], NT)
-
-    @pl.when(j == 0)
-    def _():
-        grad_ref[...] = d_one_ref[...] + dot(d_red_ref[...], ad_ref[0:16, :]) + part
-
-    @pl.when(j > 0)
-    def _():
-        grad_ref[...] += part
+def project_back_kernel(d_ref, w_ref, one_ref, d_red_ref, ad_ref, grad_ref):
+    grad = one_ref[...] + dot(d_red_ref[...], ad_ref[0:16, :])
+    for j in range(3):
+        grad += dot(d_ref[j], w_ref[j], NT)
+    grad_ref[...] = grad
 
 
 def project_back(d_qkv, d_one, d_red, wqkv, ad):
     rows, width = d_one.shape
-    single = pl.BlockSpec((rows, width), lambda i: (0, 0), pipeline_mode=pl.Buffered(1))
+    tile = 512
+    block = pl.BlockSpec((tile, width), lambda i: (i, 0))
     return pl.pallas_call(
         project_back_kernel,
-        grid=(3,),
+        grid=(rows // tile,),
         in_specs=[
-            pl.BlockSpec((1, rows, width), lambda i: (i, 0, 0)),
-            pl.BlockSpec((1, width, width), lambda i: (i, 0, 0)),
-            single,
-            constant(d_red.shape),
+            pl.BlockSpec((3, tile, width), lambda i: (0, i, 0)),
+            pl.BlockSpec(wqkv.shape, lambda i: (0, 0, 0), pipeline_mode=pl.Buffered(1)),
+            block,
+            pl.BlockSpec((tile, 16), lambda i: (i, 0)),
             constant(ad.shape),
         ],
-        out_specs=constant((rows, width)),
+        out_specs=block,
         out_shape=shape((rows, width), wide),
-        compiler_params=params(),
+        compiler_params=params(LIMITS[4]),
         cost_estimate=cost(8),
-    )(d_qkv, wqkv, d_one, d_red, ad)
+    )(*[pltpu.with_memory_space_constraint(t, pltpu.HBM) for t in (d_qkv, wqkv, d_one)], d_red, ad)
 
 
 def body(
@@ -743,10 +716,8 @@
     span = adapter_weight.shape[0] // rank
     shards = width // span
 
-    line_a = jnp.concatenate([b_qv, b_out, ln1_gain])
-    line_b = jnp.concatenate([ln1_bias, b_fc, ln2_gain, ln2_bias])
-    lines = jnp.stack([b_in, line_a, line_b])
-    pack_a, pack_b, pack_1 = pack(w_qkv, w_out, w_in, w_fc, adapter_weight.reshape(1, -1), lines)
+    vectors = b_in, b_qv, b_out, ln1_gain, ln1_bias, b_fc, ln2_gain, ln2_bias
+    pack_a, pack_b, pack_1 = pack(w_qkv, w_out, w_in, w_fc, adapter_weight, vectors)
 
     seq_ends = jnp.cumsum(seq_lengths, axis=1)
     positions = jnp.arange(length, dtype=jnp.int32)
@@ -759,12 +730,14 @@
     key_feat = jnp.where(same | ((lane == slots) & padded), masked, 0.0).astype(half)
 
     staged = devices == 32
+    split = w_fc.shape[0]
     if staged:
         list_a, state = gather_attention(pack_a, pack_b)
         ring = Ring(state)
     else:
-        list_a, list_1, list_2 = [[everyone(p, devices)] for p in (pack_a, pack_1, w_fc)]
-    qkv, reduced, factors, vec, bias_in, wqkv = project(hidden_in, list_a, places(list_a), ffn_parts, shards)
+        lists = [[everyone(p, devices)] for p in (pack_a, pack_1[split:], pack_1[:split], w_fc)]
+        list_a = lists[0]
+    qkv, qkv_far, reduced, factors, vec, bias_in, wqkv = project(hidden_in, list_a, places(list_a), ffn_parts, shards)
     before = ()
     if staged:
         ring.step(reduced)
@@ -778,14 +751,15 @@
         ring.swap(mixed, 4)
         held = ring.held
         arrays = [h.array for h in held]
-        specs = [[(i, w_fc.shape[0]) for i in range(len(held))], [(i, 0) for i in range(len(held))]]
+        specs = [[(i, start) for i in range(len(held))] for start in (2 * split, split, 0)]
     else:
-        held, arrays = list_1, [list_1[0].array, list_2[0].array]
-        specs = [[(0, 0)], [(1, 0)]]
+        held, arrays = lists[1], [h[0].array for h in lists[1:]]
+        specs = [[(0, 0)], [(1, 0)], [(2, 0)]]
+    counts = pack_1.shape[0] - split, split, split
     hidden_out, d_one, g = feed(
-        mixed, hidden_in, grad_out, inv, arrays, specs, places(held), vec, bias_in, w_fc.shape[0], pack_1.shape[0]
+        mixed, hidden_in, grad_out, inv, arrays, specs, counts, places(held), vec, bias_in
     )
-    d_qkv, d_reduced, partial_grad = attend_back(qkv, g, mixed, probs, hidden_in, reduced, factors, devices)
+    d_qkv, d_reduced, partial_grad = attend_back(qkv_far, g, mixed, probs, hidden_in, reduced, factors, devices)
     grad_in = project_back(d_qkv, d_one, d_reduced, wqkv, factors)
     owned = lax.all_to_all(partial_grad, AXES, 0, 0, tiled=True)
     owned_grad = jnp.sum(owned, axis=0).T.reshape(-1)

time: 185 us -> 172 us (0.930)
  Pallas kernels: 108 us -> 91 us
  waiting for transfers between devices: 30.3 us -> 35.3 us
  local copies, waits for them, and re-layouts: 7.08 us -> 9.09 us
    pallas_call x4, Pallas kernels: 66.8 us -> 58.7 us  [the longest x1 37.5 us: feed(): pl.pallas_call(functools.partial(feed_kernel, specs), in_specs=[SCALARS]...]
    pallas_call x1, Pallas kernels: 25.1 us -> 18.9 us  [attend_back(): pl.pallas_call(attend_back_kernel, grid=(windows, pairs // STEP), in_spec...]
    ppermute x34, waiting for transfers between devices: 30.3 us -> 35.3 us  [send(): return Held(lax.ppermute(self.array, AXES, pairs), owner)]
    unnamed x57 -> x47, local copies, waits for them, and re-layouts: 3.09 us -> 5.9 us
    pallas_call x2, Pallas kernels: 15.9 us -> 13.5 us  [attend(): pl.pallas_call(attend_kernel, grid=(pairs // STEP,), in_specs=heads + [fe...]
    another operation x2 -> x0, other arithmetic: 2.06 us -> none  [body(): lines = jnp.stack([b_in, line_a, line_b])]
  transfers between devices with their start and end apart: 35 -> 35, of which waited for: 12 -> 12; matrix products, arithmetic and copies ran while one was open for 3% -> 5% of each run, Pallas kernels for 21% -> 19%
where the time goes in v3:
time: 172 us; the launch traced here: 171 us
  Pallas kernels  91 us (53%)
  waiting for transfers between devices  35.3 us (21%)
  starting transfers between devices  31.6 us (18%)
  local copies, waits for them, and re-layouts  9.09 us (5%)
  other arithmetic  3.41 us (2%)
    pallas_call x1, Pallas kernels, feed(): pl.pallas_call(functools.partial(feed_kernel, specs), in_specs=[SCALARS]...  37.5 us
    ppermute x34, waiting for transfers between devices, send(): return Held(lax.ppermute(self.array, AXES, pairs), owner)  35.3 us
    ppermute x34, starting transfers between devices, send(): return Held(lax.ppermute(self.array, AXES, pairs), owner)  27.4 us
    pallas_call x1, Pallas kernels, attend_back(): pl.pallas_call(attend_back_kernel, grid=(windows, pairs // STEP), in_spec...  18.9 us
    pallas_call x2, Pallas kernels, attend(): pl.pallas_call(attend_kernel, grid=(pairs // STEP,), in_specs=heads + [fe...  13.5 us
    pallas_call x1, Pallas kernels, project(): pl.pallas_call(functools.partial(project_kernel, len(held), shards), grid...  10.4 us
    pallas_call x1, Pallas kernels, project_back(): pl.pallas_call(project_back_kernel, grid=(rows // tile,), in_specs=[pl.Bl...  8.74 us
    unnamed x47, local copies, waits for them, and re-layouts  5.9 us
  transfers between devices with their start and end apart: 35, of which 12 were waited for; matrix products, arithmetic and copies ran while one was open for 5% of the time, Pallas kernels for 19%

profile of v3, /device:TPU:0, one launch (start us, length us, event | category | flops | bytes accessed | tf_op | source)
XLA Modules:
  0.0 171.5 jit_solution(5519387110261705535)
XLA Ops:
  0.7 2.0 %shard_map.236 = (bf16[80,768]{1,0:T(8,128)(2,1)}, bf16[224,768]{1,0:T(8,128)(2,1)}, bf16[128,768]{1,0:T(8,128)(2,1)}) custom-call(bf16[24,2304]{1,0:T(8,128)(2,1)} %wqkv_ref.1, bf16[24,768]{1,0:T(8,128)(2,1)} %wout_ref.1, bf16[24,3072]{1,0:T(8,128)(2,1)} %win_ref.1, bf16[96,768]{1,0:T(8,128)(2,1)} %wfc_ref.1, f32[768]{0:T(1024)} %factor_ref.1, ...), custom_call_target="tpu_custom_call" | custom-call | flops 1600000000 | bytes 5000000 | tf_op jit(solution)/shard_map/pallas_call | solution.py:253
  2.7 3.0 %collective-permute-start.2 = (bf16[1,80,768]{2,1,0:T(8,128)(2,1)}, bf16[1,80,768]{2,1,0:T(8,128)(2,1)S(1)}, u32[]{:S(2)}, u32[]{:S(2)}) collective-permute-start(bf16[1,80,768]{2,1,0:T(8,128)(2,1)} %bitcast.10), channel_id=1, source_target_pairs={{0,8},{1,9},{2,10},{3,11},{4,12},{5,13},{6,14},{7,15},{8,16},{9,17... | collective-permute-start | bytes 368648 | tf_op jit(solution)/shard_map/ppermute | solution.py:77
  5.7 2.1 %collective-permute-start.3 = (bf16[1,80,768]{2,1,0:T(8,128)(2,1)}, bf16[1,80,768]{2,1,0:T(8,128)(2,1)S(1)}, u32[]{:S(2)}, u32[]{:S(2)}) collective-permute-start(bf16[1,80,768]{2,1,0:T(8,128)(2,1)} %bitcast.11), channel_id=1, source_target_pairs={{0,24},{1,25},{2,26},{3,27},{4,28},{5,29},{6,30},{7,31},{8,0},{9,1... | collective-permute-start | bytes 368648 | tf_op jit(solution)/shard_map/ppermute | solution.py:77
  8.8 1.5 collective-permute-start
  13.4 1.6 collective-permute-start.4
  15.2 5.2 %collective-permute-done.4 = bf16[2,80,768]{2,1,0:T(8,128)(2,1)S(1)} collective-permute-done((bf16[2,80,768]{2,1,0:T(8,128)(2,1)S(1)}, bf16[2,80,768]{2,1,0:T(8,128)(2,1)S(1)}, u32[]{:S(2)}, u32[]{:S(2)}) %collective-permute-start.4) | collective-permute-done | bytes 245792 | tf_op jit(solution)/shard_map/ppermute | solution.py:77
  20.4 1.6 collective-permute-start.7
  22.1 1.4 collective-permute-start.6
  25.9 2.7 %collective-permute-done.6 = bf16[1,80,768]{2,1,0:T(8,128)(2,1)S(1)} collective-permute-done((bf16[1,80,768]{2,1,0:T(8,128)(2,1)}, bf16[1,80,768]{2,1,0:T(8,128)(2,1)S(1)}, u32[]{:S(2)}, u32[]{:S(2)}) %collective-permute-start.6) | collective-permute-done | bytes 122912 | tf_op jit(solution)/shard_map/ppermute | solution.py:77
  28.6 3.5 %collective-permute-start.19 = (bf16[1,224,768]{2,1,0:T(8,128)(2,1)}, bf16[1,224,768]{2,1,0:T(8,128)(2,1)}, u32[]{:S(2)}, u32[]{:S(2)}) collective-permute-start(bf16[1,224,768]{2,1,0:T(8,128)(2,1)} %bitcast.8), channel_id=1, source_target_pairs={{0,8},{1,25},{2,10},{3,27},{4,12},{5,29},{6,14},{7,31},{8,16},{9,1... | collective-permute-start | bytes 1032200 | tf_op jit(solution)/shard_map/ppermute | solution.py:77
  34.5 6.3 %collective-permute-done.19 = bf16[1,224,768]{2,1,0:T(8,128)(2,1)} collective-permute-done((bf16[1,224,768]{2,1,0:T(8,128)(2,1)}, bf16[1,224,768]{2,1,0:T(8,128)(2,1)}, u32[]{:S(2)}, u32[]{:S(2)}) %collective-permute-start.19) | collective-permute-done | bytes 344096 | tf_op jit(solution)/shard_map/ppermute | solution.py:77
  44.7 1.5 collective-permute-start.16
  46.3 10.4 %shard_map.237 = (bf16[3,1024,768]{2,1,0:T(8,128)(2,1)S(1)}, bf16[3,1024,768]{2,1,0:T(8,128)(2,1)}, bf16[1024,16]{1,0:T(8,128)(2,1)}, bf16[32,768]{1,0:T(8,128)(...) custom-call(s32[32]{0:T(128)S(1)} %dynamic-slice_bitcast_fusion.table_ref, ...), custom_call_target="tpu_custom_call" | custom-call | flops 6400000000 | bytes 20000000 | tf_op jit(solution)/shard_map/pallas_call | solution.py:332
  58.4 6.7 %shard_map.238 = (bf16[1024,768]{1,0:T(8,128)(2,1)}, f32[1024,768]{1,0:T(8,128)}, bf16[2,6,1024,512]{3,2,1,0:T(8,128)(2,1)}) custom-call(bf16[3,1024,768]{2,1,0:T(8,128)(2,1)S(1)} %get-tuple-element.49.q_ref.k_ref.v_ref, bf16[3,1024,768]{2,1,0:T(8,128)(2,1)S(1)} %get-tuple-element.49.q_ref.k_ref.v_ref, ...), custom_call_target="tpu_custom_call" | custom-call | flops 4800000000 | bytes 15000000 | tf_op jit(solution)/shard_map/pallas_call | solution.py:415
  67.2 1.5 collective-permute-start.30
  69.3 6.8 %shard_map.239 = (bf16[1024,768]{1,0:T(8,128)(2,1)}, f32[1024,768]{1,0:T(8,128)}, bf16[2,6,1024,512]{3,2,1,0:T(8,128)(2,1)}) custom-call(bf16[3,1024,768]{2,1,0:T(8,128)(2,1)S(1)} %get-tuple-element.49.q_ref.k_ref.v_ref, bf16[3,1024,768]{2,1,0:T(8,128)(2,1)S(1)} %get-tuple-element.49.q_ref.k_ref.v_ref, ...), custom_call_target="tpu_custom_call", output_to_operand_aliasing={{0}: (5, {}), {1}: (6, {}), {2}: (7, {})} | custom-call | flops 4800000000 | bytes 15000000 | tf_op jit(solution)/shard_map/pallas_call | solution.py:415
  76.1 2.1 %collective-permute-done.30 = bf16[1,224,768]{2,1,0:T(8,128)(2,1)S(1)} collective-permute-done((bf16[1,224,768]{2,1,0:T(8,128)(2,1)S(1)}, bf16[1,224,768]{2,1,0:T(8,128)(2,1)S(1)}, u32[]{:S(2)}, u32[]{:S(2)}) %collective-permute-start.30) | collective-permute-done | bytes 344096 | tf_op jit(solution)/shard_map/ppermute | solution.py:77
  78.3 1.4 collective-permute-start.31
  80.3 7.3 %collective-permute-done.26.refs_9_ = bf16[2,224,768]{2,1,0:T(8,128)(2,1)S(1)} collective-permute-done((bf16[2,224,768]{2,1,0:T(8,128)(2,1)S(1)}, bf16[2,224,768]{2,1,0:T(8,128)(2,1)S(1)}, u32[]{:S(2)}, u32[]{:S(2)}) %collective-permute-start.26) | collective-permute-done | bytes 688160 | tf_op jit(solution)/shard_map/ppermute | solution.py:77
  87.6 7.4 %collective-permute-done.31.refs_13_ = bf16[2,224,768]{2,1,0:T(8,128)(2,1)S(1)} collective-permute-done((bf16[2,224,768]{2,1,0:T(8,128)(2,1)S(1)}, bf16[2,224,768]{2,1,0:T(8,128)(2,1)S(1)}, u32[]{:S(2)}, u32[]{:S(2)}) %collective-permute-start.31) | collective-permute-done | bytes 688160 | tf_op jit(solution)/shard_map/ppermute | solution.py:77
  100.3 37.5 %shard_map.240 = (bf16[1024,768]{1,0:T(8,128)(2,1)}, f32[1024,768]{1,0:T(8,128)}, bf16[1024,768]{1,0:T(8,128)(2,1)}) custom-call(s32[32]{0:T(128)} %dynamic-slice_bitcast_fusion.1.table_ref, f32[8,768]{1,0:T(8,128)} %get-tuple-element.47.vec_ref, bf16[4,1,768]{2,1,0:T(2,128)(2,1)} %get-tuple-element.48.bin_ref, ...), custom_call_target="tpu_custom_call" | custom-call | flops 32000000000 | bytes 100000000 | tf_op jit(solution)/shard_map/pallas_call | solution.py:652
  137.8 18.9 %shard_map.241 = (bf16[3,1024,768]{2,1,0:T(8,128)(2,1)}, bf16[1024,16]{1,0:T(8,128)(2,1)}, f32[32,8,96]{2,1,0:T(8,128)}) custom-call(bf16[3,1024,768]{2,1,0:T(8,128)(2,1)} %get-tuple-element.78.q_ref.k_ref.v_ref, bf16[3,1024,768]{2,1,0:T(8,128)(2,1)} %get-tuple-element.78.q_ref.k_ref.v_ref, bf16[3,1024,768]{2,1,0:T(8,128)(2,1)} %get-tuple-element.78.q_ref.k_ref.v_ref, ...), custom_call_target="tpu_custom_call" | custom-call | flops 16000000000 | bytes 50000000 | tf_op jit(solution)/shard_map/pallas_call | solution.py:511
  156.7 4.2 %all-to-all-start = ((f32[32,8,96]{2,1,0:T(8,128)}), f32[32,8,96]{2,1,0:T(8,128)S(1)}, u32[]{:S(2)}, u32[]{:S(2)}) async-start(f32[32,8,96]{2,1,0:T(8,128)} %get-tuple-element.86), calls=%async_computation | async-start | bytes 262144 | tf_op jit(solution)/shard_map/all_to_all | solution.py:764
  161.8 8.7 %shard_map.242 = f32[1024,768]{1,0:T(8,128)} custom-call(bf16[3,1024,768]{2,1,0:T(8,128)(2,1)} %get-tuple-element.82.d_ref, bf16[3,768,768]{2,1,0:T(8,128)(2,1)} %get-tuple-element.83.w_ref, f32[1024,768]{1,0:T(8,128)} %get-tuple-element.84.one_ref, bf16[1024,16]{1,0:T(8,128)(2,1)S(1)} %copy-done.1, bf16[32,768]{1,0:T(8,128)(2,1)S(1)} %copy-done.3), custom_call_target="tpu_custom_call" | custom-call | flops 6400000000 | bytes 20000000 | tf_op jit(solution)/shard_map/pallas_call | solution.py:687
  (120 shorter events, 25.2 us)
Async XLA Ops:
  2.7 9.4 %collective-permute-start.2 = (bf16[1,80,768]{2,1,0:T(8,128)(2,1)}, bf16[1,80,768]{2,1,0:T(8,128)(2,1)S(1)}, u32[]{:S(2)}, u32[]{:S(2)}) collective-permute-start(bf16[1,80,768]{2,1,0:T(8,128)(2,1)} %bitcast.10), channel_id=1, source_target_pairs={{0,8},{1,9},{2,10},{3,11},{4,12},{5,13},{6,14},{7,15},{8,16},{9,17... | collective-permute-start | bytes 368648 | tf_op jit(solution)/shard_map/ppermute | solution.py:77
  7.8 14.2 %collective-permute-start.5 = (bf16[1,80,768]{2,1,0:T(8,128)(2,1)}, bf16[1,80,768]{2,1,0:T(8,128)(2,1)}, u32[]{:S(2)}, u32[]{:S(2)}) collective-permute-start(bf16[1,80,768]{2,1,0:T(8,128)(2,1)} %bitcast.12), channel_id=1, source_target_pairs={{0,16},{1,17},{2,18},{3,19},{4,20},{5,21},{6,22},{7,23},{8,24},{9,... | collective-permute-start | bytes 368648 | tf_op jit(solution)/shard_map/ppermute | solution.py:77
  8.8 14.7 %collective-permute-start = (bf16[1,80,768]{2,1,0:T(8,128)(2,1)}, bf16[1,80,768]{2,1,0:T(8,128)(2,1)S(1)}, u32[]{:S(2)}, u32[]{:S(2)}) collective-permute-start(bf16[1,80,768]{2,1,0:T(8,128)(2,1)} %bitcast.13), channel_id=1, source_target_pairs={{0,2},{1,5},{2,0},{3,7},{4,6},{5,1},{6,4},{7,3},{8,10},{9,13},{10,... | collective-permute-start | bytes 368648 | tf_op jit(solution)/shard_map/ppermute | solution.py:77
  10.3 21.9 %collective-permute-start.15 = (bf16[1,224,768]{2,1,0:T(8,128)(2,1)}, bf16[1,224,768]{2,1,0:T(8,128)(2,1)}, u32[]{:S(2)}, u32[]{:S(2)}) collective-permute-start(bf16[1,224,768]{2,1,0:T(8,128)(2,1)} %bitcast.7), channel_id=1, source_target_pairs={{0,2},{1,5},{2,0},{3,7},{4,6},{5,1},{6,4},{7,3},{8,10},{9,13},{10,... | collective-permute-start | bytes 1032200 | tf_op jit(solution)/shard_map/ppermute | solution.py:77
  20.4 12.5 %collective-permute-start.7 = (bf16[4,80,768]{2,1,0:T(8,128)(2,1)S(1)}, bf16[4,80,768]{2,1,0:T(8,128)(2,1)S(1)}, u32[]{:S(2)}, u32[]{:S(2)}) collective-permute-start(bf16[4,80,768]{2,1,0:T(8,128)(2,1)S(1)} %constant_dynamic-update-slice_fusion.refs_2_), channel_id=1, source_target_pairs={{0,4},{1,3},{2,6},{3,1},{4,0},{5,7},{6,2},{7,5},{8,12},{9,11},{10,... | collective-permute-start | bytes 1474568 | tf_op jit(solution)/shard_map/ppermute | solution.py:77
  24.9 9.4 %collective-permute-start.9 = (bf16[2,80,768]{2,1,0:T(8,128)(2,1)S(1)}, bf16[2,80,768]{2,1,0:T(8,128)(2,1)S(1)}, u32[]{:S(2)}, u32[]{:S(2)}) collective-permute-start(bf16[2,80,768]{2,1,0:T(8,128)(2,1)S(1)} %pad_maximum_fusion.refs_0_), channel_id=1, source_target_pairs={{0,1},{1,0},{2,3},{3,2},{4,5},{5,4},{6,7},{7,6},{8,9},{9,8},{10,11... | collective-permute-start | bytes 737288 | tf_op jit(solution)/shard_map/ppermute | solution.py:77
  28.6 12.2 %collective-permute-start.19 = (bf16[1,224,768]{2,1,0:T(8,128)(2,1)}, bf16[1,224,768]{2,1,0:T(8,128)(2,1)}, u32[]{:S(2)}, u32[]{:S(2)}) collective-permute-start(bf16[1,224,768]{2,1,0:T(8,128)(2,1)} %bitcast.8), channel_id=1, source_target_pairs={{0,8},{1,25},{2,10},{3,27},{4,12},{5,29},{6,14},{7,31},{8,16},{9,1... | collective-permute-start | bytes 1032200 | tf_op jit(solution)/shard_map/ppermute | solution.py:77
  32.8 13.5 %collective-permute-start.11 = (bf16[4,80,768]{2,1,0:T(8,128)(2,1)S(1)}, bf16[4,80,768]{2,1,0:T(8,128)(2,1)S(1)}, u32[]{:S(2)}, u32[]{:S(2)}) collective-permute-start(bf16[4,80,768]{2,1,0:T(8,128)(2,1)S(1)} %constant_dynamic-update-slice_fusion.refs_2_), channel_id=1, source_target_pairs={{0,1},{1,0},{2,3},{3,2},{4,5},{5,4},{6,7},{7,6},{8,9},{9,8},{10,11... | collective-permute-start | bytes 1474568 | tf_op jit(solution)/shard_map/ppermute | solution.py:77
  32.8 13.4 %collective-permute-start.13 = (bf16[4,80,768]{2,1,0:T(8,128)(2,1)S(1)}, bf16[4,80,768]{2,1,0:T(8,128)(2,1)S(1)}, u32[]{:S(2)}, u32[]{:S(2)}) collective-permute-start(bf16[4,80,768]{2,1,0:T(8,128)(2,1)S(1)} %collective-permute-done.7.refs_4_), channel_id=1, source_target_pairs={{0,1},{1,0},{2,3},{3,2},{4,5},{5,4},{6,7},{7,6},{8,9},{9,8},{10,11... | collective-permute-start | bytes 1474568 | tf_op jit(solution)/shard_map/ppermute | solution.py:77
  34.3 9.7 %collective-permute-start.12 = (bf16[2,80,768]{2,1,0:T(8,128)(2,1)S(1)}, bf16[2,80,768]{2,1,0:T(8,128)(2,1)S(1)}, u32[]{:S(2)}, u32[]{:S(2)}) collective-permute-start(bf16[2,80,768]{2,1,0:T(8,128)(2,1)S(1)} %constant_dynamic-update-slice_fusion.3.refs_3_), channel_id=1, source_target_pairs={{0,1},{1,0},{2,3},{3,2},{4,5},{5,4},{6,7},{7,6},{8,9},{9,8},{10,11... | collective-permute-start | bytes 737288 | tf_op jit(solution)/shard_map/ppermute | solution.py:77
  44.1 12.6 %collective-permute-start.24 = (bf16[1,224,768]{2,1,0:T(8,128)(2,1)}, bf16[1,224,768]{2,1,0:T(8,128)(2,1)S(1)}, u32[]{:S(2)}, u32[]{:S(2)}) collective-permute-start(bf16[1,224,768]{2,1,0:T(8,128)(2,1)} %collective-permute-done.19), channel_id=1, source_target_pairs={{0,8},{1,25},{2,10},{3,27},{4,12},{5,29},{6,14},{7,31},{8,16},{9,1... | collective-permute-start | bytes 1032200 | tf_op jit(solution)/shard_map/ppermute | solution.py:77
  44.1 21.0 %collective-permute-start.20 = (bf16[1,224,768]{2,1,0:T(8,128)(2,1)}, bf16[1,224,768]{2,1,0:T(8,128)(2,1)S(1)}, u32[]{:S(2)}, u32[]{:S(2)}) collective-permute-start(bf16[1,224,768]{2,1,0:T(8,128)(2,1)} %collective-permute-done.19), channel_id=1, source_target_pairs={{0,2},{1,5},{2,0},{3,7},{4,6},{5,1},{6,4},{7,3},{8,10},{9,13},{10,... | collective-permute-start | bytes 1032200 | tf_op jit(solution)/shard_map/ppermute | solution.py:77
  44.7 20.4 %collective-permute-start.16 = (bf16[2,224,768]{2,1,0:T(8,128)(2,1)S(1)}, bf16[2,224,768]{2,1,0:T(8,128)(2,1)S(1)}, u32[]{:S(2)}, u32[]{:S(2)}) collective-permute-start(bf16[2,224,768]{2,1,0:T(8,128)(2,1)S(1)} %constant_dynamic-update-slice_fusion.5.refs_0_), channel_id=1, source_target_pairs={{0,4},{1,3},{2,6},{3,1},{4,0},{5,7},{6,2},{7,5},{8,12},{9,11},{10,... | collective-permute-start | bytes 2064392 | tf_op jit(solution)/shard_map/ppermute | solution.py:77
  56.7 10.5 %collective-permute-start.25 = (bf16[1,224,768]{2,1,0:T(8,128)(2,1)S(1)}, bf16[1,224,768]{2,1,0:T(8,128)(2,1)S(1)}, u32[]{:S(2)}, u32[]{:S(2)}) collective-permute-start(bf16[1,224,768]{2,1,0:T(8,128)(2,1)S(1)} %collective-permute-done.24), channel_id=1, source_target_pairs={{0,2},{1,5},{2,0},{3,7},{4,6},{5,1},{6,4},{7,3},{8,10},{9,13},{10,... | collective-permute-start | bytes 1032200 | tf_op jit(solution)/shard_map/ppermute | solution.py:77
  57.9 9.4 %collective-permute-start.29 = (bf16[1,224,768]{2,1,0:T(8,128)(2,1)S(1)}, bf16[1,224,768]{2,1,0:T(8,128)(2,1)S(1)}, u32[]{:S(2)}, u32[]{:S(2)}) collective-permute-start(bf16[1,224,768]{2,1,0:T(8,128)(2,1)S(1)} %collective-permute-done.24), channel_id=1, source_target_pairs={{0,8},{1,25},{2,10},{3,27},{4,12},{5,29},{6,14},{7,31},{8,16},{9,1... | collective-permute-start | bytes 1032200 | tf_op jit(solution)/shard_map/ppermute | solution.py:77
  66.4 13.8 %collective-permute-start.21 = (bf16[2,224,768]{2,1,0:T(8,128)(2,1)S(1)}, bf16[2,224,768]{2,1,0:T(8,128)(2,1)S(1)}, u32[]{:S(2)}, u32[]{:S(2)}) collective-permute-start(bf16[2,224,768]{2,1,0:T(8,128)(2,1)S(1)} %constant_dynamic-update-slice_fusion.7.refs_4_), channel_id=1, source_target_pairs={{0,4},{1,3},{2,6},{3,1},{4,0},{5,7},{6,2},{7,5},{8,12},{9,11},{10,... | collective-permute-start | bytes 2064392 | tf_op jit(solution)/shard_map/ppermute | solution.py:77
  67.2 11.0 %collective-permute-start.30 = (bf16[1,224,768]{2,1,0:T(8,128)(2,1)S(1)}, bf16[1,224,768]{2,1,0:T(8,128)(2,1)S(1)}, u32[]{:S(2)}, u32[]{:S(2)}) collective-permute-start(bf16[1,224,768]{2,1,0:T(8,128)(2,1)S(1)} %collective-permute-done.29), channel_id=1, source_target_pairs={{0,2},{1,5},{2,0},{3,7},{4,6},{5,1},{6,4},{7,3},{8,10},{9,13},{10,... | collective-permute-start | bytes 1032200 | tf_op jit(solution)/shard_map/ppermute | solution.py:77
  68.7 18.9 %collective-permute-start.26 = (bf16[2,224,768]{2,1,0:T(8,128)(2,1)S(1)}, bf16[2,224,768]{2,1,0:T(8,128)(2,1)S(1)}, u32[]{:S(2)}, u32[]{:S(2)}) collective-permute-start(bf16[2,224,768]{2,1,0:T(8,128)(2,1)S(1)} %constant_dynamic-update-slice_fusion.9.refs_8_), channel_id=1, source_target_pairs={{0,4},{1,3},{2,6},{3,1},{4,0},{5,7},{6,2},{7,5},{8,12},{9,11},{10,... | collective-permute-start | bytes 2064392 | tf_op jit(solution)/shard_map/ppermute | solution.py:77
  78.3 16.7 %collective-permute-start.31 = (bf16[2,224,768]{2,1,0:T(8,128)(2,1)S(1)}, bf16[2,224,768]{2,1,0:T(8,128)(2,1)S(1)}, u32[]{:S(2)}, u32[]{:S(2)}) collective-permute-start(bf16[2,224,768]{2,1,0:T(8,128)(2,1)S(1)} %constant_dynamic-update-slice_fusion.11.refs_12_), channel_id=1, source_target_pairs={{0,4},{1,3},{2,6},{3,1},{4,0},{5,7},{6,2},{7,5},{8,12},{9,11},{10,... | collective-permute-start | bytes 2064392 | tf_op jit(solution)/shard_map/ppermute | solution.py:77
  79.7 15.3 %collective-permute-start.17 = (bf16[2,224,768]{2,1,0:T(8,128)(2,1)S(1)}, bf16[2,224,768]{2,1,0:T(8,128)(2,1)S(1)}, u32[]{:S(2)}, u32[]{:S(2)}) collective-permute-start(bf16[2,224,768]{2,1,0:T(8,128)(2,1)S(1)} %constant_dynamic-update-slice_fusion.5.refs_0_), channel_id=1, source_target_pairs={{0,1},{1,0},{2,3},{3,2},{4,5},{5,4},{6,7},{7,6},{8,9},{9,8},{10,11... | collective-permute-start | bytes 2064392 | tf_op jit(solution)/shard_map/ppermute | solution.py:77
  79.7 15.8 %collective-permute-start.18 = (bf16[2,224,768]{2,1,0:T(8,128)(2,1)S(1)}, bf16[2,224,768]{2,1,0:T(8,128)(2,1)S(1)}, u32[]{:S(2)}, u32[]{:S(2)}) collective-permute-start(bf16[2,224,768]{2,1,0:T(8,128)(2,1)S(1)} %collective-permute-done.16.refs_1_), channel_id=1, source_target_pairs={{0,1},{1,0},{2,3},{3,2},{4,5},{5,4},{6,7},{7,6},{8,9},{9,8},{10,11... | collective-permute-start | bytes 2064392 | tf_op jit(solution)/shard_map/ppermute | solution.py:77
  80.2 15.4 %collective-permute-start.22 = (bf16[2,224,768]{2,1,0:T(8,128)(2,1)S(1)}, bf16[2,224,768]{2,1,0:T(8,128)(2,1)S(1)}, u32[]{:S(2)}, u32[]{:S(2)}) collective-permute-start(bf16[2,224,768]{2,1,0:T(8,128)(2,1)S(1)} %constant_dynamic-update-slice_fusion.7.refs_4_), channel_id=1, source_target_pairs={{0,1},{1,0},{2,3},{3,2},{4,5},{5,4},{6,7},{7,6},{8,9},{9,8},{10,11... | collective-permute-start | bytes 2064392 | tf_op jit(solution)/shard_map/ppermute | solution.py:77
  87.6 11.1 %collective-permute-start.23 = (bf16[2,224,768]{2,1,0:T(8,128)(2,1)S(1)}, bf16[2,224,768]{2,1,0:T(8,128)(2,1)}, u32[]{:S(2)}, u32[]{:S(2)}) collective-permute-start(bf16[2,224,768]{2,1,0:T(8,128)(2,1)S(1)} %collective-permute-done.21.refs_5_), channel_id=1, source_target_pairs={{0,1},{1,0},{2,3},{3,2},{4,5},{5,4},{6,7},{7,6},{8,9},{9,8},{10,11... | collective-permute-start | bytes 2064392 | tf_op jit(solution)/shard_map/ppermute | solution.py:77
  156.7 13.9 %all-to-all-start = ((f32[32,8,96]{2,1,0:T(8,128)}), f32[32,8,96]{2,1,0:T(8,128)S(1)}, u32[]{:S(2)}, u32[]{:S(2)}) async-start(f32[32,8,96]{2,1,0:T(8,128)} %get-tuple-element.86), calls=%async_computation | async-start | bytes 262144 | tf_op jit(solution)/shard_map/all_to_all | solution.py:764
  (31 other events, 387.4 us)

commit v4 on v3

--- a/solution.py
+++ b/solution.py
@@ -179,14 +179,23 @@
             if len(self.ways) < 3:
                 self.turn()
             else:
-                self.waiting.append((self.now, self.now.send(first_way)))
+                self.last = [self.now, self.now.send(first_way), self.now.send(second_way)]
                 self.now = None
+
+    def end(self, token):
+        self.last.append(after(self.last[1], Held(token, None)).send(second_way))
+        self.hand_over(token, self.last[:3])
+        self.held += [self.last[3], self.last[3].send(other_core)]
+
+    def hand_over(self, token, some):
+        arrays = lax.optimization_barrier((token, *[h.array for h in some]))[1:]
+        for array, h in zip(arrays, some):
+            h = Held(array, h.owner)
+            self.held += [h, h.send(other_core)]
 
     def swap(self, token, count):
         for pair, second in list(zip(self.ways, self.seconds))[len(self.held) // 4 : count]:
-            gated = lax.optimization_barrier((token, pair.array, second.array))[1:]
-            pair, second = Held(gated[0], pair.owner), Held(gated[1], second.owner)
-            self.held += [pair, second, pair.send(other_core), second.send(other_core)]
+            self.hand_over(token, [pair, second])
 
 
 def everyone(array, devices):
@@ -197,14 +206,15 @@
 def places(held):
     table = np.concatenate([h.owner for h in held], axis=1)
     assert all(sorted(line) == list(range(len(table))) for line in table)
-    return lax.dynamic_index_in_dim(jnp.asarray(table, jnp.int32), lax.axis_index(AXES), 0, keepdims=False)
-
-
-def place_blocks(table_ref, block_refs, all_ref):
+    return jnp.asarray(table, jnp.int32)
+
+
+def place_blocks(me_ref, table_ref, block_refs, all_ref):
+    me = me_ref[0]
     i = 0
     for ref in block_refs:
         for b in range(ref.shape[0]):
-            all_ref[table_ref[i]] = ref[b]
+            all_ref[table_ref[me, i]] = ref[b]
             i += 1
 
 
@@ -263,19 +273,20 @@
 
 
 def unfold(pieces, piece, per):
-    devices, rows, lanes = pieces.shape
-    width = WIDTH
-    part = width // per
-    lane = lax.broadcasted_iota(jnp.int32, (lanes, width), 1)
-    row = lax.broadcasted_iota(jnp.int32, (lanes, width), 0)
+    devices, lanes = pieces.shape[0], pieces.shape[-1]
+    rows = pieces.shape[1:-1]
+    part = WIDTH // per
+    lane = lax.broadcasted_iota(jnp.int32, (lanes, WIDTH), 1)
+    row = lax.broadcasted_iota(jnp.int32, (lanes, WIDTH), 0)
     repeat = (lane % part + piece == row).astype(wide).astype(half)
-    spread = dot(pieces.reshape(devices * rows, lanes), repeat).reshape(devices // per, per, rows, width)
-    shard = lax.broadcasted_iota(jnp.int32, (per, rows, width), 0)
-    place = lax.broadcasted_iota(jnp.int32, (per, rows, width), 2) // part
+    spread = dot(pieces.reshape(-1, lanes), repeat).reshape(devices // per, per, *rows, WIDTH)
+    dims = (per, *rows, WIDTH)
+    shard = lax.broadcasted_iota(jnp.int32, dims, 0)
+    place = lax.broadcasted_iota(jnp.int32, dims, len(dims) - 1) // part
     return jnp.sum(jnp.where((shard == place)[None], spread, 0.0), axis=1)
 
 
-def project_kernel(blocks, shards, table_ref, x_ref, *refs):
+def project_kernel(blocks, shards, me_ref, table_ref, x_ref, *refs):
     block_refs = refs[:blocks]
     qkv_ref, far_ref, red_ref, ad_ref, vec_ref, bin_ref, wout_ref, ga_ref, w_ref, bias_ref, sem, sems = refs[blocks:]
     devices = ga_ref.shape[0]
@@ -285,23 +296,23 @@
 
     @pl.when(pl.program_id(0) == 0)
     def _():
-        place_blocks(table_ref, block_refs, ga_ref)
+        place_blocks(me_ref, table_ref, block_refs, ga_ref)
         for d in range(devices):
             span = slice(rows * d, rows * d + rows)
             for j in range(3):
                 w_ref[j, span, :] = ga_ref[d, rows * j : rows * (j + 1), :]
         keep.start()
         small = ga_ref[:, 3 * rows :, :PAIR]
-        lines = ga_ref[:, 3 * rows :, PAIR : 2 * PAIR]
+        lines = [ga_ref[:, 3 * rows + i, PAIR : 2 * PAIR] for i in range(3)]
         ad_ref[...] = unfold(small, 0, shards).reshape(4 * ADAPTER_RANK, width).astype(half)
-        bin_ref[...] = unfold(lines, 0, shards)[:, 0:1].astype(half)
-        bias = unfold(lines, 0, devices // 2)[:, 1:2]
-        bias_ref[0], bias_ref[1], bias_ref[2] = bias[0], jnp.zeros_like(bias[0]), bias[1]
-        vecs = [unfold(lines, rows * j, devices)[0] for j in range(4)]
-        vec_ref[...] = jnp.concatenate(
-            [vecs[2][1:2], vecs[3][1:2], vecs[0][2:3], vecs[1][2:3], vecs[2][2:3], vecs[3][2:3], vecs[0][0:2]],
-            axis=0,
-        )
+        line = unfold(lines[0], 0, shards).astype(half)
+        for j in range(bin_ref.shape[0]):
+            bin_ref[j] = line[j : j + 1]
+        bias = unfold(lines[1], 0, devices // 2)
+        bias_ref[0], bias_ref[1], bias_ref[2] = bias[0:1], jnp.zeros_like(bias[0:1]), bias[1:2]
+        vecs = [unfold(lines[1], rows * j, devices) for j in (2, 3)]
+        vecs += [unfold(lines[2], rows * j, devices) for j in range(4)]
+        vec_ref[...] = jnp.concatenate(vecs + vecs[:2], axis=0)
 
         red_ref[...] = dot(x_ref[...], ad_ref[0:16, :], NT).astype(half)
 
@@ -326,13 +337,13 @@
     return pl.BlockSpec(dims, lambda i: (0,) * len(dims))
 
 
-def project(x, held, table, parts, shards):
+def project(me, x, held, parts, shards):
     rows, width = x.shape
     devices = held[0].owner.shape[0]
     return pl.pallas_call(
         functools.partial(project_kernel, len(held), shards),
         grid=(3,),
-        in_specs=[SCALARS, NEAR] + [NEAR] * len(held),
+        in_specs=[SCALARS, SCALARS, NEAR] + [NEAR] * len(held),
         out_specs=[
             NEAR,
             PLACED,
@@ -360,7 +371,7 @@
         ],
         compiler_params=params(LIMITS[0]),
         cost_estimate=cost(8),
-    )(table, x, *[h.array for h in held])
+    )(me, places(held), x, *[h.array for h in held])
 
 
 STEP = 2
@@ -532,7 +543,7 @@
     )(*[pltpu.with_memory_space_constraint(t, pltpu.HBM) for t in (qkv, qkv, qkv, g, mixed, p, x)], red, ad)
 
 
-def feed_kernel(specs, table_ref, vec_ref, bin_ref, mixed_ref, x_ref, grad_ref, inv_ref, *refs):
+def feed_kernel(specs, me_ref, table_ref, vec_ref, bin_ref, mixed_ref, x_ref, grad_ref, inv_ref, *refs):
     arrays = 1 + max(i for spec in specs for i, _ in spec)
     block_refs = refs[:arrays]
     out_out, d_one_out, g_out = refs[arrays : arrays + 3]
@@ -545,6 +556,7 @@
     parts = win_ref.shape[0]
     per = devices // parts
     rows = width // devices
+    me = me_ref[0]
     copies = []
     for n, (target, spec) in enumerate(zip((wo_ref, one_ref, fc_ref), specs)):
         count = target.shape[1]
@@ -554,7 +566,7 @@
             for b in range(ref.shape[0]):
                 source = ref.at[b] if ref.shape[1] == count else ref.at[b, pl.ds(start, count)]
                 i = len(some)
-                some.append(pltpu.make_async_copy(source, target.at[table_ref[i]], sems.at[n, i]))
+                some.append(pltpu.make_async_copy(source, target.at[table_ref[me, i]], sems.at[n, i]))
         copies.append(some)
     for copy in copies[0]:
         copy.start()
@@ -644,14 +656,14 @@
         copy.wait()
 
 
-def feed(mixed, x, grad, inv, arrays, specs, counts, table, vec, bias):
+def feed(me, mixed, x, grad, inv, arrays, specs, counts, table, vec, bias):
     rows, width = x.shape
     devices = table.shape[0]
     parts = bias.shape[0]
     vmem = pltpu.VMEM
     return pl.pallas_call(
         functools.partial(feed_kernel, specs),
-        in_specs=[SCALARS] + [NEAR] * 6 + [PLACED] * len(arrays),
+        in_specs=[SCALARS, SCALARS] + [NEAR] * 6 + [PLACED] * len(arrays),
         out_specs=[PLACED] * 3,
         out_shape=[shape((rows, width), half), shape((rows, width), wide), shape((rows, width), half)],
         scratch_shapes=[vmem((devices, count, width), half) for count in counts]
@@ -670,7 +682,7 @@
         ],
         compiler_params=params(LIMITS[2]),
         cost_estimate=cost(40),
-    )(table, vec, bias, mixed, x, grad, inv, *arrays)
+    )(me, table, vec, bias, mixed, x, grad, inv, *arrays)
 
 
 def project_back_kernel(d_ref, w_ref, one_ref, d_red_ref, ad_ref, grad_ref):
@@ -698,7 +710,7 @@
         out_shape=shape((rows, width), wide),
         compiler_params=params(LIMITS[4]),
         cost_estimate=cost(8),
-    )(*[pltpu.with_memory_space_constraint(t, pltpu.HBM) for t in (d_qkv, wqkv, d_one)], d_red, ad)
+    )(*[pltpu.with_memory_space_constraint(t, pltpu.HBM) for t in (d_qkv, wqkv, d_one, d_red)], ad)
 
 
 def body(
@@ -730,6 +742,7 @@
     key_feat = jnp.where(same | ((lane == slots) & padded), masked, 0.0).astype(half)
 
     staged = devices == 32
+    me = lax.axis_index(AXES).astype(jnp.int32).reshape(1)
     split = w_fc.shape[0]
     if staged:
         list_a, state = gather_attention(pack_a, pack_b)
@@ -737,18 +750,19 @@
     else:
         lists = [[everyone(p, devices)] for p in (pack_a, pack_1[split:], pack_1[:split], w_fc)]
         list_a = lists[0]
-    qkv, qkv_far, reduced, factors, vec, bias_in, wqkv = project(hidden_in, list_a, places(list_a), ffn_parts, shards)
+    qkv, qkv_far, reduced, factors, vec, bias_in, wqkv = project(me, hidden_in, list_a, ffn_parts, shards)
     before = ()
     if staged:
         ring.step(reduced)
+        ring.swap(reduced, 1)
     for w in range(windows):
         before = attend(w, qkv, query_feat, key_feat, before)
         if staged:
             ring.step(before[0])
-            ring.swap(before[0], w + 1)
+            ring.swap(before[0], w + 2)
     mixed, inv, probs = before
     if staged:
-        ring.swap(mixed, 4)
+        ring.end(mixed)
         held = ring.held
         arrays = [h.array for h in held]
         specs = [[(i, start) for i in range(len(held))] for start in (2 * split, split, 0)]
@@ -757,7 +771,7 @@
         specs = [[(0, 0)], [(1, 0)], [(2, 0)]]
     counts = pack_1.shape[0] - split, split, split
     hidden_out, d_one, g = feed(
-        mixed, hidden_in, grad_out, inv, arrays, specs, counts, places(held), vec, bias_in
+        me, mixed, hidden_in, grad_out, inv, arrays, specs, counts, places(held), vec, bias_in
     )
     d_qkv, d_reduced, partial_grad = attend_back(qkv_far, g, mixed, probs, hidden_in, reduced, factors, devices)
     grad_in = project_back(d_qkv, d_one, d_reduced, wqkv, factors)

time: 172 us -> 165 us (0.959)
  waiting for transfers between devices: 35.3 us -> 25.7 us
  starting transfers between devices: 31.6 us -> 36.8 us
  local copies, waits for them, and re-layouts: 9.09 us -> 7.07 us
    ppermute x34 -> x37, waiting for transfers between devices: 35.3 us -> 25.7 us  [send(): return Held(lax.ppermute(self.array, AXES, pairs), owner)]
    ppermute x34 -> x37, starting transfers between devices: 27.4 us -> 31.5 us  [send(): return Held(lax.ppermute(self.array, AXES, pairs), owner)]
    squeeze x2 -> x0, local copies, waits for them, and re-layouts: 1.89 us -> none  [places(): lax.dynamic_index_in_dim(jnp.asarray(table, jnp.int32), lax.axis_index(AX...]
    unnamed x47 -> x58, local copies, waits for them, and re-layouts: 5.9 us -> 5.8 us
  transfers between devices with their start and end apart: 35 -> 38, of which waited for: 12 -> 12; matrix products, arithmetic and copies ran while one was open for 5% -> 3% of each run, Pallas kernels for 19% -> 20%
where the time goes in v4:
time: 165 us; the launch traced here: 164 us
  Pallas kernels  91.5 us (55%)
  starting transfers between devices  36.8 us (22%)
  waiting for transfers between devices  25.7 us (16%)
  local copies, waits for them, and re-layouts  7.07 us (4%)
  other arithmetic  2.24 us (1%)
    pallas_call x1, Pallas kernels, feed(): pl.pallas_call(functools.partial(feed_kernel, specs), in_specs=[SCALARS,...  37.5 us
    ppermute x37, starting transfers between devices, send(): return Held(lax.ppermute(self.array, AXES, pairs), owner)  31.5 us
    ppermute x37, waiting for transfers between devices, send(): return Held(lax.ppermute(self.array, AXES, pairs), owner)  25.7 us
    pallas_call x1, Pallas kernels, attend_back(): pl.pallas_call(attend_back_kernel, grid=(windows, pairs // STEP), in_spec...  19 us
    pallas_call x2, Pallas kernels, attend(): pl.pallas_call(attend_kernel, grid=(pairs // STEP,), in_specs=heads + [fe...  13.4 us
    pallas_call x1, Pallas kernels, project(): pl.pallas_call(functools.partial(project_kernel, len(held), shards), grid...  10.8 us
    pallas_call x1, Pallas kernels, project_back(): pl.pallas_call(project_back_kernel, grid=(rows // tile,), in_specs=[pl.Bl...  8.77 us
    unnamed x58, local copies, waits for them, and re-layouts  5.8 us
  transfers between devices with their start and end apart: 38, of which 12 were waited for; matrix products, arithmetic and copies ran while one was open for 3% of the time, Pallas kernels for 20%

profile of v4, /device:TPU:0, one launch (start us, length us, event | category | flops | bytes accessed | tf_op | source)
XLA Modules:
  0.0 164.4 jit_solution(5848425214168066144)
XLA Ops:
  0.7 2.0 %shard_map.236 = (bf16[80,768]{1,0:T(8,128)(2,1)}, bf16[224,768]{1,0:T(8,128)(2,1)}, bf16[128,768]{1,0:T(8,128)(2,1)}) custom-call(bf16[24,2304]{1,0:T(8,128)(2,1)} %wqkv_ref.1, bf16[24,768]{1,0:T(8,128)(2,1)} %wout_ref.1, bf16[24,3072]{1,0:T(8,128)(2,1)} %win_ref.1, bf16[96,768]{1,0:T(8,128)(2,1)} %wfc_ref.1, f32[768]{0:T(1024)} %factor_ref.1, ...), custom_call_target="tpu_custom_call" | custom-call | flops 1600000000 | bytes 5000000 | tf_op jit(solution)/shard_map/pallas_call | solution.py:263
  2.7 3.1 %collective-permute-start.2 = (bf16[1,80,768]{2,1,0:T(8,128)(2,1)}, bf16[1,80,768]{2,1,0:T(8,128)(2,1)S(1)}, u32[]{:S(2)}, u32[]{:S(2)}) collective-permute-start(bf16[1,80,768]{2,1,0:T(8,128)(2,1)} %bitcast.7), channel_id=1, source_target_pairs={{0,8},{1,9},{2,10},{3,11},{4,12},{5,13},{6,14},{7,15},{8,16},{9,17... | collective-permute-start | bytes 368648 | tf_op jit(solution)/shard_map/ppermute | solution.py:77
  5.8 2.1 %collective-permute-start.3 = (bf16[1,80,768]{2,1,0:T(8,128)(2,1)}, bf16[1,80,768]{2,1,0:T(8,128)(2,1)S(1)}, u32[]{:S(2)}, u32[]{:S(2)}) collective-permute-start(bf16[1,80,768]{2,1,0:T(8,128)(2,1)} %bitcast.8), channel_id=1, source_target_pairs={{0,24},{1,25},{2,26},{3,27},{4,28},{5,29},{6,30},{7,31},{8,0},{9,1... | collective-permute-start | bytes 368648 | tf_op jit(solution)/shard_map/ppermute | solution.py:77
  7.9 1.6 %collective-permute-start = (bf16[1,80,768]{2,1,0:T(8,128)(2,1)}, bf16[1,80,768]{2,1,0:T(8,128)(2,1)S(1)}, u32[]{:S(2)}, u32[]{:S(2)}) collective-permute-start(bf16[1,80,768]{2,1,0:T(8,128)(2,1)} %bitcast.9), channel_id=1, source_target_pairs={{0,2},{1,5},{2,0},{3,7},{4,6},{5,1},{6,4},{7,3},{8,10},{9,13},{10,... | collective-permute-start | bytes 368648 | tf_op jit(solution)/shard_map/ppermute | solution.py:77
  13.4 1.6 collective-permute-start.4
  15.9 1.6 collective-permute-start.1
  17.5 1.7 %collective-permute-done.5 = bf16[1,80,768]{2,1,0:T(8,128)(2,1)S(1)} collective-permute-done((bf16[1,80,768]{2,1,0:T(8,128)(2,1)}, bf16[1,80,768]{2,1,0:T(8,128)(2,1)S(1)}, u32[]{:S(2)}, u32[]{:S(2)}) %collective-permute-start.5) | collective-permute-done | bytes 122912 | tf_op jit(solution)/shard_map/ppermute | solution.py:77
  19.3 1.5 collective-permute-start.6
  20.8 2.3 %collective-permute-done.4 = bf16[2,80,768]{2,1,0:T(8,128)(2,1)S(1)} collective-permute-done((bf16[2,80,768]{2,1,0:T(8,128)(2,1)S(1)}, bf16[2,80,768]{2,1,0:T(8,128)(2,1)S(1)}, u32[]{:S(2)}, u32[]{:S(2)}) %collective-permute-start.4) | collective-permute-done | bytes 245792 | tf_op jit(solution)/shard_map/ppermute | solution.py:77
  23.1 2.4 %collective-permute-start.7 = (bf16[4,80,768]{2,1,0:T(8,128)(2,1)S(1)}, bf16[4,80,768]{2,1,0:T(8,128)(2,1)}, u32[]{:S(2)}, u32[]{:S(2)}) collective-permute-start(bf16[4,80,768]{2,1,0:T(8,128)(2,1)S(1)} %constant_dynamic-update-slice_fusion.refs_2_), channel_id=1, source_target_pairs={{0,4},{1,3},{2,6},{3,1},{4,0},{5,7},{6,2},{7,5},{8,12},{9,11},{10,... | collective-permute-start | bytes 1474568 | tf_op jit(solution)/shard_map/ppermute | solution.py:77
  25.5 2.9 %collective-permute-start.19 = (bf16[1,224,768]{2,1,0:T(8,128)(2,1)}, bf16[1,224,768]{2,1,0:T(8,128)(2,1)}, u32[]{:S(2)}, u32[]{:S(2)}) collective-permute-start(bf16[1,224,768]{2,1,0:T(8,128)(2,1)} %bitcast.5), channel_id=1, source_target_pairs={{0,8},{1,25},{2,10},{3,27},{4,12},{5,29},{6,14},{7,31},{8,16},{9,1... | collective-permute-start | bytes 1032200 | tf_op jit(solution)/shard_map/ppermute | solution.py:77
  29.1 3.3 %collective-permute-done.7.refs_4_ = bf16[4,80,768]{2,1,0:T(8,128)(2,1)} collective-permute-done((bf16[4,80,768]{2,1,0:T(8,128)(2,1)S(1)}, bf16[4,80,768]{2,1,0:T(8,128)(2,1)}, u32[]{:S(2)}, u32[]{:S(2)}) %collective-permute-start.7) | collective-permute-done | bytes 491552 | tf_op jit(solution)/shard_map/ppermute | solution.py:77
  33.6 3.7 %collective-permute-done.19 = bf16[1,224,768]{2,1,0:T(8,128)(2,1)} collective-permute-done((bf16[1,224,768]{2,1,0:T(8,128)(2,1)}, bf16[1,224,768]{2,1,0:T(8,128)(2,1)}, u32[]{:S(2)}, u32[]{:S(2)}) %collective-permute-start.19) | collective-permute-done | bytes 344096 | tf_op jit(solution)/shard_map/ppermute | solution.py:77
  43.5 10.8 %shard_map.237 = (bf16[3,1024,768]{2,1,0:T(8,128)(2,1)S(1)}, bf16[3,1024,768]{2,1,0:T(8,128)(2,1)}, bf16[1024,16]{1,0:T(8,128)(2,1)}, bf16[32,768]{1,0:T(8,128)(...) custom-call(s32[1]{0:T(128)} %bitcast.me_ref, s32[32,32]{1,0:T(8,128)S(1)} %copy-done.3, ...), custom_call_target="tpu_custom_call" | custom-call | flops 6400000000 | bytes 20000000 | tf_op jit(solution)/shard_map/pallas_call | solution.py:343
  58.1 6.7 %shard_map.238 = (bf16[1024,768]{1,0:T(8,128)(2,1)}, f32[1024,768]{1,0:T(8,128)}, bf16[2,6,1024,512]{3,2,1,0:T(8,128)(2,1)}) custom-call(bf16[3,1024,768]{2,1,0:T(8,128)(2,1)S(1)} %get-tuple-element.49.q_ref.k_ref.v_ref, bf16[3,1024,768]{2,1,0:T(8,128)(2,1)S(1)} %get-tuple-element.49.q_ref.k_ref.v_ref, ...), custom_call_target="tpu_custom_call" | custom-call | flops 4800000000 | bytes 15000000 | tf_op jit(solution)/shard_map/pallas_call | solution.py:426
  69.0 6.7 %shard_map.239 = (bf16[1024,768]{1,0:T(8,128)(2,1)}, f32[1024,768]{1,0:T(8,128)}, bf16[2,6,1024,512]{3,2,1,0:T(8,128)(2,1)}) custom-call(bf16[3,1024,768]{2,1,0:T(8,128)(2,1)S(1)} %get-tuple-element.49.q_ref.k_ref.v_ref, bf16[3,1024,768]{2,1,0:T(8,128)(2,1)S(1)} %get-tuple-element.49.q_ref.k_ref.v_ref, ...), custom_call_target="tpu_custom_call", output_to_operand_aliasing={{0}: (5, {}), {1}: (6, {}), {2}: (7, {})} | custom-call | flops 4800000000 | bytes 15000000 | tf_op jit(solution)/shard_map/pallas_call | solution.py:426
  75.8 2.0 %collective-permute-done.30.refs_14_ = bf16[1,224,768]{2,1,0:T(8,128)(2,1)S(1)} collective-permute-done((bf16[1,224,768]{2,1,0:T(8,128)(2,1)S(1)}, bf16[1,224,768]{2,1,0:T(8,128)(2,1)S(1)}, u32[]{:S(2)}, u32[]{:S(2)}) %collective-permute-start.30) | collective-permute-done | bytes 344096 | tf_op jit(solution)/shard_map/ppermute | solution.py:77
  78.6 4.7 %collective-permute-done.31.refs_16_ = bf16[1,224,768]{2,1,0:T(8,128)(2,1)S(1)} collective-permute-done((bf16[1,224,768]{2,1,0:T(8,128)(2,1)S(1)}, bf16[1,224,768]{2,1,0:T(8,128)(2,1)S(1)}, u32[]{:S(2)}, u32[]{:S(2)}) %collective-permute-start.31) | collective-permute-done | bytes 344096 | tf_op jit(solution)/shard_map/ppermute | solution.py:77
  84.7 2.4 %collective-permute-done.35.refs_18_ = bf16[1,224,768]{2,1,0:T(8,128)(2,1)} collective-permute-done((bf16[1,224,768]{2,1,0:T(8,128)(2,1)S(1)}, bf16[1,224,768]{2,1,0:T(8,128)(2,1)}, u32[]{:S(2)}, u32[]{:S(2)}) %collective-permute-start.35) | collective-permute-done | bytes 344096 | tf_op jit(solution)/shard_map/ppermute | solution.py:77
  89.5 2.4 %collective-permute-done.36.refs_19_ = bf16[1,224,768]{2,1,0:T(8,128)(2,1)S(1)} collective-permute-done((bf16[1,224,768]{2,1,0:T(8,128)(2,1)}, bf16[1,224,768]{2,1,0:T(8,128)(2,1)S(1)}, u32[]{:S(2)}, u32[]{:S(2)}) %collective-permute-start.36) | collective-permute-done | bytes 344096 | tf_op jit(solution)/shard_map/ppermute | solution.py:77
  92.9 37.5 %shard_map.240 = (bf16[1024,768]{1,0:T(8,128)(2,1)}, f32[1024,768]{1,0:T(8,128)}, bf16[1024,768]{1,0:T(8,128)(2,1)}) custom-call(s32[1]{0:T(128)} %bitcast.me_ref, s32[32,32]{1,0:T(8,128)} %constant.55.clone.table_ref, f32[8,768]{1,0:T(8,128)} %get-tuple-element.47.vec_ref, bf16[4,1,768]{2,1,0:T(2,128)(2,1)} %get-tuple-element.48.bin_ref, ...), custom_call_target="tpu_custom_call" | custom-call | flops 32000000000 | bytes 100000000 | tf_op jit(solution)/shard_map/pallas_call | solution.py:664
  130.4 19.0 %shard_map.241 = (bf16[3,1024,768]{2,1,0:T(8,128)(2,1)}, bf16[1024,16]{1,0:T(8,128)(2,1)}, f32[32,8,96]{2,1,0:T(8,128)}) custom-call(bf16[3,1024,768]{2,1,0:T(8,128)(2,1)} %get-tuple-element.78.q_ref.k_ref.v_ref, bf16[3,1024,768]{2,1,0:T(8,128)(2,1)} %get-tuple-element.78.q_ref.k_ref.v_ref, bf16[3,1024,768]{2,1,0:T(8,128)(2,1)} %get-tuple-element.78.q_ref.k_ref.v_ref, ...), custom_call_target="tpu_custom_call" | custom-call | flops 16000000000 | bytes 50000000 | tf_op jit(solution)/shard_map/pallas_call | solution.py:522
  149.3 5.4 %all-to-all-start = ((f32[32,8,96]{2,1,0:T(8,128)}), f32[32,8,96]{2,1,0:T(8,128)S(1)}, u32[]{:S(2)}, u32[]{:S(2)}) async-start(f32[32,8,96]{2,1,0:T(8,128)} %get-tuple-element.86), calls=%async_computation | async-start | bytes 262144 | tf_op jit(solution)/shard_map/all_to_all | solution.py:778
  154.8 8.8 %shard_map.242 = f32[1024,768]{1,0:T(8,128)} custom-call(bf16[3,1024,768]{2,1,0:T(8,128)(2,1)} %get-tuple-element.82.d_ref, bf16[3,768,768]{2,1,0:T(8,128)(2,1)} %get-tuple-element.83.w_ref, f32[1024,768]{1,0:T(8,128)} %get-tuple-element.84.one_ref, bf16[1024,16]{1,0:T(8,128)(2,1)} %get-tuple-element.85.d_red_ref, bf16[32,768]{1,0:T(8,128)(2,1)S(1)} %copy-done.5), custom_call_target="tpu_custom_call" | custom-call | flops 6400000000 | bytes 20000000 | tf_op jit(solution)/shard_map/pallas_call | solution.py:699
  (134 shorter events, 27.3 us)
Async XLA Ops:
  2.7 9.5 %collective-permute-start.2 = (bf16[1,80,768]{2,1,0:T(8,128)(2,1)}, bf16[1,80,768]{2,1,0:T(8,128)(2,1)S(1)}, u32[]{:S(2)}, u32[]{:S(2)}) collective-permute-start(bf16[1,80,768]{2,1,0:T(8,128)(2,1)} %bitcast.7), channel_id=1, source_target_pairs={{0,8},{1,9},{2,10},{3,11},{4,12},{5,13},{6,14},{7,15},{8,16},{9,17... | collective-permute-start | bytes 368648 | tf_op jit(solution)/shard_map/ppermute | solution.py:77
  9.5 9.7 %collective-permute-start.5 = (bf16[1,80,768]{2,1,0:T(8,128)(2,1)}, bf16[1,80,768]{2,1,0:T(8,128)(2,1)S(1)}, u32[]{:S(2)}, u32[]{:S(2)}) collective-permute-start(bf16[1,80,768]{2,1,0:T(8,128)(2,1)} %bitcast.10), channel_id=1, source_target_pairs={{0,16},{1,17},{2,18},{3,19},{4,20},{5,21},{6,22},{7,23},{8,24},{9,... | collective-permute-start | bytes 368648 | tf_op jit(solution)/shard_map/ppermute | solution.py:77
  10.3 18.0 %collective-permute-start.15 = (bf16[1,224,768]{2,1,0:T(8,128)(2,1)}, bf16[1,224,768]{2,1,0:T(8,128)(2,1)}, u32[]{:S(2)}, u32[]{:S(2)}) collective-permute-start(bf16[1,224,768]{2,1,0:T(8,128)(2,1)} %bitcast.4), channel_id=1, source_target_pairs={{0,2},{1,5},{2,0},{3,7},{4,6},{5,1},{6,4},{7,3},{8,10},{9,13},{10,... | collective-permute-start | bytes 1032200 | tf_op jit(solution)/shard_map/ppermute | solution.py:77
  13.4 9.6 %collective-permute-start.4 = (bf16[2,80,768]{2,1,0:T(8,128)(2,1)S(1)}, bf16[2,80,768]{2,1,0:T(8,128)(2,1)S(1)}, u32[]{:S(2)}, u32[]{:S(2)}) collective-permute-start(bf16[2,80,768]{2,1,0:T(8,128)(2,1)S(1)} %pad_maximum_fusion.1), channel_id=1, source_target_pairs={{0,2},{1,5},{2,0},{3,7},{4,6},{5,1},{6,4},{7,3},{8,10},{9,13},{10,... | collective-permute-start | bytes 737288 | tf_op jit(solution)/shard_map/ppermute | solution.py:77
  15.9 13.0 %collective-permute-start.1 = (bf16[2,80,768]{2,1,0:T(8,128)(2,1)S(1)}, bf16[2,80,768]{2,1,0:T(8,128)(2,1)S(1)}, u32[]{:S(2)}, u32[]{:S(2)}) collective-permute-start(bf16[2,80,768]{2,1,0:T(8,128)(2,1)S(1)} %pad_maximum_fusion.refs_0_), channel_id=1, source_target_pairs={{0,4},{1,3},{2,6},{3,1},{4,0},{5,7},{6,2},{7,5},{8,12},{9,11},{10,... | collective-permute-start | bytes 737288 | tf_op jit(solution)/shard_map/ppermute | solution.py:77
  17.5 14.8 %collective-permute-start.9 = (bf16[2,80,768]{2,1,0:T(8,128)(2,1)S(1)}, bf16[2,80,768]{2,1,0:T(8,128)(2,1)S(1)}, u32[]{:S(2)}, u32[]{:S(2)}) collective-permute-start(bf16[2,80,768]{2,1,0:T(8,128)(2,1)S(1)} %pad_maximum_fusion.refs_0_), channel_id=1, source_target_pairs={{0,1},{1,0},{2,3},{3,2},{4,5},{5,4},{6,7},{7,6},{8,9},{9,8},{10,11... | collective-permute-start | bytes 737288 | tf_op jit(solution)/shard_map/ppermute | solution.py:77
  23.1 9.3 %collective-permute-start.7 = (bf16[4,80,768]{2,1,0:T(8,128)(2,1)S(1)}, bf16[4,80,768]{2,1,0:T(8,128)(2,1)}, u32[]{:S(2)}, u32[]{:S(2)}) collective-permute-start(bf16[4,80,768]{2,1,0:T(8,128)(2,1)S(1)} %constant_dynamic-update-slice_fusion.refs_2_), channel_id=1, source_target_pairs={{0,4},{1,3},{2,6},{3,1},{4,0},{5,7},{6,2},{7,5},{8,12},{9,11},{10,... | collective-permute-start | bytes 1474568 | tf_op jit(solution)/shard_map/ppermute | solution.py:77
  25.5 11.8 %collective-permute-start.19 = (bf16[1,224,768]{2,1,0:T(8,128)(2,1)}, bf16[1,224,768]{2,1,0:T(8,128)(2,1)}, u32[]{:S(2)}, u32[]{:S(2)}) collective-permute-start(bf16[1,224,768]{2,1,0:T(8,128)(2,1)} %bitcast.5), channel_id=1, source_target_pairs={{0,8},{1,25},{2,10},{3,27},{4,12},{5,29},{6,14},{7,31},{8,16},{9,1... | collective-permute-start | bytes 1032200 | tf_op jit(solution)/shard_map/ppermute | solution.py:77
  28.4 8.9 %collective-permute-start.8 = (bf16[2,80,768]{2,1,0:T(8,128)(2,1)S(1)}, bf16[2,80,768]{2,1,0:T(8,128)(2,1)}, u32[]{:S(2)}, u32[]{:S(2)}) collective-permute-start(bf16[2,80,768]{2,1,0:T(8,128)(2,1)S(1)} %constant_dynamic-update-slice_fusion.3.refs_3_), channel_id=1, source_target_pairs={{0,4},{1,3},{2,6},{3,1},{4,0},{5,7},{6,2},{7,5},{8,12},{9,11},{10,... | collective-permute-start | bytes 737288 | tf_op jit(solution)/shard_map/ppermute | solution.py:77
  29.0 13.6 %collective-permute-start.11 = (bf16[4,80,768]{2,1,0:T(8,128)(2,1)S(1)}, bf16[4,80,768]{2,1,0:T(8,128)(2,1)}, u32[]{:S(2)}, u32[]{:S(2)}) collective-permute-start(bf16[4,80,768]{2,1,0:T(8,128)(2,1)S(1)} %constant_dynamic-update-slice_fusion.refs_2_), channel_id=1, source_target_pairs={{0,1},{1,0},{2,3},{3,2},{4,5},{5,4},{6,7},{7,6},{8,9},{9,8},{10,11... | collective-permute-start | bytes 1474568 | tf_op jit(solution)/shard_map/ppermute | solution.py:77
  32.3 10.2 %collective-permute-start.13 = (bf16[4,80,768]{2,1,0:T(8,128)(2,1)}, bf16[4,80,768]{2,1,0:T(8,128)(2,1)}, u32[]{:S(2)}, u32[]{:S(2)}) collective-permute-start(bf16[4,80,768]{2,1,0:T(8,128)(2,1)} %collective-permute-done.7.refs_4_), channel_id=1, source_target_pairs={{0,1},{1,0},{2,3},{3,2},{4,5},{5,4},{6,7},{7,6},{8,9},{9,8},{10,11... | collective-permute-start | bytes 1474568 | tf_op jit(solution)/shard_map/ppermute | solution.py:77
  40.2 16.1 %collective-permute-start.20 = (bf16[1,224,768]{2,1,0:T(8,128)(2,1)}, bf16[1,224,768]{2,1,0:T(8,128)(2,1)S(1)}, u32[]{:S(2)}, u32[]{:S(2)}) collective-permute-start(bf16[1,224,768]{2,1,0:T(8,128)(2,1)} %collective-permute-done.19), channel_id=1, source_target_pairs={{0,2},{1,5},{2,0},{3,7},{4,6},{5,1},{6,4},{7,3},{8,10},{9,13},{10,... | collective-permute-start | bytes 1032200 | tf_op jit(solution)/shard_map/ppermute | solution.py:77
  40.8 13.6 %collective-permute-start.24 = (bf16[1,224,768]{2,1,0:T(8,128)(2,1)}, bf16[1,224,768]{2,1,0:T(8,128)(2,1)S(1)}, u32[]{:S(2)}, u32[]{:S(2)}) collective-permute-start(bf16[1,224,768]{2,1,0:T(8,128)(2,1)} %collective-permute-done.19), channel_id=1, source_target_pairs={{0,8},{1,25},{2,10},{3,27},{4,12},{5,29},{6,14},{7,31},{8,16},{9,1... | collective-permute-start | bytes 1032200 | tf_op jit(solution)/shard_map/ppermute | solution.py:77
  41.8 24.5 %collective-permute-start.16 = (bf16[2,224,768]{2,1,0:T(8,128)(2,1)S(1)}, bf16[2,224,768]{2,1,0:T(8,128)(2,1)S(1)}, u32[]{:S(2)}, u32[]{:S(2)}) collective-permute-start(bf16[2,224,768]{2,1,0:T(8,128)(2,1)S(1)} %constant_dynamic-update-slice_fusion.5.refs_0_), channel_id=1, source_target_pairs={{0,4},{1,3},{2,6},{3,1},{4,0},{5,7},{6,2},{7,5},{8,12},{9,11},{10,... | collective-permute-start | bytes 2064392 | tf_op jit(solution)/shard_map/ppermute | solution.py:77
  54.4 10.5 %collective-permute-start.25 = (bf16[1,224,768]{2,1,0:T(8,128)(2,1)S(1)}, bf16[1,224,768]{2,1,0:T(8,128)(2,1)S(1)}, u32[]{:S(2)}, u32[]{:S(2)}) collective-permute-start(bf16[1,224,768]{2,1,0:T(8,128)(2,1)S(1)} %collective-permute-done.24), channel_id=1, source_target_pairs={{0,2},{1,5},{2,0},{3,7},{4,6},{5,1},{6,4},{7,3},{8,10},{9,13},{10,... | collective-permute-start | bytes 1032200 | tf_op jit(solution)/shard_map/ppermute | solution.py:77
  54.8 12.0 %collective-permute-start.29 = (bf16[1,224,768]{2,1,0:T(8,128)(2,1)S(1)}, bf16[1,224,768]{2,1,0:T(8,128)(2,1)S(1)}, u32[]{:S(2)}, u32[]{:S(2)}) collective-permute-start(bf16[1,224,768]{2,1,0:T(8,128)(2,1)S(1)} %collective-permute-done.24), channel_id=1, source_target_pairs={{0,8},{1,25},{2,10},{3,27},{4,12},{5,29},{6,14},{7,31},{8,16},{9,1... | collective-permute-start | bytes 1032200 | tf_op jit(solution)/shard_map/ppermute | solution.py:77
  57.3 11.0 %collective-permute-start.21 = (bf16[2,224,768]{2,1,0:T(8,128)(2,1)S(1)}, bf16[2,224,768]{2,1,0:T(8,128)(2,1)S(1)}, u32[]{:S(2)}, u32[]{:S(2)}) collective-permute-start(bf16[2,224,768]{2,1,0:T(8,128)(2,1)S(1)} %constant_dynamic-update-slice_fusion.7.refs_4_), channel_id=1, source_target_pairs={{0,4},{1,3},{2,6},{3,1},{4,0},{5,7},{6,2},{7,5},{8,12},{9,11},{10,... | collective-permute-start | bytes 2064392 | tf_op jit(solution)/shard_map/ppermute | solution.py:77
  64.9 19.1 %collective-permute-start.26 = (bf16[2,224,768]{2,1,0:T(8,128)(2,1)S(1)}, bf16[2,224,768]{2,1,0:T(8,128)(2,1)}, u32[]{:S(2)}, u32[]{:S(2)}) collective-permute-start(bf16[2,224,768]{2,1,0:T(8,128)(2,1)S(1)} %constant_dynamic-update-slice_fusion.9.refs_8_), channel_id=1, source_target_pairs={{0,4},{1,3},{2,6},{3,1},{4,0},{5,7},{6,2},{7,5},{8,12},{9,11},{10,... | collective-permute-start | bytes 2064392 | tf_op jit(solution)/shard_map/ppermute | solution.py:77
  66.2 17.9 %collective-permute-start.17 = (bf16[2,224,768]{2,1,0:T(8,128)(2,1)S(1)}, bf16[2,224,768]{2,1,0:T(8,128)(2,1)S(1)}, u32[]{:S(2)}, u32[]{:S(2)}) collective-permute-start(bf16[2,224,768]{2,1,0:T(8,128)(2,1)S(1)} %constant_dynamic-update-slice_fusion.5.refs_0_), channel_id=1, source_target_pairs={{0,1},{1,0},{2,3},{3,2},{4,5},{5,4},{6,7},{7,6},{8,9},{9,8},{10,11... | collective-permute-start | bytes 2064392 | tf_op jit(solution)/shard_map/ppermute | solution.py:77
  66.3 18.2 %collective-permute-start.18 = (bf16[2,224,768]{2,1,0:T(8,128)(2,1)S(1)}, bf16[2,224,768]{2,1,0:T(8,128)(2,1)S(1)}, u32[]{:S(2)}, u32[]{:S(2)}) collective-permute-start(bf16[2,224,768]{2,1,0:T(8,128)(2,1)S(1)} %collective-permute-done.16.refs_2_), channel_id=1, source_target_pairs={{0,1},{1,0},{2,3},{3,2},{4,5},{5,4},{6,7},{7,6},{8,9},{9,8},{10,11... | collective-permute-start | bytes 2064392 | tf_op jit(solution)/shard_map/ppermute | solution.py:77
  66.8 11.0 %collective-permute-start.30 = (bf16[1,224,768]{2,1,0:T(8,128)(2,1)S(1)}, bf16[1,224,768]{2,1,0:T(8,128)(2,1)S(1)}, u32[]{:S(2)}, u32[]{:S(2)}) collective-permute-start(bf16[1,224,768]{2,1,0:T(8,128)(2,1)S(1)} %collective-permute-done.29.refs_12_), channel_id=1, source_target_pairs={{0,2},{1,5},{2,0},{3,7},{4,6},{5,1},{6,4},{7,3},{8,10},{9,13},{10,... | collective-permute-start | bytes 1032200 | tf_op jit(solution)/shard_map/ppermute | solution.py:77
  68.3 15.0 %collective-permute-start.31 = (bf16[1,224,768]{2,1,0:T(8,128)(2,1)S(1)}, bf16[1,224,768]{2,1,0:T(8,128)(2,1)S(1)}, u32[]{:S(2)}, u32[]{:S(2)}) collective-permute-start(bf16[1,224,768]{2,1,0:T(8,128)(2,1)S(1)} %collective-permute-done.29.refs_12_), channel_id=1, source_target_pairs={{0,4},{1,3},{2,6},{3,1},{4,0},{5,7},{6,2},{7,5},{8,12},{9,11},{10,... | collective-permute-start | bytes 1032200 | tf_op jit(solution)/shard_map/ppermute | solution.py:77
  77.8 9.2 %collective-permute-start.35 = (bf16[1,224,768]{2,1,0:T(8,128)(2,1)S(1)}, bf16[1,224,768]{2,1,0:T(8,128)(2,1)}, u32[]{:S(2)}, u32[]{:S(2)}) collective-permute-start(bf16[1,224,768]{2,1,0:T(8,128)(2,1)S(1)} %collective-permute-done.30.refs_14_), channel_id=1, source_target_pairs={{0,4},{1,3},{2,6},{3,1},{4,0},{5,7},{6,2},{7,5},{8,12},{9,11},{10,... | collective-permute-start | bytes 1032200 | tf_op jit(solution)/shard_map/ppermute | solution.py:77
  149.3 14.2 %all-to-all-start = ((f32[32,8,96]{2,1,0:T(8,128)}), f32[32,8,96]{2,1,0:T(8,128)S(1)}, u32[]{:S(2)}, u32[]{:S(2)}) async-start(f32[32,8,96]{2,1,0:T(8,128)} %get-tuple-element.86), calls=%async_computation | async-start | bytes 262144 | tf_op jit(solution)/shard_map/all_to_all | solution.py:778
  (40 other events, 461.1 us)

commit v5 on v4

--- a/solution.py
+++ b/solution.py
@@ -174,6 +174,8 @@
             pair = join_after(token, *self.waiting.pop())
             self.ways.append(pair)
             self.seconds.append(pair.send(second_way))
+            if len(self.ways) == 3:
+                self.early = [pair, pair.send(other_core)]
         if self.now is not None:
             self.now = after(self.now, Held(token, None))
             if len(self.ways) < 3:
@@ -195,7 +197,11 @@
 
     def swap(self, token, count):
         for pair, second in list(zip(self.ways, self.seconds))[len(self.held) // 4 : count]:
-            self.hand_over(token, [pair, second])
+            if len(self.held) == 8:
+                self.held += self.early
+                self.hand_over(token, [second])
+            else:
+                self.hand_over(token, [pair, second])
 
 
 def everyone(array, devices):

time: 165 us -> 165 us (level)
  no operation moved by 1% of the time
where the time goes in v5:
time: 165 us; the launch traced here: 164 us
  Pallas kernels  91.5 us (55%)
  starting transfers between devices  36.9 us (22%)
  waiting for transfers between devices  25.7 us (16%)
  local copies, waits for them, and re-layouts  6.81 us (4%)
  other arithmetic  2.24 us (1%)
    pallas_call x1, Pallas kernels, feed(): pl.pallas_call(functools.partial(feed_kernel, specs), in_specs=[SCALARS,...  37.5 us
    ppermute x37, starting transfers between devices, send(): return Held(lax.ppermute(self.array, AXES, pairs), owner)  31.5 us
    ppermute x37, waiting for transfers between devices, send(): return Held(lax.ppermute(self.array, AXES, pairs), owner)  25.7 us
    pallas_call x1, Pallas kernels, attend_back(): pl.pallas_call(attend_back_kernel, grid=(windows, pairs // STEP), in_spec...  19 us
    pallas_call x2, Pallas kernels, attend(): pl.pallas_call(attend_kernel, grid=(pairs // STEP,), in_specs=heads + [fe...  13.4 us
    pallas_call x1, Pallas kernels, project(): pl.pallas_call(functools.partial(project_kernel, len(held), shards), grid...  10.8 us
    pallas_call x1, Pallas kernels, project_back(): pl.pallas_call(project_back_kernel, grid=(rows // tile,), in_specs=[pl.Bl...  8.77 us
    unnamed x58, local copies, waits for them, and re-layouts  5.54 us
  transfers between devices with their start and end apart: 38, of which 12 were waited for; matrix products, arithmetic and copies ran while one was open for 3% of the time, Pallas kernels for 20%

profile of v5, /device:TPU:0, one launch (start us, length us, event | category | flops | bytes accessed | tf_op | source)
XLA Modules:
  0.0 164.2 jit_solution(13925366788730543130)
XLA Ops:
  0.7 2.0 %shard_map.236 = (bf16[80,768]{1,0:T(8,128)(2,1)}, bf16[224,768]{1,0:T(8,128)(2,1)}, bf16[128,768]{1,0:T(8,128)(2,1)}) custom-call(bf16[24,2304]{1,0:T(8,128)(2,1)} %wqkv_ref.1, bf16[24,768]{1,0:T(8,128)(2,1)} %wout_ref.1, bf16[24,3072]{1,0:T(8,128)(2,1)} %win_ref.1, bf16[96,768]{1,0:T(8,128)(2,1)} %wfc_ref.1, f32[768]{0:T(1024)} %factor_ref.1, ...), custom_call_target="tpu_custom_call" | custom-call | flops 1600000000 | bytes 5000000 | tf_op jit(solution)/shard_map/pallas_call | solution.py:269
  2.7 3.1 %collective-permute-start.2 = (bf16[1,80,768]{2,1,0:T(8,128)(2,1)}, bf16[1,80,768]{2,1,0:T(8,128)(2,1)S(1)}, u32[]{:S(2)}, u32[]{:S(2)}) collective-permute-start(bf16[1,80,768]{2,1,0:T(8,128)(2,1)} %bitcast.7), channel_id=1, source_target_pairs={{0,8},{1,9},{2,10},{3,11},{4,12},{5,13},{6,14},{7,15},{8,16},{9,17... | collective-permute-start | bytes 368648 | tf_op jit(solution)/shard_map/ppermute | solution.py:77
  5.8 2.1 %collective-permute-start.3 = (bf16[1,80,768]{2,1,0:T(8,128)(2,1)}, bf16[1,80,768]{2,1,0:T(8,128)(2,1)S(1)}, u32[]{:S(2)}, u32[]{:S(2)}) collective-permute-start(bf16[1,80,768]{2,1,0:T(8,128)(2,1)} %bitcast.8), channel_id=1, source_target_pairs={{0,24},{1,25},{2,26},{3,27},{4,28},{5,29},{6,30},{7,31},{8,0},{9,1... | collective-permute-start | bytes 368648 | tf_op jit(solution)/shard_map/ppermute | solution.py:77
  7.9 1.6 %collective-permute-start = (bf16[1,80,768]{2,1,0:T(8,128)(2,1)}, bf16[1,80,768]{2,1,0:T(8,128)(2,1)S(1)}, u32[]{:S(2)}, u32[]{:S(2)}) collective-permute-start(bf16[1,80,768]{2,1,0:T(8,128)(2,1)} %bitcast.9), channel_id=1, source_target_pairs={{0,2},{1,5},{2,0},{3,7},{4,6},{5,1},{6,4},{7,3},{8,10},{9,13},{10,... | collective-permute-start | bytes 368648 | tf_op jit(solution)/shard_map/ppermute | solution.py:77
  13.4 1.6 collective-permute-start.4
  15.9 1.6 collective-permute-start.1
  17.5 1.7 %collective-permute-done.5 = bf16[1,80,768]{2,1,0:T(8,128)(2,1)S(1)} collective-permute-done((bf16[1,80,768]{2,1,0:T(8,128)(2,1)}, bf16[1,80,768]{2,1,0:T(8,128)(2,1)S(1)}, u32[]{:S(2)}, u32[]{:S(2)}) %collective-permute-start.5) | collective-permute-done | bytes 122912 | tf_op jit(solution)/shard_map/ppermute | solution.py:77
  19.3 1.5 collective-permute-start.6
  20.8 2.3 %collective-permute-done.4 = bf16[2,80,768]{2,1,0:T(8,128)(2,1)S(1)} collective-permute-done((bf16[2,80,768]{2,1,0:T(8,128)(2,1)S(1)}, bf16[2,80,768]{2,1,0:T(8,128)(2,1)S(1)}, u32[]{:S(2)}, u32[]{:S(2)}) %collective-permute-start.4) | collective-permute-done | bytes 245792 | tf_op jit(solution)/shard_map/ppermute | solution.py:77
  23.1 2.4 %collective-permute-start.7 = (bf16[4,80,768]{2,1,0:T(8,128)(2,1)S(1)}, bf16[4,80,768]{2,1,0:T(8,128)(2,1)}, u32[]{:S(2)}, u32[]{:S(2)}) collective-permute-start(bf16[4,80,768]{2,1,0:T(8,128)(2,1)S(1)} %constant_dynamic-update-slice_fusion.refs_2_), channel_id=1, source_target_pairs={{0,4},{1,3},{2,6},{3,1},{4,0},{5,7},{6,2},{7,5},{8,12},{9,11},{10,... | collective-permute-start | bytes 1474568 | tf_op jit(solution)/shard_map/ppermute | solution.py:77
  25.5 2.9 %collective-permute-start.19 = (bf16[1,224,768]{2,1,0:T(8,128)(2,1)}, bf16[1,224,768]{2,1,0:T(8,128)(2,1)}, u32[]{:S(2)}, u32[]{:S(2)}) collective-permute-start(bf16[1,224,768]{2,1,0:T(8,128)(2,1)} %bitcast.5), channel_id=1, source_target_pairs={{0,8},{1,25},{2,10},{3,27},{4,12},{5,29},{6,14},{7,31},{8,16},{9,1... | collective-permute-start | bytes 1032200 | tf_op jit(solution)/shard_map/ppermute | solution.py:77
  29.1 3.3 %collective-permute-done.7.refs_4_ = bf16[4,80,768]{2,1,0:T(8,128)(2,1)} collective-permute-done((bf16[4,80,768]{2,1,0:T(8,128)(2,1)S(1)}, bf16[4,80,768]{2,1,0:T(8,128)(2,1)}, u32[]{:S(2)}, u32[]{:S(2)}) %collective-permute-start.7) | collective-permute-done | bytes 491552 | tf_op jit(solution)/shard_map/ppermute | solution.py:77
  33.6 3.7 %collective-permute-done.19 = bf16[1,224,768]{2,1,0:T(8,128)(2,1)} collective-permute-done((bf16[1,224,768]{2,1,0:T(8,128)(2,1)}, bf16[1,224,768]{2,1,0:T(8,128)(2,1)}, u32[]{:S(2)}, u32[]{:S(2)}) %collective-permute-start.19) | collective-permute-done | bytes 344096 | tf_op jit(solution)/shard_map/ppermute | solution.py:77
  43.5 10.8 %shard_map.237 = (bf16[3,1024,768]{2,1,0:T(8,128)(2,1)S(1)}, bf16[3,1024,768]{2,1,0:T(8,128)(2,1)}, bf16[1024,16]{1,0:T(8,128)(2,1)}, bf16[32,768]{1,0:T(8,128)(...) custom-call(s32[1]{0:T(128)} %bitcast.me_ref, s32[32,32]{1,0:T(8,128)S(1)} %copy-done.3, ...), custom_call_target="tpu_custom_call" | custom-call | flops 6400000000 | bytes 20000000 | tf_op jit(solution)/shard_map/pallas_call | solution.py:349
  58.1 6.7 %shard_map.238 = (bf16[1024,768]{1,0:T(8,128)(2,1)}, f32[1024,768]{1,0:T(8,128)}, bf16[2,6,1024,512]{3,2,1,0:T(8,128)(2,1)}) custom-call(bf16[3,1024,768]{2,1,0:T(8,128)(2,1)S(1)} %get-tuple-element.48.q_ref.k_ref.v_ref, bf16[3,1024,768]{2,1,0:T(8,128)(2,1)S(1)} %get-tuple-element.48.q_ref.k_ref.v_ref, ...), custom_call_target="tpu_custom_call" | custom-call | flops 4800000000 | bytes 15000000 | tf_op jit(solution)/shard_map/pallas_call | solution.py:432
  69.0 6.7 %shard_map.239 = (bf16[1024,768]{1,0:T(8,128)(2,1)}, f32[1024,768]{1,0:T(8,128)}, bf16[2,6,1024,512]{3,2,1,0:T(8,128)(2,1)}) custom-call(bf16[3,1024,768]{2,1,0:T(8,128)(2,1)S(1)} %get-tuple-element.48.q_ref.k_ref.v_ref, bf16[3,1024,768]{2,1,0:T(8,128)(2,1)S(1)} %get-tuple-element.48.q_ref.k_ref.v_ref, ...), custom_call_target="tpu_custom_call", output_to_operand_aliasing={{0}: (5, {}), {1}: (6, {}), {2}: (7, {})} | custom-call | flops 4800000000 | bytes 15000000 | tf_op jit(solution)/shard_map/pallas_call | solution.py:432
  75.8 2.0 %collective-permute-done.30.refs_14_ = bf16[1,224,768]{2,1,0:T(8,128)(2,1)S(1)} collective-permute-done((bf16[1,224,768]{2,1,0:T(8,128)(2,1)S(1)}, bf16[1,224,768]{2,1,0:T(8,128)(2,1)S(1)}, u32[]{:S(2)}, u32[]{:S(2)}) %collective-permute-start.30) | collective-permute-done | bytes 344096 | tf_op jit(solution)/shard_map/ppermute | solution.py:77
  78.6 4.7 %collective-permute-done.31.refs_16_ = bf16[1,224,768]{2,1,0:T(8,128)(2,1)S(1)} collective-permute-done((bf16[1,224,768]{2,1,0:T(8,128)(2,1)S(1)}, bf16[1,224,768]{2,1,0:T(8,128)(2,1)S(1)}, u32[]{:S(2)}, u32[]{:S(2)}) %collective-permute-start.31) | collective-permute-done | bytes 344096 | tf_op jit(solution)/shard_map/ppermute | solution.py:77
  84.7 2.4 %collective-permute-done.35.refs_18_ = bf16[1,224,768]{2,1,0:T(8,128)(2,1)} collective-permute-done((bf16[1,224,768]{2,1,0:T(8,128)(2,1)S(1)}, bf16[1,224,768]{2,1,0:T(8,128)(2,1)}, u32[]{:S(2)}, u32[]{:S(2)}) %collective-permute-start.35) | collective-permute-done | bytes 344096 | tf_op jit(solution)/shard_map/ppermute | solution.py:77
  89.5 2.4 %collective-permute-done.36.refs_19_ = bf16[1,224,768]{2,1,0:T(8,128)(2,1)S(1)} collective-permute-done((bf16[1,224,768]{2,1,0:T(8,128)(2,1)}, bf16[1,224,768]{2,1,0:T(8,128)(2,1)S(1)}, u32[]{:S(2)}, u32[]{:S(2)}) %collective-permute-start.36) | collective-permute-done | bytes 344096 | tf_op jit(solution)/shard_map/ppermute | solution.py:77
  92.6 37.5 %shard_map.240 = (bf16[1024,768]{1,0:T(8,128)(2,1)}, f32[1024,768]{1,0:T(8,128)}, bf16[1024,768]{1,0:T(8,128)(2,1)}) custom-call(s32[1]{0:T(128)} %bitcast.me_ref, s32[32,32]{1,0:T(8,128)} %constant.55.clone.table_ref, f32[8,768]{1,0:T(8,128)} %get-tuple-element.46.vec_ref, bf16[4,1,768]{2,1,0:T(2,128)(2,1)} %get-tuple-element.47.bin_ref, ...), custom_call_target="tpu_custom_call" | custom-call | flops 32000000000 | bytes 100000000 | tf_op jit(solution)/shard_map/pallas_call | solution.py:670
  130.1 19.0 %shard_map.241 = (bf16[3,1024,768]{2,1,0:T(8,128)(2,1)}, bf16[1024,16]{1,0:T(8,128)(2,1)}, f32[32,8,96]{2,1,0:T(8,128)}) custom-call(bf16[3,1024,768]{2,1,0:T(8,128)(2,1)} %get-tuple-element.76.q_ref.k_ref.v_ref, bf16[3,1024,768]{2,1,0:T(8,128)(2,1)} %get-tuple-element.76.q_ref.k_ref.v_ref, bf16[3,1024,768]{2,1,0:T(8,128)(2,1)} %get-tuple-element.76.q_ref.k_ref.v_ref, ...), custom_call_target="tpu_custom_call" | custom-call | flops 16000000000 | bytes 50000000 | tf_op jit(solution)/shard_map/pallas_call | solution.py:528
  149.1 5.4 %all-to-all-start = ((f32[32,8,96]{2,1,0:T(8,128)}), f32[32,8,96]{2,1,0:T(8,128)S(1)}, u32[]{:S(2)}, u32[]{:S(2)}) async-start(f32[32,8,96]{2,1,0:T(8,128)} %get-tuple-element.84), calls=%async_computation | async-start | bytes 262144 | tf_op jit(solution)/shard_map/all_to_all | solution.py:784
  154.5 8.8 %shard_map.242 = f32[1024,768]{1,0:T(8,128)} custom-call(bf16[3,1024,768]{2,1,0:T(8,128)(2,1)} %get-tuple-element.80.d_ref, bf16[3,768,768]{2,1,0:T(8,128)(2,1)} %get-tuple-element.81.w_ref, f32[1024,768]{1,0:T(8,128)} %get-tuple-element.82.one_ref, bf16[1024,16]{1,0:T(8,128)(2,1)} %get-tuple-element.83.d_red_ref, bf16[32,768]{1,0:T(8,128)(2,1)S(1)} %copy-done.5), custom_call_target="tpu_custom_call" | custom-call | flops 6400000000 | bytes 20000000 | tf_op jit(solution)/shard_map/pallas_call | solution.py:705
  (134 shorter events, 27.1 us)
Async XLA Ops:
  2.7 9.5 %collective-permute-start.2 = (bf16[1,80,768]{2,1,0:T(8,128)(2,1)}, bf16[1,80,768]{2,1,0:T(8,128)(2,1)S(1)}, u32[]{:S(2)}, u32[]{:S(2)}) collective-permute-start(bf16[1,80,768]{2,1,0:T(8,128)(2,1)} %bitcast.7), channel_id=1, source_target_pairs={{0,8},{1,9},{2,10},{3,11},{4,12},{5,13},{6,14},{7,15},{8,16},{9,17... | collective-permute-start | bytes 368648 | tf_op jit(solution)/shard_map/ppermute | solution.py:77
  9.5 9.7 %collective-permute-start.5 = (bf16[1,80,768]{2,1,0:T(8,128)(2,1)}, bf16[1,80,768]{2,1,0:T(8,128)(2,1)S(1)}, u32[]{:S(2)}, u32[]{:S(2)}) collective-permute-start(bf16[1,80,768]{2,1,0:T(8,128)(2,1)} %bitcast.10), channel_id=1, source_target_pairs={{0,16},{1,17},{2,18},{3,19},{4,20},{5,21},{6,22},{7,23},{8,24},{9,... | collective-permute-start | bytes 368648 | tf_op jit(solution)/shard_map/ppermute | solution.py:77
  10.3 18.0 %collective-permute-start.15 = (bf16[1,224,768]{2,1,0:T(8,128)(2,1)}, bf16[1,224,768]{2,1,0:T(8,128)(2,1)}, u32[]{:S(2)}, u32[]{:S(2)}) collective-permute-start(bf16[1,224,768]{2,1,0:T(8,128)(2,1)} %bitcast.4), channel_id=1, source_target_pairs={{0,2},{1,5},{2,0},{3,7},{4,6},{5,1},{6,4},{7,3},{8,10},{9,13},{10,... | collective-permute-start | bytes 1032200 | tf_op jit(solution)/shard_map/ppermute | solution.py:77
  13.4 9.6 %collective-permute-start.4 = (bf16[2,80,768]{2,1,0:T(8,128)(2,1)S(1)}, bf16[2,80,768]{2,1,0:T(8,128)(2,1)S(1)}, u32[]{:S(2)}, u32[]{:S(2)}) collective-permute-start(bf16[2,80,768]{2,1,0:T(8,128)(2,1)S(1)} %pad_maximum_fusion.1), channel_id=1, source_target_pairs={{0,2},{1,5},{2,0},{3,7},{4,6},{5,1},{6,4},{7,3},{8,10},{9,13},{10,... | collective-permute-start | bytes 737288 | tf_op jit(solution)/shard_map/ppermute | solution.py:77
  15.9 13.0 %collective-permute-start.1 = (bf16[2,80,768]{2,1,0:T(8,128)(2,1)S(1)}, bf16[2,80,768]{2,1,0:T(8,128)(2,1)S(1)}, u32[]{:S(2)}, u32[]{:S(2)}) collective-permute-start(bf16[2,80,768]{2,1,0:T(8,128)(2,1)S(1)} %pad_maximum_fusion.refs_0_), channel_id=1, source_target_pairs={{0,4},{1,3},{2,6},{3,1},{4,0},{5,7},{6,2},{7,5},{8,12},{9,11},{10,... | collective-permute-start | bytes 737288 | tf_op jit(solution)/shard_map/ppermute | solution.py:77
  17.5 14.8 %collective-permute-start.9 = (bf16[2,80,768]{2,1,0:T(8,128)(2,1)S(1)}, bf16[2,80,768]{2,1,0:T(8,128)(2,1)S(1)}, u32[]{:S(2)}, u32[]{:S(2)}) collective-permute-start(bf16[2,80,768]{2,1,0:T(8,128)(2,1)S(1)} %pad_maximum_fusion.refs_0_), channel_id=1, source_target_pairs={{0,1},{1,0},{2,3},{3,2},{4,5},{5,4},{6,7},{7,6},{8,9},{9,8},{10,11... | collective-permute-start | bytes 737288 | tf_op jit(solution)/shard_map/ppermute | solution.py:77
  23.1 9.3 %collective-permute-start.7 = (bf16[4,80,768]{2,1,0:T(8,128)(2,1)S(1)}, bf16[4,80,768]{2,1,0:T(8,128)(2,1)}, u32[]{:S(2)}, u32[]{:S(2)}) collective-permute-start(bf16[4,80,768]{2,1,0:T(8,128)(2,1)S(1)} %constant_dynamic-update-slice_fusion.refs_2_), channel_id=1, source_target_pairs={{0,4},{1,3},{2,6},{3,1},{4,0},{5,7},{6,2},{7,5},{8,12},{9,11},{10,... | collective-permute-start | bytes 1474568 | tf_op jit(solution)/shard_map/ppermute | solution.py:77
  25.5 11.8 %collective-permute-start.19 = (bf16[1,224,768]{2,1,0:T(8,128)(2,1)}, bf16[1,224,768]{2,1,0:T(8,128)(2,1)}, u32[]{:S(2)}, u32[]{:S(2)}) collective-permute-start(bf16[1,224,768]{2,1,0:T(8,128)(2,1)} %bitcast.5), channel_id=1, source_target_pairs={{0,8},{1,25},{2,10},{3,27},{4,12},{5,29},{6,14},{7,31},{8,16},{9,1... | collective-permute-start | bytes 1032200 | tf_op jit(solution)/shard_map/ppermute | solution.py:77
  28.4 8.9 %collective-permute-start.8 = (bf16[2,80,768]{2,1,0:T(8,128)(2,1)S(1)}, bf16[2,80,768]{2,1,0:T(8,128)(2,1)}, u32[]{:S(2)}, u32[]{:S(2)}) collective-permute-start(bf16[2,80,768]{2,1,0:T(8,128)(2,1)S(1)} %constant_dynamic-update-slice_fusion.3.refs_3_), channel_id=1, source_target_pairs={{0,4},{1,3},{2,6},{3,1},{4,0},{5,7},{6,2},{7,5},{8,12},{9,11},{10,... | collective-permute-start | bytes 737288 | tf_op jit(solution)/shard_map/ppermute | solution.py:77
  29.0 13.6 %collective-permute-start.11 = (bf16[4,80,768]{2,1,0:T(8,128)(2,1)S(1)}, bf16[4,80,768]{2,1,0:T(8,128)(2,1)}, u32[]{:S(2)}, u32[]{:S(2)}) collective-permute-start(bf16[4,80,768]{2,1,0:T(8,128)(2,1)S(1)} %constant_dynamic-update-slice_fusion.refs_2_), channel_id=1, source_target_pairs={{0,1},{1,0},{2,3},{3,2},{4,5},{5,4},{6,7},{7,6},{8,9},{9,8},{10,11... | collective-permute-start | bytes 1474568 | tf_op jit(solution)/shard_map/ppermute | solution.py:77
  32.3 10.2 %collective-permute-start.13 = (bf16[4,80,768]{2,1,0:T(8,128)(2,1)}, bf16[4,80,768]{2,1,0:T(8,128)(2,1)}, u32[]{:S(2)}, u32[]{:S(2)}) collective-permute-start(bf16[4,80,768]{2,1,0:T(8,128)(2,1)} %collective-permute-done.7.refs_4_), channel_id=1, source_target_pairs={{0,1},{1,0},{2,3},{3,2},{4,5},{5,4},{6,7},{7,6},{8,9},{9,8},{10,11... | collective-permute-start | bytes 1474568 | tf_op jit(solution)/shard_map/ppermute | solution.py:77
  40.2 16.1 %collective-permute-start.20 = (bf16[1,224,768]{2,1,0:T(8,128)(2,1)}, bf16[1,224,768]{2,1,0:T(8,128)(2,1)S(1)}, u32[]{:S(2)}, u32[]{:S(2)}) collective-permute-start(bf16[1,224,768]{2,1,0:T(8,128)(2,1)} %collective-permute-done.19), channel_id=1, source_target_pairs={{0,2},{1,5},{2,0},{3,7},{4,6},{5,1},{6,4},{7,3},{8,10},{9,13},{10,... | collective-permute-start | bytes 1032200 | tf_op jit(solution)/shard_map/ppermute | solution.py:77
  40.8 13.6 %collective-permute-start.24 = (bf16[1,224,768]{2,1,0:T(8,128)(2,1)}, bf16[1,224,768]{2,1,0:T(8,128)(2,1)S(1)}, u32[]{:S(2)}, u32[]{:S(2)}) collective-permute-start(bf16[1,224,768]{2,1,0:T(8,128)(2,1)} %collective-permute-done.19), channel_id=1, source_target_pairs={{0,8},{1,25},{2,10},{3,27},{4,12},{5,29},{6,14},{7,31},{8,16},{9,1... | collective-permute-start | bytes 1032200 | tf_op jit(solution)/shard_map/ppermute | solution.py:77
  41.8 24.5 %collective-permute-start.16 = (bf16[2,224,768]{2,1,0:T(8,128)(2,1)S(1)}, bf16[2,224,768]{2,1,0:T(8,128)(2,1)S(1)}, u32[]{:S(2)}, u32[]{:S(2)}) collective-permute-start(bf16[2,224,768]{2,1,0:T(8,128)(2,1)S(1)} %constant_dynamic-update-slice_fusion.5.refs_0_), channel_id=1, source_target_pairs={{0,4},{1,3},{2,6},{3,1},{4,0},{5,7},{6,2},{7,5},{8,12},{9,11},{10,... | collective-permute-start | bytes 2064392 | tf_op jit(solution)/shard_map/ppermute | solution.py:77
  54.4 10.5 %collective-permute-start.25 = (bf16[1,224,768]{2,1,0:T(8,128)(2,1)S(1)}, bf16[1,224,768]{2,1,0:T(8,128)(2,1)S(1)}, u32[]{:S(2)}, u32[]{:S(2)}) collective-permute-start(bf16[1,224,768]{2,1,0:T(8,128)(2,1)S(1)} %collective-permute-done.24), channel_id=1, source_target_pairs={{0,2},{1,5},{2,0},{3,7},{4,6},{5,1},{6,4},{7,3},{8,10},{9,13},{10,... | collective-permute-start | bytes 1032200 | tf_op jit(solution)/shard_map/ppermute | solution.py:77
  54.8 12.0 %collective-permute-start.29 = (bf16[1,224,768]{2,1,0:T(8,128)(2,1)S(1)}, bf16[1,224,768]{2,1,0:T(8,128)(2,1)S(1)}, u32[]{:S(2)}, u32[]{:S(2)}) collective-permute-start(bf16[1,224,768]{2,1,0:T(8,128)(2,1)S(1)} %collective-permute-done.24), channel_id=1, source_target_pairs={{0,8},{1,25},{2,10},{3,27},{4,12},{5,29},{6,14},{7,31},{8,16},{9,1... | collective-permute-start | bytes 1032200 | tf_op jit(solution)/shard_map/ppermute | solution.py:77
  57.3 11.0 %collective-permute-start.21 = (bf16[2,224,768]{2,1,0:T(8,128)(2,1)S(1)}, bf16[2,224,768]{2,1,0:T(8,128)(2,1)S(1)}, u32[]{:S(2)}, u32[]{:S(2)}) collective-permute-start(bf16[2,224,768]{2,1,0:T(8,128)(2,1)S(1)} %constant_dynamic-update-slice_fusion.7.refs_4_), channel_id=1, source_target_pairs={{0,4},{1,3},{2,6},{3,1},{4,0},{5,7},{6,2},{7,5},{8,12},{9,11},{10,... | collective-permute-start | bytes 2064392 | tf_op jit(solution)/shard_map/ppermute | solution.py:77
  64.9 19.1 %collective-permute-start.27 = (bf16[2,224,768]{2,1,0:T(8,128)(2,1)S(1)}, bf16[2,224,768]{2,1,0:T(8,128)(2,1)}, u32[]{:S(2)}, u32[]{:S(2)}) collective-permute-start(bf16[2,224,768]{2,1,0:T(8,128)(2,1)S(1)} %constant_dynamic-update-slice_fusion.9.refs_8_), channel_id=1, source_target_pairs={{0,4},{1,3},{2,6},{3,1},{4,0},{5,7},{6,2},{7,5},{8,12},{9,11},{10,... | collective-permute-start | bytes 2064392 | tf_op jit(solution)/shard_map/ppermute | solution.py:77
  66.2 17.9 %collective-permute-start.17 = (bf16[2,224,768]{2,1,0:T(8,128)(2,1)S(1)}, bf16[2,224,768]{2,1,0:T(8,128)(2,1)S(1)}, u32[]{:S(2)}, u32[]{:S(2)}) collective-permute-start(bf16[2,224,768]{2,1,0:T(8,128)(2,1)S(1)} %constant_dynamic-update-slice_fusion.5.refs_0_), channel_id=1, source_target_pairs={{0,1},{1,0},{2,3},{3,2},{4,5},{5,4},{6,7},{7,6},{8,9},{9,8},{10,11... | collective-permute-start | bytes 2064392 | tf_op jit(solution)/shard_map/ppermute | solution.py:77
  66.3 18.3 %collective-permute-start.18 = (bf16[2,224,768]{2,1,0:T(8,128)(2,1)S(1)}, bf16[2,224,768]{2,1,0:T(8,128)(2,1)S(1)}, u32[]{:S(2)}, u32[]{:S(2)}) collective-permute-start(bf16[2,224,768]{2,1,0:T(8,128)(2,1)S(1)} %collective-permute-done.16.refs_2_), channel_id=1, source_target_pairs={{0,1},{1,0},{2,3},{3,2},{4,5},{5,4},{6,7},{7,6},{8,9},{9,8},{10,11... | collective-permute-start | bytes 2064392 | tf_op jit(solution)/shard_map/ppermute | solution.py:77
  66.8 11.0 %collective-permute-start.30 = (bf16[1,224,768]{2,1,0:T(8,128)(2,1)S(1)}, bf16[1,224,768]{2,1,0:T(8,128)(2,1)S(1)}, u32[]{:S(2)}, u32[]{:S(2)}) collective-permute-start(bf16[1,224,768]{2,1,0:T(8,128)(2,1)S(1)} %collective-permute-done.29.refs_12_), channel_id=1, source_target_pairs={{0,2},{1,5},{2,0},{3,7},{4,6},{5,1},{6,4},{7,3},{8,10},{9,13},{10,... | collective-permute-start | bytes 1032200 | tf_op jit(solution)/shard_map/ppermute | solution.py:77
  68.3 15.0 %collective-permute-start.31 = (bf16[1,224,768]{2,1,0:T(8,128)(2,1)S(1)}, bf16[1,224,768]{2,1,0:T(8,128)(2,1)S(1)}, u32[]{:S(2)}, u32[]{:S(2)}) collective-permute-start(bf16[1,224,768]{2,1,0:T(8,128)(2,1)S(1)} %collective-permute-done.29.refs_12_), channel_id=1, source_target_pairs={{0,4},{1,3},{2,6},{3,1},{4,0},{5,7},{6,2},{7,5},{8,12},{9,11},{10,... | collective-permute-start | bytes 1032200 | tf_op jit(solution)/shard_map/ppermute | solution.py:77
  77.8 9.2 %collective-permute-start.35 = (bf16[1,224,768]{2,1,0:T(8,128)(2,1)S(1)}, bf16[1,224,768]{2,1,0:T(8,128)(2,1)}, u32[]{:S(2)}, u32[]{:S(2)}) collective-permute-start(bf16[1,224,768]{2,1,0:T(8,128)(2,1)S(1)} %collective-permute-done.30.refs_14_), channel_id=1, source_target_pairs={{0,4},{1,3},{2,6},{3,1},{4,0},{5,7},{6,2},{7,5},{8,12},{9,11},{10,... | collective-permute-start | bytes 1032200 | tf_op jit(solution)/shard_map/ppermute | solution.py:77
  149.1 14.2 %all-to-all-start = ((f32[32,8,96]{2,1,0:T(8,128)}), f32[32,8,96]{2,1,0:T(8,128)S(1)}, u32[]{:S(2)}, u32[]{:S(2)}) async-start(f32[32,8,96]{2,1,0:T(8,128)} %get-tuple-element.84), calls=%async_computation | async-start | bytes 262144 | tf_op jit(solution)/shard_map/all_to_all | solution.py:784
  (40 other events, 459.6 us)
